TPU v7x, 32 devices: a whole 2x2x4 slice. The times are simulated.
32 devices in a mesh: tile: 8 (over z, y), group: 4 (over x, core).
Axes of the slice: x: 2, y: 2, z: 4, core: 2. Of those that a mesh axis runs over, the one named last changes fastest.
Arguments:
- tracers: float32 [32, 16, 64, 256], P('group', None, 'tile'), may hold values from -6 to 6
- emissions: float32 [32, 64, 256], P('group', 'tile'), may hold values from -6 to 6
- winds: float32 [4, 2, 16, 64, 256], P('group', None, None, 'tile'), may hold values from -1.44 to 1.44, as said below
- diffusivity: float32 [4, 15, 64, 256], P('group', None, 'tile'), may hold values from 0.05 to 2
- substeps: int32 [8], replicated, may hold values from 1 to 6, as said below
- loader: int32 [8], replicated, may hold values from 0 to 3
Outputs:
- mixed: float32 [32, 16, 64, 256], P('group', None, 'tile')
Inputs may be any that keep to these rules, and one draw needn't show every extreme that they name: The first and the last tile take 6 substeps. `winds`: divided by the substep count of the tile that holds the face (for a meridional value on a tile's first row, by the smaller count of that tile and the tile south of it), every entry lies within -0.24 to 0.24.
All inputs are finite; a program needn't handle non-finite values.
Results may differ from a plain program's by a relative error of at most 0.00002.
Values sent between devices are 32-bit elements; how exact they have to be, the bound alone decides.
No kernel may reach another device: no remote copies, remote signals or barrier semaphores. Data moves between devices by JAX's collectives and lax.ppermute only.
A program may use at most 64 MiB of HBM per device.

v0:
```python
import jax
import jax.numpy as jnp
from jax import lax
from jax.sharding import PartitionSpec as P

ROUNDS = 6


def spread(value, axis, root):
    mine = lax.axis_index(axis) == root
    return lax.psum(jnp.where(mine, value, jnp.zeros_like(value)), axis)


def from_behind(value, axis, by):
    count = lax.axis_size(axis)
    pairs = [(i, i + by) for i in range(count) if 0 <= i + by < count]
    return lax.ppermute(value, axis, pairs)


def thomas_solve(mixing, coefficient):
    levels = mixing.shape[1]
    zero_plane = jnp.zeros_like(coefficient[0])
    previous_ratio = zero_plane
    previous_value = jnp.zeros_like(mixing[:, 0])
    ratios = []
    values = []
    for level in range(levels):
        lower_coef = coefficient[level - 1] if level > 0 else zero_plane
        upper_coef = coefficient[level] if level < levels - 1 else zero_plane
        pivot = 1.0 / (1.0 + lower_coef + upper_coef - lower_coef * previous_ratio)
        previous_ratio = upper_coef * pivot
        previous_value = (mixing[:, level] + lower_coef * previous_value) * pivot
        ratios.append(previous_ratio)
        values.append(previous_value)
    solved = [None] * levels
    current = values[levels - 1]
    solved[levels - 1] = current
    for level in range(levels - 2, -1, -1):
        current = values[level] + ratios[level] * current
        solved[level] = current
    return jnp.stack(solved, axis=1)


def zonal_tendency(mixing, zonal):
    from_west = jnp.roll(mixing, 1, axis=3)
    west_flux = jnp.maximum(zonal, 0.0) * from_west + jnp.minimum(zonal, 0.0) * mixing
    east_flux = jnp.roll(west_flux, -1, axis=3)
    return east_flux - west_flux


def shards(tracers, emissions, winds, diffusivity, substeps, loader):
    tile_position = lax.axis_index("tile")
    tile_numbers = jnp.arange(substeps.shape[0])
    loader_slot = jnp.sum(jnp.where(tile_numbers == tile_position, loader, 0))
    local_winds, coefficient = (
        spread(winds[0], "group", loader_slot),
        spread(diffusivity[0], "group", loader_slot),
    )
    height = tracers.shape[2]
    row_global = tile_position * height + jnp.arange(height)
    zonal = local_winds[0]
    meridional = local_winds[1] * (row_global > 0).astype(jnp.float32)[:, None]
    count = jnp.sum(jnp.where(tile_numbers == tile_position, substeps, 0))
    count_float = count.astype(jnp.float32)
    mixing = tracers
    for substep in range(ROUNDS):
        fraction = jnp.where(substep < count, 1.0 / count_float, jnp.float32(0.0))
        below_row = from_behind(mixing[:, :, -1:], "tile", 1)
        from_south = jnp.concatenate([below_row, mixing[:, :, :-1]], axis=2)
        south_flux = (
            jnp.maximum(meridional, 0.0) * from_south + jnp.minimum(meridional, 0.0) * mixing
        )
        above_flux = from_behind(south_flux[:, :, :1], "tile", -1)
        north_flux = jnp.concatenate([south_flux[:, :, 1:], above_flux], axis=2)
        mixing = mixing - fraction * (zonal_tendency(mixing, zonal) + (north_flux - south_flux))
    mixing = mixing.at[:, 0].add(emissions)
    return thomas_solve(mixing, coefficient)


def solution(mesh):
    return jax.shard_map(
        shards,
        mesh=mesh,
        in_specs=(
            P("group", None, "tile", None),
            P("group", "tile", None),
            P("group", None, None, "tile", None),
            P("group", None, "tile", None),
            P(),
            P(),
        ),
        out_specs=P("group", None, "tile", None),
        check_vma=False,
    )
```

profile of v0, /device:TPU:8, one launch (start us, length us, event | category | flops | bytes accessed | tf_op | source)
XLA Modules:
  0.0 150.7 jit_solution(2287822702019247253)
XLA Ops:
  6.5 1.4 fusion.47
  8.6 0.7 select_bitcast_fusion
  10.2 3.4 %collective-permute-start = (f32[8,16,1,256]{3,1,2,0:T(8,128)S(1)}, f32[8,16,1,256]{3,1,2,0:T(8,128)S(1)}, u32[]{:S(2)}, u32[]{:S(2)}) collective-permute-start(f32[8,16,1,256]{3,1,2,0:T(8,128)S(1)} %copy.50), channel_id=1, source_target_pairs={{0,4},{4,8},{8,12},{12,16},{16,20},{20,24},{24,28},{1,5},{5,9},{9,... | collective-permute-start | bytes 393224 | tf_op jit(solution)/shard_map/ppermute | solution.py:17
  13.6 5.8 %collective-permute-done = f32[8,16,1,256]{3,1,2,0:T(8,128)S(1)} collective-permute-done((f32[8,16,1,256]{3,1,2,0:T(8,128)S(1)}, f32[8,16,1,256]{3,1,2,0:T(8,128)S(1)}, u32[]{:S(2)}, u32[]{:S(2)}) %collective-permute-start) | collective-permute-done | bytes 131104 | tf_op jit(solution)/shard_map/ppermute | solution.py:17
  19.4 0.8 copy.24
  20.2 24.6 %all-reduce.3.cloned.1.call-done = (f32[15,8,256]{2,1,0:T(8,128)}, f32[2,16,8,256]{3,2,1,0:T(8,128)}) async-done(((f32[15,8,256]{2,1,0:T(8,128)}, f32[2,16,8,256]{3,2,1,0:T(8,128)}), (f32[15,8,256]{2,1,0:T(8,128)}, f32[2,16,8,256]{3,2,1,0:T(8,128)})) %all-reduce.3.cloned.1.call-update) | async-done | bytes 385040 | tf_op jit(solution)/shard_map/psum | solution.py:11
  44.8 1.1 maximum_bitcast_fusion
  46.6 0.8 copy.26
  47.5 3.3 %collective-permute-start.1 = (f32[8,16,1,256]{3,1,2,0:T(8,128)}, f32[8,16,1,256]{3,1,2,0:T(8,128)}, u32[]{:S(2)}, u32[]{:S(2)}) collective-permute-start(f32[8,16,1,256]{3,1,2,0:T(8,128)} %copy.26), channel_id=1, source_target_pairs={{4,0},{8,4},{12,8},{16,12},{20,16},{24,20},{28,24},{5,1},{9,5},{13... | collective-permute-start | bytes 393224 | tf_op jit(solution)/shard_map/ppermute | solution.py:17
  52.7 2.0 %collective-permute-done.1 = f32[8,16,1,256]{3,1,2,0:T(8,128)} collective-permute-done((f32[8,16,1,256]{3,1,2,0:T(8,128)}, f32[8,16,1,256]{3,1,2,0:T(8,128)}, u32[]{:S(2)}, u32[]{:S(2)}) %collective-permute-start.1) | collective-permute-done | bytes 131104 | tf_op jit(solution)/shard_map/ppermute | solution.py:17
  54.6 1.0 copy.27
  56.5 4.3 %collective-permute-start.2 = (f32[8,16,1,256]{3,1,2,0:T(8,128)S(1)}, f32[8,16,1,256]{3,1,2,0:T(8,128)S(1)}, u32[]{:S(2)}, u32[]{:S(2)}) collective-permute-start(f32[8,16,1,256]{3,1,2,0:T(8,128)S(1)} %copy.29), channel_id=1, source_target_pairs={{0,4},{4,8},{8,12},{12,16},{16,20},{20,24},{24,28},{1,5},{5,9},{9,... | collective-permute-start | bytes 393224 | tf_op jit(solution)/shard_map/ppermute | solution.py:17
  65.9 2.7 %collective-permute-start.3 = (f32[8,16,1,256]{3,1,2,0:T(8,128)S(1)}, f32[8,16,1,256]{3,1,2,0:T(8,128)S(1)}, u32[]{:S(2)}, u32[]{:S(2)}) collective-permute-start(f32[8,16,1,256]{3,1,2,0:T(8,128)S(1)} %copy.31), channel_id=1, source_target_pairs={{4,0},{8,4},{12,8},{16,12},{20,16},{24,20},{28,24},{5,1},{9,5},{13... | collective-permute-start | bytes 393224 | tf_op jit(solution)/shard_map/ppermute | solution.py:17
  69.1 3.6 %collective-permute-done.3 = f32[8,16,1,256]{3,1,2,0:T(8,128)S(1)} collective-permute-done((f32[8,16,1,256]{3,1,2,0:T(8,128)S(1)}, f32[8,16,1,256]{3,1,2,0:T(8,128)S(1)}, u32[]{:S(2)}, u32[]{:S(2)}) %collective-permute-start.3) | collective-permute-done | bytes 131104 | tf_op jit(solution)/shard_map/ppermute | solution.py:17
  73.7 3.6 %collective-permute-start.4 = (f32[8,16,1,256]{3,1,2,0:T(8,128)S(1)}, f32[8,16,1,256]{3,1,2,0:T(8,128)S(1)}, u32[]{:S(2)}, u32[]{:S(2)}) collective-permute-start(f32[8,16,1,256]{3,1,2,0:T(8,128)S(1)} %copy.33), channel_id=1, source_target_pairs={{0,4},{4,8},{8,12},{12,16},{16,20},{20,24},{24,28},{1,5},{5,9},{9,... | collective-permute-start | bytes 393224 | tf_op jit(solution)/shard_map/ppermute | solution.py:17
  77.6 3.9 %collective-permute-done.4 = f32[8,16,1,256]{3,1,2,0:T(8,128)S(1)} collective-permute-done((f32[8,16,1,256]{3,1,2,0:T(8,128)S(1)}, f32[8,16,1,256]{3,1,2,0:T(8,128)S(1)}, u32[]{:S(2)}, u32[]{:S(2)}) %collective-permute-start.4) | collective-permute-done | bytes 131104 | tf_op jit(solution)/shard_map/ppermute | solution.py:17
  82.4 2.7 %collective-permute-start.5 = (f32[8,16,1,256]{3,1,2,0:T(8,128)S(1)}, f32[8,16,1,256]{3,1,2,0:T(8,128)S(1)}, u32[]{:S(2)}, u32[]{:S(2)}) collective-permute-start(f32[8,16,1,256]{3,1,2,0:T(8,128)S(1)} %copy.35), channel_id=1, source_target_pairs={{4,0},{8,4},{12,8},{16,12},{20,16},{24,20},{28,24},{5,1},{9,5},{13... | collective-permute-start | bytes 393224 | tf_op jit(solution)/shard_map/ppermute | solution.py:17
  85.7 3.6 %collective-permute-done.5 = f32[8,16,1,256]{3,1,2,0:T(8,128)S(1)} collective-permute-done((f32[8,16,1,256]{3,1,2,0:T(8,128)S(1)}, f32[8,16,1,256]{3,1,2,0:T(8,128)S(1)}, u32[]{:S(2)}, u32[]{:S(2)}) %collective-permute-start.5) | collective-permute-done | bytes 131104 | tf_op jit(solution)/shard_map/ppermute | solution.py:17
  90.3 3.7 %collective-permute-start.6 = (f32[8,16,1,256]{3,1,2,0:T(8,128)S(1)}, f32[8,16,1,256]{3,1,2,0:T(8,128)S(1)}, u32[]{:S(2)}, u32[]{:S(2)}) collective-permute-start(f32[8,16,1,256]{3,1,2,0:T(8,128)S(1)} %copy.37), channel_id=1, source_target_pairs={{0,4},{4,8},{8,12},{12,16},{16,20},{20,24},{24,28},{1,5},{5,9},{9,... | collective-permute-start | bytes 393224 | tf_op jit(solution)/shard_map/ppermute | solution.py:17
  94.2 3.9 %collective-permute-done.6 = f32[8,16,1,256]{3,1,2,0:T(8,128)S(1)} collective-permute-done((f32[8,16,1,256]{3,1,2,0:T(8,128)S(1)}, f32[8,16,1,256]{3,1,2,0:T(8,128)S(1)}, u32[]{:S(2)}, u32[]{:S(2)}) %collective-permute-start.6) | collective-permute-done | bytes 131104 | tf_op jit(solution)/shard_map/ppermute | solution.py:17
  99.1 4.1 %collective-permute-start.7 = (f32[8,16,1,256]{3,1,2,0:T(8,128)S(1)}, f32[8,16,1,256]{3,1,2,0:T(8,128)S(1)}, u32[]{:S(2)}, u32[]{:S(2)}) collective-permute-start(f32[8,16,1,256]{3,1,2,0:T(8,128)S(1)} %copy.39), channel_id=1, source_target_pairs={{4,0},{8,4},{12,8},{16,12},{20,16},{24,20},{28,24},{5,1},{9,5},{13... | collective-permute-start | bytes 393224 | tf_op jit(solution)/shard_map/ppermute | solution.py:17
  103.7 3.8 %collective-permute-done.7 = f32[8,16,1,256]{3,1,2,0:T(8,128)S(1)} collective-permute-done((f32[8,16,1,256]{3,1,2,0:T(8,128)S(1)}, f32[8,16,1,256]{3,1,2,0:T(8,128)S(1)}, u32[]{:S(2)}, u32[]{:S(2)}) %collective-permute-start.7) | collective-permute-done | bytes 131104 | tf_op jit(solution)/shard_map/ppermute | solution.py:17
  108.5 3.6 %collective-permute-start.8 = (f32[8,16,1,256]{3,1,2,0:T(8,128)S(1)}, f32[8,16,1,256]{3,1,2,0:T(8,128)S(1)}, u32[]{:S(2)}, u32[]{:S(2)}) collective-permute-start(f32[8,16,1,256]{3,1,2,0:T(8,128)S(1)} %copy.41), channel_id=1, source_target_pairs={{0,4},{4,8},{8,12},{12,16},{16,20},{20,24},{24,28},{1,5},{5,9},{9,... | collective-permute-start | bytes 393224 | tf_op jit(solution)/shard_map/ppermute | solution.py:17
  112.4 3.9 %collective-permute-done.8 = f32[8,16,1,256]{3,1,2,0:T(8,128)S(1)} collective-permute-done((f32[8,16,1,256]{3,1,2,0:T(8,128)S(1)}, f32[8,16,1,256]{3,1,2,0:T(8,128)S(1)}, u32[]{:S(2)}, u32[]{:S(2)}) %collective-permute-start.8) | collective-permute-done | bytes 131104 | tf_op jit(solution)/shard_map/ppermute | solution.py:17
  117.3 2.5 %collective-permute-start.9 = (f32[8,16,1,256]{3,1,2,0:T(8,128)S(1)}, f32[8,16,1,256]{3,1,2,0:T(8,128)S(1)}, u32[]{:S(2)}, u32[]{:S(2)}) collective-permute-start(f32[8,16,1,256]{3,1,2,0:T(8,128)S(1)} %copy.43), channel_id=1, source_target_pairs={{4,0},{8,4},{12,8},{16,12},{20,16},{24,20},{28,24},{5,1},{9,5},{13... | collective-permute-start | bytes 393224 | tf_op jit(solution)/shard_map/ppermute | solution.py:17
  120.3 3.8 %collective-permute-done.9 = f32[8,16,1,256]{3,1,2,0:T(8,128)S(1)} collective-permute-done((f32[8,16,1,256]{3,1,2,0:T(8,128)S(1)}, f32[8,16,1,256]{3,1,2,0:T(8,128)S(1)}, u32[]{:S(2)}, u32[]{:S(2)}) %collective-permute-start.9) | collective-permute-done | bytes 131104 | tf_op jit(solution)/shard_map/ppermute | solution.py:17
  125.1 3.4 %collective-permute-start.10 = (f32[8,16,1,256]{3,1,2,0:T(8,128)S(1)}, f32[8,16,1,256]{3,1,2,0:T(8,128)S(1)}, u32[]{:S(2)}, u32[]{:S(2)}) collective-permute-start(f32[8,16,1,256]{3,1,2,0:T(8,128)S(1)} %copy.45), channel_id=1, source_target_pairs={{0,4},{4,8},{8,12},{12,16},{16,20},{20,24},{24,28},{1,5},{5,9},{9,... | collective-permute-start | bytes 393224 | tf_op jit(solution)/shard_map/ppermute | solution.py:17
  128.8 4.1 %collective-permute-done.10 = f32[8,16,1,256]{3,1,2,0:T(8,128)S(1)} collective-permute-done((f32[8,16,1,256]{3,1,2,0:T(8,128)S(1)}, f32[8,16,1,256]{3,1,2,0:T(8,128)S(1)}, u32[]{:S(2)}, u32[]{:S(2)}) %collective-permute-start.10) | collective-permute-done | bytes 131104 | tf_op jit(solution)/shard_map/ppermute | solution.py:17
  133.8 2.5 %collective-permute-start.11 = (f32[8,16,1,256]{3,1,2,0:T(8,128)S(1)}, f32[8,16,1,256]{3,1,2,0:T(8,128)S(1)}, u32[]{:S(2)}, u32[]{:S(2)}) collective-permute-start(f32[8,16,1,256]{3,1,2,0:T(8,128)S(1)} %copy.47), channel_id=1, source_target_pairs={{4,0},{8,4},{12,8},{16,12},{20,16},{24,20},{28,24},{5,1},{9,5},{13... | collective-permute-start | bytes 393224 | tf_op jit(solution)/shard_map/ppermute | solution.py:17
  136.9 3.8 %collective-permute-done.11 = f32[8,16,1,256]{3,1,2,0:T(8,128)S(1)} collective-permute-done((f32[8,16,1,256]{3,1,2,0:T(8,128)S(1)}, f32[8,16,1,256]{3,1,2,0:T(8,128)S(1)}, u32[]{:S(2)}, u32[]{:S(2)}) %collective-permute-start.11) | collective-permute-done | bytes 131104 | tf_op jit(solution)/shard_map/ppermute | solution.py:17
  141.5 0.8 copy-done.7
  142.8 1.1 copy.49
  (113 shorter events, 16.8 us)
Async XLA Ops:
  6.5 3.5 %copy-start = (f32[8,16,8,256]{3,2,1,0:T(8,128)S(1)}, f32[8,16,8,256]{3,2,1,0:T(8,128)}, u32[]{:S(2)}) copy-start(f32[8,16,8,256]{3,2,1,0:T(8,128)} %param.8) | copy-start | bytes 3145732
  6.5 38.3 %all-reduce.3.cloned.1.call-start = ((), (), s32[]{:S(2)}) async-start(), calls=%async_computation | async-start | bytes 770048 | tf_op jit(solution)/shard_map/psum | solution.py:11
  10.2 9.2 %collective-permute-start = (f32[8,16,1,256]{3,1,2,0:T(8,128)S(1)}, f32[8,16,1,256]{3,1,2,0:T(8,128)S(1)}, u32[]{:S(2)}, u32[]{:S(2)}) collective-permute-start(f32[8,16,1,256]{3,1,2,0:T(8,128)S(1)} %copy.50), channel_id=1, source_target_pairs={{0,4},{4,8},{8,12},{12,16},{16,20},{20,24},{24,28},{1,5},{5,9},{9,... | collective-permute-start | bytes 393224 | tf_op jit(solution)/shard_map/ppermute | solution.py:17
  44.8 1.1 copy-start.6
  45.9 0.7 copy-start.3
  46.6 5.7 %copy-start.1 = (f32[8,16,8,256]{3,2,0,1:T(8,128)}, f32[8,16,8,256]{3,2,0,1:T(8,128)S(1)}, u32[]{:S(2)}) copy-start(f32[8,16,8,256]{3,2,0,1:T(8,128)S(1)} %get-tuple-element.66) | copy-start | bytes 3145732
  47.5 7.2 %collective-permute-start.1 = (f32[8,16,1,256]{3,1,2,0:T(8,128)}, f32[8,16,1,256]{3,1,2,0:T(8,128)}, u32[]{:S(2)}, u32[]{:S(2)}) collective-permute-start(f32[8,16,1,256]{3,1,2,0:T(8,128)} %copy.26), channel_id=1, source_target_pairs={{4,0},{8,4},{12,8},{16,12},{20,16},{24,20},{28,24},{5,1},{9,5},{13... | collective-permute-start | bytes 393224 | tf_op jit(solution)/shard_map/ppermute | solution.py:17
  52.6 3.1 %copy-start.2 = (f32[8,16,8,256]{3,2,0,1:T(8,128)S(1)}, f32[8,16,8,256]{3,2,0,1:T(8,128)}, u32[]{:S(2)}) copy-start(f32[8,16,8,256]{3,2,0,1:T(8,128)} %copy-done.1) | copy-start | bytes 3145732
  56.5 7.8 %collective-permute-start.2 = (f32[8,16,1,256]{3,1,2,0:T(8,128)S(1)}, f32[8,16,1,256]{3,1,2,0:T(8,128)S(1)}, u32[]{:S(2)}, u32[]{:S(2)}) collective-permute-start(f32[8,16,1,256]{3,1,2,0:T(8,128)S(1)} %copy.29), channel_id=1, source_target_pairs={{0,4},{4,8},{8,12},{12,16},{16,20},{20,24},{24,28},{1,5},{5,9},{9,... | collective-permute-start | bytes 393224 | tf_op jit(solution)/shard_map/ppermute | solution.py:17
  64.1 0.9 copy-start.4
  65.8 2.8 %copy-start.5 = (f32[15,8,256]{2,1,0:T(8,128)S(1)}, f32[15,8,256]{2,1,0:T(8,128)}, u32[]{:S(2)}) copy-start(f32[15,8,256]{2,1,0:T(8,128)} %get-tuple-element.17) | copy-start | bytes 368644
  65.9 6.9 %collective-permute-start.3 = (f32[8,16,1,256]{3,1,2,0:T(8,128)S(1)}, f32[8,16,1,256]{3,1,2,0:T(8,128)S(1)}, u32[]{:S(2)}, u32[]{:S(2)}) collective-permute-start(f32[8,16,1,256]{3,1,2,0:T(8,128)S(1)} %copy.31), channel_id=1, source_target_pairs={{4,0},{8,4},{12,8},{16,12},{20,16},{24,20},{28,24},{5,1},{9,5},{13... | collective-permute-start | bytes 393224 | tf_op jit(solution)/shard_map/ppermute | solution.py:17
  73.7 7.8 %collective-permute-start.4 = (f32[8,16,1,256]{3,1,2,0:T(8,128)S(1)}, f32[8,16,1,256]{3,1,2,0:T(8,128)S(1)}, u32[]{:S(2)}, u32[]{:S(2)}) collective-permute-start(f32[8,16,1,256]{3,1,2,0:T(8,128)S(1)} %copy.33), channel_id=1, source_target_pairs={{0,4},{4,8},{8,12},{12,16},{16,20},{20,24},{24,28},{1,5},{5,9},{9,... | collective-permute-start | bytes 393224 | tf_op jit(solution)/shard_map/ppermute | solution.py:17
  82.4 6.9 %collective-permute-start.5 = (f32[8,16,1,256]{3,1,2,0:T(8,128)S(1)}, f32[8,16,1,256]{3,1,2,0:T(8,128)S(1)}, u32[]{:S(2)}, u32[]{:S(2)}) collective-permute-start(f32[8,16,1,256]{3,1,2,0:T(8,128)S(1)} %copy.35), channel_id=1, source_target_pairs={{4,0},{8,4},{12,8},{16,12},{20,16},{24,20},{28,24},{5,1},{9,5},{13... | collective-permute-start | bytes 393224 | tf_op jit(solution)/shard_map/ppermute | solution.py:17
  90.3 7.9 %collective-permute-start.6 = (f32[8,16,1,256]{3,1,2,0:T(8,128)S(1)}, f32[8,16,1,256]{3,1,2,0:T(8,128)S(1)}, u32[]{:S(2)}, u32[]{:S(2)}) collective-permute-start(f32[8,16,1,256]{3,1,2,0:T(8,128)S(1)} %copy.37), channel_id=1, source_target_pairs={{0,4},{4,8},{8,12},{12,16},{16,20},{20,24},{24,28},{1,5},{5,9},{9,... | collective-permute-start | bytes 393224 | tf_op jit(solution)/shard_map/ppermute | solution.py:17
  99.1 8.4 %collective-permute-start.7 = (f32[8,16,1,256]{3,1,2,0:T(8,128)S(1)}, f32[8,16,1,256]{3,1,2,0:T(8,128)S(1)}, u32[]{:S(2)}, u32[]{:S(2)}) collective-permute-start(f32[8,16,1,256]{3,1,2,0:T(8,128)S(1)} %copy.39), channel_id=1, source_target_pairs={{4,0},{8,4},{12,8},{16,12},{20,16},{24,20},{28,24},{5,1},{9,5},{13... | collective-permute-start | bytes 393224 | tf_op jit(solution)/shard_map/ppermute | solution.py:17
  108.5 7.8 %collective-permute-start.8 = (f32[8,16,1,256]{3,1,2,0:T(8,128)S(1)}, f32[8,16,1,256]{3,1,2,0:T(8,128)S(1)}, u32[]{:S(2)}, u32[]{:S(2)}) collective-permute-start(f32[8,16,1,256]{3,1,2,0:T(8,128)S(1)} %copy.41), channel_id=1, source_target_pairs={{0,4},{4,8},{8,12},{12,16},{16,20},{20,24},{24,28},{1,5},{5,9},{9,... | collective-permute-start | bytes 393224 | tf_op jit(solution)/shard_map/ppermute | solution.py:17
  117.3 6.9 %collective-permute-start.9 = (f32[8,16,1,256]{3,1,2,0:T(8,128)S(1)}, f32[8,16,1,256]{3,1,2,0:T(8,128)S(1)}, u32[]{:S(2)}, u32[]{:S(2)}) collective-permute-start(f32[8,16,1,256]{3,1,2,0:T(8,128)S(1)} %copy.43), channel_id=1, source_target_pairs={{4,0},{8,4},{12,8},{16,12},{20,16},{24,20},{28,24},{5,1},{9,5},{13... | collective-permute-start | bytes 393224 | tf_op jit(solution)/shard_map/ppermute | solution.py:17
  125.1 7.8 %collective-permute-start.10 = (f32[8,16,1,256]{3,1,2,0:T(8,128)S(1)}, f32[8,16,1,256]{3,1,2,0:T(8,128)S(1)}, u32[]{:S(2)}, u32[]{:S(2)}) collective-permute-start(f32[8,16,1,256]{3,1,2,0:T(8,128)S(1)} %copy.45), channel_id=1, source_target_pairs={{0,4},{4,8},{8,12},{12,16},{16,20},{20,24},{24,28},{1,5},{5,9},{9,... | collective-permute-start | bytes 393224 | tf_op jit(solution)/shard_map/ppermute | solution.py:17
  133.8 6.9 %collective-permute-start.11 = (f32[8,16,1,256]{3,1,2,0:T(8,128)S(1)}, f32[8,16,1,256]{3,1,2,0:T(8,128)S(1)}, u32[]{:S(2)}, u32[]{:S(2)}) collective-permute-start(f32[8,16,1,256]{3,1,2,0:T(8,128)S(1)} %copy.47), channel_id=1, source_target_pairs={{4,0},{8,4},{12,8},{16,12},{20,16},{24,20},{28,24},{5,1},{9,5},{13... | collective-permute-start | bytes 393224 | tf_op jit(solution)/shard_map/ppermute | solution.py:17
  141.5 0.8 copy-start.7
Sparse Core Ops, SparseCore 0:
  10.2 34.5 all-reduce.2
where the time goes:
time: 151 us
  waiting for transfers between devices  67.1 us (44%)
  starting transfers between devices  39.8 us (26%)
  between operations  19.3 us (13%)
  other arithmetic  12.3 us (8%)
  local copies, waits for them, and re-layouts  12.2 us (8%)
    ppermute x12, waiting for transfers between devices, from_behind(): return lax.ppermute(value, axis, pairs)  42.5 us
    ppermute x12, starting transfers between devices, from_behind(): return lax.ppermute(value, axis, pairs)  39.8 us
    psum x1, waiting for transfers between devices, spread(): return lax.psum(jnp.where(mine, value, jnp.zeros_like(value)), axis)  24.6 us
    add x6, other arithmetic, shards(): jnp.maximum(meridional, 0.0) * from_south  4.09 us
    sub x6, other arithmetic, shards(): mixing - fraction * (zonal_tendency(mixing, zonal) + (north_flux - south_...  3.85 us
    ppermute x12, local copies, waits for them, and re-layouts, from_behind(): return lax.ppermute(value, axis, pairs)  3.17 us
  transfers between devices with their start and end apart: 13, of which 13 were waited for; matrix products, arithmetic and copies ran while one was open for 3% of the time, Pallas kernels for 0%

commit v1 on v0

v1 whole, which is shorter than its diff:
```python
import functools

import jax
import jax.numpy as jnp
from jax import lax
from jax.experimental import pallas as pl
from jax.experimental.pallas import tpu as pltpu
from jax.sharding import PartitionSpec as P

ROUNDS = 6
PARTS = ((2, "relay"), (2, "relay"), (2, "relay"), (1, "relay"), (1, "straight"))
TOGETHER = 4


def exchange(value, axis, bit):
    count = lax.axis_size(axis)
    return lax.ppermute(value, axis, [(i, i ^ bit) for i in range(count)])


def shift(value, axis, by):
    count = lax.axis_size(axis)
    return lax.ppermute(value, axis, [(i, i + by) for i in range(count) if 0 <= i + by < count])


def relay(value, axis):
    count = lax.axis_size(axis)
    pairs = [(i, i + 2) for i in range(0, count - 2, 2)] + [(i, i - 2) for i in range(3, count, 2)]
    return lax.ppermute(value, axis, pairs)


def window_kernel(
    parts, has_prior, scalars, own, pair, far, wind_own, wind_pair, wind_far, mixing_coef, source, *rest
):
    if has_prior:
        rest = rest[1:]
    out, coef, values, ratios = rest
    tracers, levels, height, width = own.shape
    rows = 3 * height
    even = scalars[3] == 1
    first = scalars[4] == 1
    counts = [scalars[0], scalars[1], scalars[2]]

    def band(per_tile, dtype):
        return jnp.concatenate([jnp.full((height, width), c, dtype) for c in per_tile], axis=0)

    def stacked(middle, near, distant):
        south = jnp.where(even, distant, near)
        north = jnp.where(even, near, distant)
        return jnp.concatenate([south, middle, north], axis=0)

    ones = jnp.ones((height, width), jnp.float32)
    fraction = jnp.concatenate([ones / (ones * c.astype(jnp.float32)) for c in counts], axis=0)
    row = lax.broadcasted_iota(jnp.int32, (height, width), 0)
    pole = jnp.logical_and(row == 0, first)

    def prepare(level, carry):
        zonal = stacked(wind_own[0, level], wind_pair[0, level], wind_far[0, level])
        meridional = stacked(
            jnp.where(pole, 0.0, wind_own[1, level]), wind_pair[1, level], wind_far[1, level]
        )
        plus, minus = jnp.maximum(zonal, 0.0), jnp.minimum(zonal, 0.0)
        plus_east, minus_east = pltpu.roll(plus, width - 1, 1), pltpu.roll(minus, width - 1, 1)
        up, down = jnp.maximum(meridional, 0.0), jnp.minimum(meridional, 0.0)
        up_north, down_north = pltpu.roll(up, rows - 1, 0), pltpu.roll(down, rows - 1, 0)
        coef[level, 0] = 1.0 - fraction * ((plus_east - minus) + (up_north - down))
        coef[level, 1] = fraction * plus
        coef[level, 2] = -fraction * minus_east
        coef[level, 3] = fraction * up
        coef[level, 4] = -fraction * down_north
        return carry

    lax.fori_loop(0, levels, prepare, 0)

    count_rows = band(counts, jnp.int32)
    active = [count_rows > step for step in range(ROUNDS)]
    per = min(levels, max(1, TOGETHER // tracers))

    def advance(block, carry):
        previous_coef, previous_ratio, previous_values = carry
        fields = {}
        for k in range(per):
            level = block * per + k
            for n in range(tracers):
                fields[k, n] = stacked(own[n, level], pair[n, level], far[n, level])
        for step in range(ROUNDS):
            for k in range(per):
                level = block * per + k
                for n in range(tracers):
                    q = fields[k, n]
                    new = (
                        coef[level, 0] * q
                        + coef[level, 1] * pltpu.roll(q, 1, 1)
                        + coef[level, 2] * pltpu.roll(q, width - 1, 1)
                        + coef[level, 3] * pltpu.roll(q, 1, 0)
                        + coef[level, 4] * pltpu.roll(q, rows - 1, 0)
                    )
                    fields[k, n] = jnp.where(active[step], new, q)
        for k in range(per):
            level = block * per + k
            upper = jnp.where(level < levels - 1, mixing_coef[jnp.minimum(level, levels - 2)], 0.0)
            pivot = 1.0 / (1.0 + previous_coef + upper - previous_coef * previous_ratio)
            ratio = upper * pivot
            ratios[level] = ratio
            solved = []
            for n in range(tracers):
                q = fields[k, n][height : 2 * height]
                q = q + jnp.where(level == 0, source[n], 0.0)
                value = (q + previous_coef * previous_values[n]) * pivot
                values[n, level] = value
                solved.append(value)
            previous_coef, previous_ratio, previous_values = upper, ratio, tuple(solved)
        return previous_coef, previous_ratio, previous_values

    zero = jnp.zeros((height, width), jnp.float32)
    _, _, current = lax.fori_loop(0, levels // per, advance, (zero, zero, (zero,) * tracers))
    for n in range(tracers):
        out[n, levels - 1] = current[n]

    def back(step, current):
        level = levels - 2 - step
        ratio = ratios[level]
        solved = []
        for n in range(tracers):
            value = values[n, level] + ratio * current[n]
            out[n, level] = value
            solved.append(value)
        return tuple(solved)

    lax.fori_loop(0, levels - 1, back, current)


def window(scalars, tracers, emissions, start, count, pair, far, winds, mixing_coef, prior):
    levels, height, width = tracers.shape[1:]
    whole = pl.BlockSpec(memory_space=pltpu.VMEM)
    at = start // count
    part = pl.BlockSpec((count, levels, height, width), lambda i: (at, 0, 0, 0))
    in_specs = [
        pl.BlockSpec(memory_space=pltpu.SMEM),
        part,
        whole,
        whole,
        whole,
        whole,
        whole,
        whole,
        pl.BlockSpec((count, height, width), lambda i: (at, 0, 0)),
    ]
    operands = [scalars, tracers, pair, far, *winds, mixing_coef, emissions]
    if prior is not None:
        in_specs.append(pl.BlockSpec(memory_space=pl.ANY))
        operands.append(prior)
    cost = count * levels * height * width * 3 * ROUNDS * 16
    return pl.pallas_call(
        functools.partial(window_kernel, None, prior is not None),
        grid=(1,),
        out_shape=jax.ShapeDtypeStruct(tracers.shape, tracers.dtype),
        in_specs=in_specs,
        out_specs=part,
        scratch_shapes=[
            pltpu.VMEM((levels, 5, 3 * height, width), jnp.float32),
            pltpu.VMEM((count, levels, height, width), jnp.float32),
            pltpu.VMEM((levels, height, width), jnp.float32),
        ],
        input_output_aliases={} if prior is None else {len(operands) - 1: 0},
        compiler_params=pltpu.CompilerParams(vmem_limit_bytes=32 * 1024 * 1024),
        cost_estimate=pl.CostEstimate(flops=cost, bytes_accessed=4 * 1024 * 1024, transcendentals=0),
    )(*operands)


def shards(tracers, emissions, winds, diffusivity, substeps, loader):
    tiles, groups = lax.axis_size("tile"), lax.axis_size("group")
    tile, group = lax.axis_index("tile"), lax.axis_index("group")
    even = tile % 2 == 0
    slot = loader[tile]
    scalars = jnp.stack(
        [
            substeps[jnp.maximum(tile - 1, 0)],
            substeps[tile],
            substeps[jnp.minimum(tile + 1, tiles - 1)],
            even.astype(jnp.int32),
            (tile == 0).astype(jnp.int32),
        ]
    )

    levels = winds.shape[2]
    half = levels // 2
    padded = jnp.pad(diffusivity, ((0, 0), (0, 1), (0, 0), (0, 0)))
    met = jnp.concatenate([winds[0], padded], axis=0)
    low, high = met[:, :half], met[:, half:]
    core = group % 2 == 1
    other = exchange(jnp.where(core, low, high), "group", 1)
    met = jnp.where(slot % 2 == group % 2, jnp.where(core, high, low), other)
    bit = 2
    while bit < groups:
        other = exchange(met, "group", bit)
        met = jnp.where((slot & bit) == (group & bit), met, other)
        bit *= 2
    wind_pair = exchange(met[:2], "tile", 1)
    wind_far = relay(wind_pair, "tile")
    bundle = jnp.concatenate([met, wind_pair, wind_far], axis=0)
    other = exchange(bundle, "group", 1)
    bundle = jnp.concatenate(
        [jnp.where(core, other, bundle), jnp.where(core, bundle, other)], axis=1
    )
    winds_here = (bundle[:2], bundle[3:5], bundle[5:7])
    mixing_coef = bundle[2]

    start = 0
    result = None
    for count, way in PARTS:
        part = tracers[start : start + count]
        if way == "relay":
            pair = exchange(part, "tile", 1)
            far = relay(pair, "tile")
        else:
            up, down = shift(part, "tile", 1), shift(part, "tile", -1)
            pair, far = jnp.where(even, down, up), jnp.where(even, up, down)
        result = window(
            scalars, tracers, emissions, start, count, pair, far, winds_here, mixing_coef, result
        )
        start += count
    return result


def solution(mesh):
    return jax.shard_map(
        shards,
        mesh=mesh,
        in_specs=(
            P("group", None, "tile", None),
            P("group", "tile", None),
            P("group", None, None, "tile", None),
            P("group", None, "tile", None),
            P(),
            P(),
        ),
        out_specs=P("group", None, "tile", None),
        check_vma=False,
    )
```

time: 151 us -> 85.6 us (0.57)
  waiting for transfers between devices: 67.1 us -> 15.8 us
  Pallas kernels: 0 us -> 29.3 us
  between operations: 19.3 us -> 2.84 us
  starting transfers between devices: 39.8 us -> 28.7 us
  other arithmetic: 12.3 us -> 2.24 us
  local copies, waits for them, and re-layouts: 12.2 us -> 5.39 us
    pallas_call x0 -> x5, Pallas kernels: none -> 29.3 us  [window(): pl.pallas_call(functools.partial(window_kernel, None, prior is not None),...]
    ppermute x12 -> x15, waiting for transfers between devices: 42.5 us -> 15.8 us  [the longest x8 14.6 us: exchange(): return lax.ppermute(value, axis, [(i, i ^ bit) for i in range(count)])]
    psum x1 -> x0, waiting for transfers between devices: 24.6 us -> none  [spread(): return lax.psum(jnp.where(mine, value, jnp.zeros_like(value)), axis)]
    ppermute x12 -> x15, starting transfers between devices: 39.8 us -> 28.7 us  [the longest x5 15.4 us: relay(): return lax.ppermute(value, axis, pairs)]
    slice x46 -> x3, local copies, waits for them, and re-layouts: 6.36 us -> 1.59 us  [the longest x2 1.58 us: shards(): part = tracers[start:start + count]]
    add x6 -> x0, other arithmetic: 4.09 us -> none  [shards(): jnp.maximum(meridional, 0.0) * from_south]
    sub x6 -> x0, other arithmetic: 3.85 us -> none  [shards(): mixing - fraction * (zonal_tendency(mixing, zonal) + (north_flux - south_...]
    ppermute x12 -> x0, local copies, waits for them, and re-layouts: 3.17 us -> none  [from_behind(): return lax.ppermute(value, axis, pairs)]
  transfers between devices with their start and end apart: 13 -> 15, of which waited for: 13 -> 5; matrix products, arithmetic and copies ran while one was open for 3% -> 7% of each run, Pallas kernels for 0% -> 24%
where the time goes in v1:
time: 85.6 us; the launch traced here: 84.3 us
  Pallas kernels  29.3 us (34%)
  starting transfers between devices  28.7 us (34%)
  waiting for transfers between devices  15.8 us (18%)
  local copies, waits for them, and re-layouts  5.39 us (6%)
  between operations  2.84 us (3%)
  other arithmetic  2.24 us (3%)
    pallas_call x5, Pallas kernels, window(): pl.pallas_call(functools.partial(window_kernel, None, prior is not None),...  29.3 us
    ppermute x5, starting transfers between devices, relay(): return lax.ppermute(value, axis, pairs)  15.4 us
    ppermute x8, waiting for transfers between devices, exchange(): return lax.ppermute(value, axis, [(i, i ^ bit) for i in range(count)])  14.6 us
    ppermute x8, starting transfers between devices, exchange(): return lax.ppermute(value, axis, [(i, i ^ bit) for i in range(count)])  7.4 us
    ppermute x2, starting transfers between devices, shift(): lax.ppermute(value, axis, [(i, i + by) for i in range(count) if 0 <= i +...  5.83 us
    another operation x1, local copies, waits for them, and re-layouts, shards(): jnp.stack([substeps[jnp.maximum(tile - 1, 0)], substeps[tile], substeps[j...  1.94 us
  transfers between devices with their start and end apart: 15, of which 5 were waited for; matrix products, arithmetic and copies ran while one was open for 7% of the time, Pallas kernels for 24%

profile of v1, /device:TPU:8, one launch (start us, length us, event | category | flops | bytes accessed | tf_op | source)
XLA Modules:
  0.0 84.3 jit_solution(10232932529190828425)
XLA Ops:
  0.0 1.1 %select_maximum_fusion = f32[3,16,8,256]{3,2,1,0:T(8,128)S(1)} fusion(f32[1,15,8,256]{3,2,1,0:T(8,128)} %param.9, f32[2,16,8,256]{3,2,1,0:T(8,128)} %bitcast.6), kind=kLoop, calls=%fused_computation.7 | loop fusion | flops 294912 | bytes 778240 | tf_op jit(solution)/shard_map/concatenate | solution.py:188
  1.2 0.6 dynamic_slice.15
  3.8 1.6 %collective-permute-start.3 = (f32[3,8,8,256]{3,2,1,0:T(8,128)S(1)}, f32[3,8,8,256]{3,2,1,0:T(8,128)S(1)}, u32[]{:S(2)}, u32[]{:S(2)}) collective-permute-start(f32[3,8,8,256]{3,2,1,0:T(8,128)S(1)} %select_select_fusion), channel_id=1, source_target_pairs={{0,2},{1,3},{2,0},{3,1},{4,6},{5,7},{6,4},{7,5},{8,10},{9,11},{10,... | collective-permute-start | bytes 589832 | tf_op jit(solution)/shard_map/ppermute | solution.py:17
  6.0 5.1 %collective-permute-done.3 = f32[3,8,8,256]{3,2,1,0:T(8,128)S(1)} collective-permute-done((f32[3,8,8,256]{3,2,1,0:T(8,128)S(1)}, f32[3,8,8,256]{3,2,1,0:T(8,128)S(1)}, u32[]{:S(2)}, u32[]{:S(2)}) %collective-permute-start.3) | collective-permute-done | bytes 196640 | tf_op jit(solution)/shard_map/ppermute | solution.py:17
  11.2 1.6 %collective-permute-start.4 = (f32[2,8,8,256]{3,2,1,0:T(8,128)S(1)}, f32[2,8,8,256]{3,2,1,0:T(8,128)S(1)}, u32[]{:S(2)}, u32[]{:S(2)}) collective-permute-start(f32[2,8,8,256]{3,2,1,0:T(8,128)S(1)} %slice.50), channel_id=1, source_target_pairs={{0,4},{4,0},{8,12},{12,8},{16,20},{20,16},{24,28},{28,24},{1,5},{5... | collective-permute-start | bytes 393224 | tf_op jit(solution)/shard_map/ppermute | solution.py:17
  12.8 3.6 %collective-permute-done.4 = f32[2,8,8,256]{3,2,1,0:T(8,128)S(1)} collective-permute-done((f32[2,8,8,256]{3,2,1,0:T(8,128)S(1)}, f32[2,8,8,256]{3,2,1,0:T(8,128)S(1)}, u32[]{:S(2)}, u32[]{:S(2)}) %collective-permute-start.4) | collective-permute-done | bytes 131104 | tf_op jit(solution)/shard_map/ppermute | solution.py:17
  16.4 3.5 %collective-permute-start.5 = (f32[2,8,8,256]{3,2,1,0:T(8,128)S(1)}, f32[2,8,8,256]{3,2,1,0:T(8,128)S(1)}, u32[]{:S(2)}, u32[]{:S(2)}) collective-permute-start(f32[2,8,8,256]{3,2,1,0:T(8,128)S(1)} %collective-permute-done.4), channel_id=1, source_target_pairs={{0,8},{8,16},{16,24},{12,4},{20,12},{28,20},{1,9},{9,17},{17,25},{... | collective-permute-start | bytes 393224 | tf_op jit(solution)/shard_map/ppermute | solution.py:28
  19.9 0.7 fusion.5
  20.5 1.9 %collective-permute-start = (f32[1,16,8,256]{3,2,1,0:T(8,128)}, f32[1,16,8,256]{3,2,1,0:T(8,128)S(1)}, u32[]{:S(2)}, u32[]{:S(2)}) collective-permute-start(f32[1,16,8,256]{3,2,1,0:T(8,128)} %get-tuple-element.9), channel_id=1, source_target_pairs={{4,0},{8,4},{12,8},{16,12},{20,16},{24,20},{28,24},{5,1},{9,5},{13... | collective-permute-start | bytes 393224 | tf_op jit(solution)/shard_map/ppermute | solution.py:22
  22.4 3.9 %collective-permute-start.1 = (f32[1,16,8,256]{3,2,1,0:T(8,128)}, f32[1,16,8,256]{3,2,1,0:T(8,128)}, u32[]{:S(2)}, u32[]{:S(2)}) collective-permute-start(f32[1,16,8,256]{3,2,1,0:T(8,128)} %get-tuple-element.9), channel_id=1, source_target_pairs={{0,4},{4,8},{8,12},{12,16},{16,20},{20,24},{24,28},{1,5},{5,9},{9,... | collective-permute-start | bytes 393224 | tf_op jit(solution)/shard_map/ppermute | solution.py:22
  26.4 1.4 %collective-permute-start.7 = (f32[1,16,8,256]{3,2,1,0:T(8,128)S(1)}, f32[1,16,8,256]{3,2,1,0:T(8,128)S(1)}, u32[]{:S(2)}, u32[]{:S(2)}) collective-permute-start(f32[1,16,8,256]{3,2,1,0:T(8,128)S(1)} %get-tuple-element.8), channel_id=1, source_target_pairs={{0,4},{4,0},{8,12},{12,8},{16,20},{20,16},{24,28},{28,24},{1,5},{5... | collective-permute-start | bytes 393224 | tf_op jit(solution)/shard_map/ppermute | solution.py:17
  27.8 0.1 collective-permute-start.6
  27.9 0.9 %fusion.4 = (f32[2,16,8,256]{3,2,1,0:T(8,128)}, f32[2,16,8,256]{3,2,1,0:T(8,128)}, f32[2,16,8,256]{3,2,1,0:T(8,128)}) fusion(f32[8,16,8,256]{3,2,1,0:T(8,128)S(1)} %copy-done), kind=kLoop, calls=%fused_computation.21 | loop fusion | bytes 1572864 | tf_op jit(solution)/shard_map/slice | solution.py:211
  28.8 0.7 collective-permute-start.13
  29.5 4.7 %collective-permute-done.7.pair = f32[1,16,8,256]{3,2,1,0:T(8,128)S(1)} collective-permute-done((f32[1,16,8,256]{3,2,1,0:T(8,128)S(1)}, f32[1,16,8,256]{3,2,1,0:T(8,128)S(1)}, u32[]{:S(2)}, u32[]{:S(2)}) %collective-permute-start.7) | collective-permute-done | bytes 131104 | tf_op jit(solution)/shard_map/ppermute | solution.py:17
  34.2 1.6 %collective-permute-start.11 = (f32[2,16,8,256]{3,2,1,0:T(8,128)}, f32[2,16,8,256]{3,2,1,0:T(8,128)S(1)}, u32[]{:S(2)}, u32[]{:S(2)}) collective-permute-start(f32[2,16,8,256]{3,2,1,0:T(8,128)} %get-tuple-element.6), channel_id=1, source_target_pairs={{0,4},{4,0},{8,12},{12,8},{16,20},{20,16},{24,28},{28,24},{1,5},{5... | collective-permute-start | bytes 786440 | tf_op jit(solution)/shard_map/ppermute | solution.py:17
  35.8 0.4 collective-permute-start.9
  36.2 0.7 copy-done.2
  36.9 0.6 fusion.6
  37.5 1.9 %stack.19.scalars = s32[5]{0:T(128)S(1)} concatenate(s32[1]{0:T(128)} %get-tuple-element.18, s32[1]{0:T(128)} %get-tuple-element.19, s32[1]{0:T(128)} %get-tuple-element.17, s32[1]{0:T(128)} %bitcast, s32[1]{0:T(128)} %bitcast.1), dimensions={0} | concatenate | bytes 40 | tf_op jit(solution)/shard_map/stack | solution.py:175
  39.4 3.5 %collective-permute-start.8 = (f32[1,16,8,256]{3,2,1,0:T(8,128)S(1)}, f32[1,16,8,256]{3,2,1,0:T(8,128)S(1)}, u32[]{:S(2)}, u32[]{:S(2)}) collective-permute-start(f32[1,16,8,256]{3,2,1,0:T(8,128)S(1)} %collective-permute-done.7.pair), channel_id=1, source_target_pairs={{0,8},{8,16},{16,24},{12,4},{20,12},{28,20},{1,9},{9,17},{17,25},{... | collective-permute-start | bytes 393224 | tf_op jit(solution)/shard_map/ppermute | solution.py:28
  42.9 0.9 %broadcast_select_fusion.3 = (f32[1,16,8,256]{3,2,1,0:T(8,128)S(1)}, f32[1,16,8,256]{3,2,1,0:T(8,128)S(1)}) fusion(f32[1,16,8,256]{3,2,1,0:T(8,128)} %collective-permute-done.1, f32[1,16,8,256]{3,2,1,0:T(8,128)S(1)} %collective-permute-done, pred[]{:T(512)S(6)} %eq.20), kind=kLoop, calls=%fused_computation.19 | loop fusion | flops 65536 | bytes 524289 | tf_op jit(solution)/shard_map/jit(_where)/select_n | solution.py:217
  43.8 1.9 %collective-permute-start.14 = (f32[2,16,8,256]{3,2,1,0:T(8,128)S(1)}, f32[2,16,8,256]{3,2,1,0:T(8,128)S(1)}, u32[]{:S(2)}, u32[]{:S(2)}) collective-permute-start(f32[2,16,8,256]{3,2,1,0:T(8,128)S(1)} %collective-permute-done.13.pair), channel_id=1, source_target_pairs={{0,8},{8,16},{16,24},{12,4},{20,12},{28,20},{1,9},{9,17},{17,25},{... | collective-permute-start | bytes 786440 | tf_op jit(solution)/shard_map/ppermute | solution.py:28
  45.8 3.1 %collective-permute-start.12 = (f32[2,16,8,256]{3,2,1,0:T(8,128)S(1)}, f32[2,16,8,256]{3,2,1,0:T(8,128)S(1)}, u32[]{:S(2)}, u32[]{:S(2)}) collective-permute-start(f32[2,16,8,256]{3,2,1,0:T(8,128)S(1)} %collective-permute-done.11.pair), channel_id=1, source_target_pairs={{0,8},{8,16},{16,24},{12,4},{20,12},{28,20},{1,9},{9,17},{17,25},{... | collective-permute-start | bytes 786440 | tf_op jit(solution)/shard_map/ppermute | solution.py:28
  48.9 1.2 %collective-permute-done.9.pair = f32[2,16,8,256]{3,2,1,0:T(8,128)S(1)} collective-permute-done((f32[2,16,8,256]{3,2,1,0:T(8,128)}, f32[2,16,8,256]{3,2,1,0:T(8,128)S(1)}, u32[]{:S(2)}, u32[]{:S(2)}) %collective-permute-start.9) | collective-permute-done | bytes 262176 | tf_op jit(solution)/shard_map/ppermute | solution.py:17
  50.1 3.5 %collective-permute-start.10 = (f32[2,16,8,256]{3,2,1,0:T(8,128)S(1)}, f32[2,16,8,256]{3,2,1,0:T(8,128)S(1)}, u32[]{:S(2)}, u32[]{:S(2)}) collective-permute-start(f32[2,16,8,256]{3,2,1,0:T(8,128)S(1)} %collective-permute-done.9.pair), channel_id=1, source_target_pairs={{0,8},{8,16},{16,24},{12,4},{20,12},{28,20},{1,9},{9,17},{17,25},{... | collective-permute-start | bytes 786440 | tf_op jit(solution)/shard_map/ppermute | solution.py:28
  53.7 1.2 %collective-permute-done.14.far = f32[2,16,8,256]{3,2,1,0:T(8,128)S(1)} collective-permute-done((f32[2,16,8,256]{3,2,1,0:T(8,128)S(1)}, f32[2,16,8,256]{3,2,1,0:T(8,128)S(1)}, u32[]{:S(2)}, u32[]{:S(2)}) %collective-permute-start.14) | collective-permute-done | bytes 262176 | tf_op jit(solution)/shard_map/ppermute | solution.py:28
  55.0 6.7 %shard_map.64.rest_0_ = f32[8,16,8,256]{3,2,1,0:T(8,128)} custom-call(s32[5]{0:T(128)S(1)} %stack.19.scalars, f32[8,16,8,256]{3,2,1,0:T(8,128)S(1)} %copy-done, f32[2,16,8,256]{3,2,1,0:T(8,128)S(1)} %collective-permute-done.13.pair, f32[2,16,8,256]{3,2,1,0:T(8,128)S(1)} %collective-permute-done.14.far, f32[2,16,8,256]{3,2,1,0:T(8,128)S(1)} %get-tuple-element.11.wind_own, ...), custom_call_target="tpu_custom_call" | custom-call | flops 18874368 | bytes 4194304 | tf_op jit(solution)/shard_map/pallas_call | solution.py:153
  61.7 6.7 %shard_map.65.rest_0_ = f32[8,16,8,256]{3,2,1,0:T(8,128)} custom-call(s32[5]{0:T(128)S(1)} %stack.19.scalars, f32[8,16,8,256]{3,2,1,0:T(8,128)S(1)} %copy-done, f32[2,16,8,256]{3,2,1,0:T(8,128)S(1)} %collective-permute-done.11.pair, f32[2,16,8,256]{3,2,1,0:T(8,128)S(1)} %collective-permute-done.12.far, ...), custom_call_target="tpu_custom_call", output_to_operand_aliasing={{}: (9, {})} | custom-call | flops 18874368 | bytes 4194304 | tf_op jit(solution)/shard_map/pallas_call | solution.py:153
  68.4 6.7 %shard_map.66.rest_0_ = f32[8,16,8,256]{3,2,1,0:T(8,128)} custom-call(s32[5]{0:T(128)S(1)} %stack.19.scalars, f32[8,16,8,256]{3,2,1,0:T(8,128)S(1)} %copy-done, f32[2,16,8,256]{3,2,1,0:T(8,128)S(1)} %collective-permute-done.9.pair, f32[2,16,8,256]{3,2,1,0:T(8,128)S(1)} %collective-permute-done.10.far, ...), custom_call_target="tpu_custom_call", output_to_operand_aliasing={{}: (9, {})} | custom-call | flops 18874368 | bytes 4194304 | tf_op jit(solution)/shard_map/pallas_call | solution.py:153
  75.1 4.6 %shard_map.67.rest_0_ = f32[8,16,8,256]{3,2,1,0:T(8,128)} custom-call(s32[5]{0:T(128)S(1)} %stack.19.scalars, f32[8,16,8,256]{3,2,1,0:T(8,128)S(1)} %copy-done, f32[1,16,8,256]{3,2,1,0:T(8,128)S(1)} %collective-permute-done.7.pair, f32[1,16,8,256]{3,2,1,0:T(8,128)S(1)} %collective-permute-done.8.far, ...), custom_call_target="tpu_custom_call", output_to_operand_aliasing={{}: (9, {})} | custom-call | flops 9437184 | bytes 4194304 | tf_op jit(solution)/shard_map/pallas_call | solution.py:153
  79.7 4.6 %shard_map.68 = f32[8,16,8,256]{3,2,1,0:T(8,128)} custom-call(s32[5]{0:T(128)S(1)} %stack.19.scalars, f32[8,16,8,256]{3,2,1,0:T(8,128)S(1)} %copy-done, f32[1,16,8,256]{3,2,1,0:T(8,128)S(1)} %get-tuple-element.16.pair, f32[1,16,8,256]{3,2,1,0:T(8,128)S(1)} %get-tuple-element.15.far, ...), custom_call_target="tpu_custom_call", output_to_operand_aliasing={{}: (9, {})} | custom-call | flops 9437184 | bytes 4194304 | tf_op jit(solution)/shard_map/pallas_call | solution.py:153
  (26 shorter events, 0.4 us)
Async XLA Ops:
  0.0 1.2 %copy-start.3 = (s32[8]{0:T(128)S(1)}, s32[8]{0:T(128)}, u32[]{:S(2)}) copy-start(s32[8]{0:T(128)} %param.11) | copy-start | bytes 100
  1.1 18.8 %copy-start = (f32[8,16,8,256]{3,2,1,0:T(8,128)S(1)}, f32[8,16,8,256]{3,2,1,0:T(8,128)}, u32[]{:S(2)}) copy-start(f32[8,16,8,256]{3,2,1,0:T(8,128)} %own.9) | copy-start | bytes 3145732
  1.1 2.6 %collective-permute-start.2 = (f32[3,8,8,256]{3,2,1,0:T(8,128)S(1)}, f32[3,8,8,256]{3,2,1,0:T(8,128)S(1)}, u32[]{:S(2)}, u32[]{:S(2)}) collective-permute-start(f32[3,8,8,256]{3,2,1,0:T(8,128)S(1)} %slice_select_fusion), channel_id=1, source_target_pairs={{0,1},{1,0},{2,3},{3,2},{4,5},{5,4},{6,7},{7,6},{8,9},{9,8},{10,11... | collective-permute-start | bytes 589832 | tf_op jit(solution)/shard_map/ppermute | solution.py:17
  3.8 7.4 %collective-permute-start.3 = (f32[3,8,8,256]{3,2,1,0:T(8,128)S(1)}, f32[3,8,8,256]{3,2,1,0:T(8,128)S(1)}, u32[]{:S(2)}, u32[]{:S(2)}) collective-permute-start(f32[3,8,8,256]{3,2,1,0:T(8,128)S(1)} %select_select_fusion), channel_id=1, source_target_pairs={{0,2},{1,3},{2,0},{3,1},{4,6},{5,7},{6,4},{7,5},{8,10},{9,11},{10,... | collective-permute-start | bytes 589832 | tf_op jit(solution)/shard_map/ppermute | solution.py:17
  11.2 5.2 %collective-permute-start.4 = (f32[2,8,8,256]{3,2,1,0:T(8,128)S(1)}, f32[2,8,8,256]{3,2,1,0:T(8,128)S(1)}, u32[]{:S(2)}, u32[]{:S(2)}) collective-permute-start(f32[2,8,8,256]{3,2,1,0:T(8,128)S(1)} %slice.50), channel_id=1, source_target_pairs={{0,4},{4,0},{8,12},{12,8},{16,20},{20,16},{24,28},{28,24},{1,5},{5... | collective-permute-start | bytes 393224 | tf_op jit(solution)/shard_map/ppermute | solution.py:17
  16.4 11.4 %collective-permute-start.5 = (f32[2,8,8,256]{3,2,1,0:T(8,128)S(1)}, f32[2,8,8,256]{3,2,1,0:T(8,128)S(1)}, u32[]{:S(2)}, u32[]{:S(2)}) collective-permute-start(f32[2,8,8,256]{3,2,1,0:T(8,128)S(1)} %collective-permute-done.4), channel_id=1, source_target_pairs={{0,8},{8,16},{16,24},{12,4},{20,12},{28,20},{1,9},{9,17},{17,25},{... | collective-permute-start | bytes 393224 | tf_op jit(solution)/shard_map/ppermute | solution.py:28
  20.5 15.3 %collective-permute-start = (f32[1,16,8,256]{3,2,1,0:T(8,128)}, f32[1,16,8,256]{3,2,1,0:T(8,128)S(1)}, u32[]{:S(2)}, u32[]{:S(2)}) collective-permute-start(f32[1,16,8,256]{3,2,1,0:T(8,128)} %get-tuple-element.9), channel_id=1, source_target_pairs={{4,0},{8,4},{12,8},{16,12},{20,16},{24,20},{28,24},{5,1},{9,5},{13... | collective-permute-start | bytes 393224 | tf_op jit(solution)/shard_map/ppermute | solution.py:22
  22.4 17.0 %collective-permute-start.1 = (f32[1,16,8,256]{3,2,1,0:T(8,128)}, f32[1,16,8,256]{3,2,1,0:T(8,128)}, u32[]{:S(2)}, u32[]{:S(2)}) collective-permute-start(f32[1,16,8,256]{3,2,1,0:T(8,128)} %get-tuple-element.9), channel_id=1, source_target_pairs={{0,4},{4,8},{8,12},{12,16},{16,20},{20,24},{24,28},{1,5},{5,9},{9,... | collective-permute-start | bytes 393224 | tf_op jit(solution)/shard_map/ppermute | solution.py:22
  26.4 7.8 %collective-permute-start.7 = (f32[1,16,8,256]{3,2,1,0:T(8,128)S(1)}, f32[1,16,8,256]{3,2,1,0:T(8,128)S(1)}, u32[]{:S(2)}, u32[]{:S(2)}) collective-permute-start(f32[1,16,8,256]{3,2,1,0:T(8,128)S(1)} %get-tuple-element.8), channel_id=1, source_target_pairs={{0,4},{4,0},{8,12},{12,8},{16,20},{20,16},{24,28},{28,24},{1,5},{5... | collective-permute-start | bytes 393224 | tf_op jit(solution)/shard_map/ppermute | solution.py:17
  27.8 25.8 %collective-permute-start.6 = (f32[7,8,8,256]{3,2,1,0:T(8,128)S(1)}, f32[7,8,8,256]{3,2,1,0:T(8,128)S(1)}, u32[]{:S(2)}, u32[]{:S(2)}) collective-permute-start(f32[7,8,8,256]{3,2,1,0:T(8,128)S(1)} %pad_maximum_fusion), channel_id=1, source_target_pairs={{0,1},{1,0},{2,3},{3,2},{4,5},{5,4},{6,7},{7,6},{8,9},{9,8},{10,11... | collective-permute-start | bytes 1376264 | tf_op jit(solution)/shard_map/ppermute | solution.py:17
  28.8 15.1 %collective-permute-start.13 = (f32[2,16,8,256]{3,2,1,0:T(8,128)}, f32[2,16,8,256]{3,2,1,0:T(8,128)S(1)}, u32[]{:S(2)}, u32[]{:S(2)}) collective-permute-start(f32[2,16,8,256]{3,2,1,0:T(8,128)} %get-tuple-element.5), channel_id=1, source_target_pairs={{0,4},{4,0},{8,12},{12,8},{16,20},{20,16},{24,28},{28,24},{1,5},{5... | collective-permute-start | bytes 786440 | tf_op jit(solution)/shard_map/ppermute | solution.py:17
  34.2 11.6 %collective-permute-start.11 = (f32[2,16,8,256]{3,2,1,0:T(8,128)}, f32[2,16,8,256]{3,2,1,0:T(8,128)S(1)}, u32[]{:S(2)}, u32[]{:S(2)}) collective-permute-start(f32[2,16,8,256]{3,2,1,0:T(8,128)} %get-tuple-element.6), channel_id=1, source_target_pairs={{0,4},{4,0},{8,12},{12,8},{16,20},{20,16},{24,28},{28,24},{1,5},{5... | collective-permute-start | bytes 786440 | tf_op jit(solution)/shard_map/ppermute | solution.py:17
  35.8 14.2 %collective-permute-start.9 = (f32[2,16,8,256]{3,2,1,0:T(8,128)}, f32[2,16,8,256]{3,2,1,0:T(8,128)S(1)}, u32[]{:S(2)}, u32[]{:S(2)}) collective-permute-start(f32[2,16,8,256]{3,2,1,0:T(8,128)} %get-tuple-element.7), channel_id=1, source_target_pairs={{0,4},{4,0},{8,12},{12,8},{16,20},{20,16},{24,28},{28,24},{1,5},{5... | collective-permute-start | bytes 786440 | tf_op jit(solution)/shard_map/ppermute | solution.py:17
  36.2 0.7 copy-start.2
  39.4 35.7 %collective-permute-start.8 = (f32[1,16,8,256]{3,2,1,0:T(8,128)S(1)}, f32[1,16,8,256]{3,2,1,0:T(8,128)S(1)}, u32[]{:S(2)}, u32[]{:S(2)}) collective-permute-start(f32[1,16,8,256]{3,2,1,0:T(8,128)S(1)} %collective-permute-done.7.pair), channel_id=1, source_target_pairs={{0,8},{8,16},{16,24},{12,4},{20,12},{28,20},{1,9},{9,17},{17,25},{... | collective-permute-start | bytes 393224 | tf_op jit(solution)/shard_map/ppermute | solution.py:28
  43.8 11.1 %collective-permute-start.14 = (f32[2,16,8,256]{3,2,1,0:T(8,128)S(1)}, f32[2,16,8,256]{3,2,1,0:T(8,128)S(1)}, u32[]{:S(2)}, u32[]{:S(2)}) collective-permute-start(f32[2,16,8,256]{3,2,1,0:T(8,128)S(1)} %collective-permute-done.13.pair), channel_id=1, source_target_pairs={{0,8},{8,16},{16,24},{12,4},{20,12},{28,20},{1,9},{9,17},{17,25},{... | collective-permute-start | bytes 786440 | tf_op jit(solution)/shard_map/ppermute | solution.py:28
  45.8 15.9 %collective-permute-start.12 = (f32[2,16,8,256]{3,2,1,0:T(8,128)S(1)}, f32[2,16,8,256]{3,2,1,0:T(8,128)S(1)}, u32[]{:S(2)}, u32[]{:S(2)}) collective-permute-start(f32[2,16,8,256]{3,2,1,0:T(8,128)S(1)} %collective-permute-done.11.pair), channel_id=1, source_target_pairs={{0,8},{8,16},{16,24},{12,4},{20,12},{28,20},{1,9},{9,17},{17,25},{... | collective-permute-start | bytes 786440 | tf_op jit(solution)/shard_map/ppermute | solution.py:28
  50.1 18.3 %collective-permute-start.10 = (f32[2,16,8,256]{3,2,1,0:T(8,128)S(1)}, f32[2,16,8,256]{3,2,1,0:T(8,128)S(1)}, u32[]{:S(2)}, u32[]{:S(2)}) collective-permute-start(f32[2,16,8,256]{3,2,1,0:T(8,128)S(1)} %collective-permute-done.9.pair), channel_id=1, source_target_pairs={{0,8},{8,16},{16,24},{12,4},{20,12},{28,20},{1,9},{9,17},{17,25},{... | collective-permute-start | bytes 786440 | tf_op jit(solution)/shard_map/ppermute | solution.py:28
  53.7 1.3 %copy-start.1 = (f32[8,8,256]{2,1,0:T(8,128)S(1)}, f32[8,8,256]{2,1,0:T(8,128)}, u32[]{:S(2)}) copy-start(f32[8,8,256]{2,1,0:T(8,128)} %source.9) | copy-start | bytes 196612

commit v2 on v0

v2 whole, which is shorter than its diff:
```python
import functools

import jax
import jax.numpy as jnp
from jax import lax
from jax.experimental import pallas as pl
from jax.experimental.pallas import tpu as pltpu
from jax.sharding import PartitionSpec as P

ROUNDS = 6
DEEP = 8
RELAYED = (3, 3)
STRAIGHT = 2
VMEM_LIMIT = 32 * 1024 * 1024


def exchange(value, axis, bit):
    count = lax.axis_size(axis)
    return lax.ppermute(value, axis, [(i, i ^ bit) for i in range(count)])


def shift(value, axis, by):
    count = lax.axis_size(axis)
    return lax.ppermute(value, axis, [(i, i + by) for i in range(count) if 0 <= i + by < count])


def relay(value, axis):
    count = lax.axis_size(axis)
    pairs = [(i, i + 2) for i in range(0, count - 2, 2)] + [(i, i - 2) for i in range(3, count, 2)]
    return lax.ppermute(value, axis, pairs)


def in_vmem(values):
    return [pltpu.with_memory_space_constraint(value, pltpu.VMEM) for value in values]


def counts_of(substeps, tile, tiles):
    south, north = jnp.maximum(tile - 1, 0), jnp.minimum(tile + 1, tiles - 1)
    return [substeps[south], substeps[tile], substeps[north]]


def first_choice_kernel(loader, wind, wind_other, diffusion, diffusion_other, *rest):
    out = rest[-1]
    slot, group = loader[lax.axis_index("tile")], lax.axis_index("group")
    mine = slot % 2 == group % 2
    half = out.shape[1]
    base = group % 2 * half
    for k in range(half):
        for kind in range(2):
            out[kind, k] = jnp.where(mine, wind[0, kind, base + k], wind_other[0, kind, base + k])
        at = jnp.minimum(base + k, diffusion.shape[1] - 1)
        out[2, k] = jnp.where(mine, diffusion[0, at], diffusion_other[0, at])


def next_choice_kernel(bit, loader, met, other, out):
    slot, group = loader[lax.axis_index("tile")], lax.axis_index("group")
    out[...] = jnp.where((slot & bit) == (group & bit), met[...], other[...])


def last_choice_kernel(bit, loader, met, other, *rest):
    wind, up, down, mix = rest[-4:]
    slot, group = loader[lax.axis_index("tile")], lax.axis_index("group")
    mine = (slot & bit) == (group & bit)
    _, height, deep, width = wind.shape
    reach = up.shape[1]
    for kind in range(2):
        for j in range(height):
            value = jnp.where(mine, met[kind, :, j, :], other[kind, :, j, :])
            wind[kind, j] = value
            if j < reach:
                down[kind, j] = value
            if j >= height - reach:
                up[kind, j - (height - reach)] = value
    mix[...] = jnp.where(mine, met[2], other[2])


def pack_kernel(relayed, tracers, *outs):
    even = lax.axis_index("tile") % 2 == 0
    _, levels, height, _ = tracers.shape
    rest, up, down = outs[-3:]
    reach = up.shape[2]
    skip = height - reach
    for g in range(levels // DEEP):
        deep = slice(g * DEEP, (g + 1) * DEEP)
        start = 0
        for part, count in zip(outs, relayed):
            for n in range(start, start + count):
                rows = [tracers[n, deep, j, :] for j in range(height)]
                for j in range(reach):
                    part[n - start, g, j] = jnp.where(even, rows[j], rows[j + skip])
                for j in range(skip):
                    rest[n, g, j] = jnp.where(even, rows[reach + j], rows[j])
            start += count
        for n in range(up.shape[0]):
            for j in range(reach):
                up[n, g, j] = tracers[start + n, deep, skip + j, :]
                down[n, g, j] = tracers[start + n, deep, j, :]


def on_core(kernel, scalars, operands, out_shape, waits=(), cost=1):
    vmem = pl.BlockSpec(memory_space=pltpu.VMEM)
    return pl.pallas_call(
        kernel,
        out_shape=out_shape,
        in_specs=[pl.BlockSpec(memory_space=pltpu.SMEM)] * len(scalars)
        + [vmem] * len(operands)
        + [pl.BlockSpec(memory_space=pl.ANY)] * len(waits),
        out_specs=jax.tree.map(lambda _: vmem, out_shape),
        compiler_params=pltpu.CompilerParams(vmem_limit_bytes=VMEM_LIMIT),
        cost_estimate=pl.CostEstimate(
            flops=0, bytes_accessed=cost * 1024 * 1024, transcendentals=0
        ),
    )(*scalars, *in_vmem(operands), *waits)


def prepare_kernel(tiles, substeps, own, own_other, up, up_other, down, down_other, mix, mix_other, *rest):
    coef, solve, faces, mixing = rest[-4:]
    _, height, _, width = own.shape
    reach = up.shape[1]
    groups = 2
    levels = groups * DEEP
    tile, core = lax.axis_index("tile"), lax.axis_index("group") % 2
    for g, here, south, north, mixed in (
        (core, own, up, down, mix),
        (1 - core, own_other, up_other, down_other, mix_other),
    ):
        for kind in range(2):
            for j in range(height):
                value = here[kind, j]
                if kind == 1 and j == 0:
                    value = jnp.where(tile == 0, 0.0, value)
                faces[kind, g, height + j] = value
            for j in range(reach):
                faces[kind, g, height - reach + j] = south[kind, j]
                faces[kind, g, 2 * height + j] = north[kind, j]
        for k in range(DEEP):
            mixing[g * DEEP + k] = mixed[k]
    counts = counts_of(substeps, tile, tiles)
    ones = jnp.ones((DEEP, width), jnp.float32)
    fractions = [ones / (ones * count.astype(jnp.float32)) for count in counts]
    reach -= 1
    for g in range(groups):
        for j in range(height - reach, 2 * height + reach):
            f = fractions[j // height]
            zonal, south, north = faces[0, g, j], faces[1, g, j], faces[1, g, j + 1]
            zonal_east = pltpu.roll(zonal, width - 1, 1)
            coef[g, j, 0] = 1.0 - f * (
                (jnp.maximum(zonal_east, 0.0) - jnp.minimum(zonal, 0.0))
                + (jnp.maximum(north, 0.0) - jnp.minimum(south, 0.0))
            )
            coef[g, j, 1] = f * jnp.maximum(zonal, 0.0)
            coef[g, j, 2] = -f * jnp.minimum(zonal_east, 0.0)
            coef[g, j, 3] = f * jnp.maximum(south, 0.0)
            coef[g, j, 4] = -f * jnp.minimum(north, 0.0)
    for j in range(height - reach, 2 * height + reach):
        coef[groups, j, 0] = ones
        for k in range(1, 5):
            coef[groups, j, k] = jnp.zeros_like(ones)
    ratio = lower = jnp.zeros((height, width), jnp.float32)
    for k in range(levels):
        upper = mixing[k] if k < levels - 1 else jnp.zeros_like(lower)
        pivot = 1.0 / (1.0 + lower + upper - lower * ratio)
        ratio = upper * pivot
        solve[k, 0] = lower
        solve[k, 1] = pivot
        solve[k, 2] = ratio
        lower = upper


def prepare(tiles, substeps, winds, mix, waits):
    _, height, half, width = winds[0].shape
    vmem = pl.BlockSpec(memory_space=pltpu.VMEM)
    return pl.pallas_call(
        functools.partial(prepare_kernel, tiles),
        out_shape=(
            pltpu.VMEM((3, 3 * height, 5, DEEP, width), jnp.float32),
            pltpu.VMEM((2 * half, 3, height, width), jnp.float32),
        ),
        in_specs=[pl.BlockSpec(memory_space=pltpu.SMEM)]
        + [vmem] * 8
        + [pl.BlockSpec(memory_space=pl.ANY)] * len(waits),
        out_specs=(vmem, vmem),
        scratch_shapes=[
            pltpu.VMEM((2, 2, 3 * height, DEEP, width), jnp.float32),
            pltpu.VMEM((2 * half, height, width), jnp.float32),
        ],
        compiler_params=pltpu.CompilerParams(vmem_limit_bytes=VMEM_LIMIT),
        cost_estimate=pl.CostEstimate(flops=0, bytes_accessed=4 * 1024 * 1024, transcendentals=0),
    )(substeps, *in_vmem([*winds, *mix]), *waits)


def window_kernel(start, last, tiles, substeps, coef, solve, own, source, *rest):
    if last:
        up, down, prior, out, field, advected, values, solved, sem = rest
        early = pltpu.make_async_copy(prior.at[:start], out.at[:start], sem.at[0])
        early.start()
        tracers, reach = up.shape[0], up.shape[2]
    else:
        pair, pair_rest, far, *rest = rest
        out, field, advected, values = rest[-4:]
        tracers, reach = pair.shape[0], pair.shape[2]
    _, levels, height, width = own.shape
    groups = levels // DEEP
    tile = lax.axis_index("tile")
    even = tile % 2 == 0
    pair_at = jnp.where(even, 3 * height - reach, 0)
    rest_at = jnp.where(even, 2 * height, reach)
    far_at = jnp.where(even, height - reach, 2 * height)
    counts = counts_of(substeps, tile, tiles)
    for n in range(tracers):
        for g in range(groups):
            deep = slice(g * DEEP, (g + 1) * DEEP)
            for j in range(height):
                field[0, n, g, height + j] = own[start + n, deep, j, :]
            for j in range(reach):
                if last:
                    field[0, n, g, height - reach + j] = up[n, g, j]
                    field[0, n, g, 2 * height + j] = down[n, g, j]
                else:
                    field[0, n, g, pair_at + j] = pair[n, g, j]
                    field[0, n, g, far_at + j] = far[n, g, j]
            if not last:
                for j in range(height - reach):
                    field[0, n, g, rest_at + j] = pair_rest[start + n, g, j]
    for step in range(ROUNDS):
        reach = ROUNDS - 1 - step
        low, high = height - reach, 2 * height + reach
        src, dst = step % 2, (step + 1) % 2
        for g in range(groups):
            pages = [jnp.where(step < count, g, groups) for count in counts]
            south = [field[src, n, g, low - 1] for n in range(tracers)]
            here = [field[src, n, g, low] for n in range(tracers)]
            for j in range(low, high):
                c = [coef[pages[j // height], j, k] for k in range(5)]
                for n in range(tracers):
                    north = field[src, n, g, j + 1]
                    new = (
                        c[0] * here[n]
                        + c[1] * pltpu.roll(here[n], 1, 1)
                        + c[2] * pltpu.roll(here[n], width - 1, 1)
                        + c[3] * south[n]
                        + c[4] * north
                    )
                    if step < ROUNDS - 1:
                        field[dst, n, g, j] = new
                    else:
                        advected[n, g * DEEP : (g + 1) * DEEP, j - height, :] = new
                    south[n], here[n] = here[n], north
    for k in range(levels):
        lower, pivot = solve[k, 0], solve[k, 1]
        for n in range(tracers):
            q = advected[n, k]
            q = q + (source[start + n] if k == 0 else lower * values[n, k - 1])
            values[n, k] = q * pivot
    for n in range(tracers):
        target = solved.at[n] if last else out.at[start + n]
        current = values[n, levels - 1]
        target[levels - 1] = current
        for k in range(levels - 2, -1, -1):
            current = values[n, k] + solve[k, 2] * current
            target[k] = current
    if last:
        late = pltpu.make_async_copy(solved, out.at[start:], sem.at[1])
        late.start()
        early.wait()
        late.wait()


def window(tiles, substeps, coef, solve, tracers, emissions, start, halos, prior):
    total, levels, height, width = tracers.shape
    count = halos[0].shape[0]
    groups = levels // DEEP
    last = start + count == total
    vmem = pl.BlockSpec(memory_space=pltpu.VMEM)
    operands = [coef, solve, tracers, emissions, *halos]
    scratch = [
        pltpu.VMEM((2, count, groups, 3 * height, DEEP, width), jnp.float32),
        pltpu.VMEM((count, levels, height, width), jnp.float32),
        pltpu.VMEM((count, levels, height, width), jnp.float32),
    ]
    aliases = {}
    if prior is not None:
        operands.append(prior)
        if not last:
            aliases = {len(operands): 0}
    if last:
        scratch += [
            pltpu.VMEM((count, levels, height, width), jnp.float32),
            pltpu.SemaphoreType.DMA((2,)),
        ]
    shape = tracers.shape
    return pl.pallas_call(
        functools.partial(window_kernel, start, last, tiles),
        out_shape=jax.ShapeDtypeStruct(shape, jnp.float32)
        if last
        else pltpu.VMEM(shape, jnp.float32),
        in_specs=[pl.BlockSpec(memory_space=pltpu.SMEM)] + [vmem] * len(operands),
        out_specs=pl.BlockSpec(memory_space=pl.ANY) if last else vmem,
        scratch_shapes=scratch,
        input_output_aliases=aliases,
        compiler_params=pltpu.CompilerParams(vmem_limit_bytes=VMEM_LIMIT),
        cost_estimate=pl.CostEstimate(
            flops=0, bytes_accessed=(2 + 4 * count) * 1024 * 1024, transcendentals=0
        ),
    )(substeps, *in_vmem(operands))


def shards(tracers, emissions, winds, diffusivity, substeps, loader):
    tiles, groups = lax.axis_size("tile"), lax.axis_size("group")
    _, levels, height, width = tracers.shape
    half = levels // 2
    relayed = sum(RELAYED)

    def rows_of(count, rows):
        return pltpu.VMEM((count, levels // DEEP, rows, DEEP, width), jnp.float32)

    *parts, rest, up, down = on_core(
        functools.partial(pack_kernel, RELAYED),
        [],
        [tracers],
        [rows_of(count, ROUNDS) for count in RELAYED]
        + [rows_of(relayed, height - ROUNDS), rows_of(STRAIGHT, ROUNDS), rows_of(STRAIGHT, ROUNDS)],
    )

    met = on_core(
        first_choice_kernel,
        [loader],
        [winds, exchange(winds, "group", 1), diffusivity, exchange(diffusivity, "group", 1)],
        pltpu.VMEM((3, half, height, width), jnp.float32),
    )
    bit = 2
    while 2 * bit < groups:
        met = on_core(
            functools.partial(next_choice_kernel, bit),
            [loader],
            [met, exchange(met, "group", bit)],
            pltpu.VMEM(met.shape, jnp.float32),
        )
        bit *= 2
    wind, wind_up, wind_down, mix = on_core(
        functools.partial(last_choice_kernel, bit),
        [loader],
        [met, exchange(met, "group", bit)],
        [
            pltpu.VMEM((2, height, half, width), jnp.float32),
            pltpu.VMEM((2, ROUNDS, half, width), jnp.float32),
            pltpu.VMEM((2, ROUNDS, half, width), jnp.float32),
            pltpu.VMEM((half, height, width), jnp.float32),
        ],
    )
    known = []
    for mine in (wind, shift(wind_up, "tile", 1), shift(wind_down, "tile", -1)):
        known += [mine, exchange(mine, "group", 1)]
    coef, solve = prepare(tiles, substeps, known, [mix, exchange(mix, "group", 1)], [])

    pairs = [exchange(part, "tile", 1) for part in parts]
    pair_rest = exchange(rest, "tile", 1)
    halos = [(pair, pair_rest, relay(pair, "tile")) for pair in pairs]
    halos.append((shift(up, "tile", 1), shift(down, "tile", -1)))
    result, start = None, 0
    for halo in halos:
        result = window(tiles, substeps, coef, solve, tracers, emissions, start, halo, result)
        start += halo[0].shape[0]
    return result


def solution(mesh):
    return jax.shard_map(
        shards,
        mesh=mesh,
        in_specs=(
            P("group", None, "tile", None),
            P("group", "tile", None),
            P("group", None, None, "tile", None),
            P("group", None, "tile", None),
            P(),
            P(),
        ),
        out_specs=P("group", None, "tile", None),
        check_vma=False,
    )
```

time: 151 us -> 50 us (0.33)
  waiting for transfers between devices: 67.1 us -> 8.15 us
  between operations: 19.3 us -> 0.2 us
  starting transfers between devices: 39.8 us -> 25.5 us
  other arithmetic: 12.3 us -> 0 us
  Pallas kernels: 0 us -> 11.5 us
  local copies, waits for them, and re-layouts: 12.2 us -> 4.39 us
    ppermute x12 -> x16, waiting for transfers between devices: 42.5 us -> 8.15 us  [the longest x10 8.13 us: exchange(): return lax.ppermute(value, axis, [(i, i ^ bit) for i in range(count)])]
    psum x1 -> x0, waiting for transfers between devices: 24.6 us -> none  [spread(): return lax.psum(jnp.where(mine, value, jnp.zeros_like(value)), axis)]
    ppermute x12 -> x16, starting transfers between devices: 39.8 us -> 25.5 us  [the longest x4 13.5 us: shift(): lax.ppermute(value, axis, [(i, i + by) for i in range(count) if 0 <= i +...]
    pallas_call x0 -> x7, Pallas kernels: none -> 11.5 us  [the longest x3 8.91 us: window(): pl.pallas_call(functools.partial(window_kernel, start, last, tiles), out_...]
    slice x46 -> x0, local copies, waits for them, and re-layouts: 6.36 us -> none  [the longest x12 2.26 us: zonal_tendency(): east_flux = jnp.roll(west_flux, -1, axis=3)]
    add x6 -> x0, other arithmetic: 4.09 us -> none  [shards(): jnp.maximum(meridional, 0.0) * from_south]
    sub x6 -> x0, other arithmetic: 3.85 us -> none  [shards(): mixing - fraction * (zonal_tendency(mixing, zonal) + (north_flux - south_...]
    ppermute x12 -> x0, local copies, waits for them, and re-layouts: 3.17 us -> none  [from_behind(): return lax.ppermute(value, axis, pairs)]
  transfers between devices with their start and end apart: 13 -> 16, of which waited for: 13 -> 2; matrix products, arithmetic and copies ran while one was open for 3% -> 0% of each run, Pallas kernels for 0% -> 17%
where the time goes in v2:
time: 50 us; the launch traced here: 49.7 us
  starting transfers between devices  25.5 us (51%)
  Pallas kernels  11.5 us (23%)
  waiting for transfers between devices  8.15 us (16%)
  local copies, waits for them, and re-layouts  4.39 us (9%)
    ppermute x4, starting transfers between devices, shift(): lax.ppermute(value, axis, [(i, i + by) for i in range(count) if 0 <= i +...  13.5 us
    pallas_call x3, Pallas kernels, window(): pl.pallas_call(functools.partial(window_kernel, start, last, tiles), out_...  8.91 us
    ppermute x10, waiting for transfers between devices, exchange(): return lax.ppermute(value, axis, [(i, i ^ bit) for i in range(count)])  8.13 us
    ppermute x2, starting transfers between devices, relay(): return lax.ppermute(value, axis, pairs)  6.96 us
    ppermute x10, starting transfers between devices, exchange(): return lax.ppermute(value, axis, [(i, i ^ bit) for i in range(count)])  5.06 us
    unnamed x14, local copies, waits for them, and re-layouts  4.39 us
    pallas_call x3, Pallas kernels, on_core(): pl.pallas_call(kernel, out_shape=out_shape, in_specs=[pl.BlockSpec(memory...  1.65 us
  transfers between devices with their start and end apart: 16, of which 2 were waited for; matrix products, arithmetic and copies ran while one was open for 0% of the time, Pallas kernels for 17%

profile of v2, /device:TPU:8, one launch (start us, length us, event | category | flops | bytes accessed | tf_op | source)
XLA Modules:
  0.0 49.7 jit_solution(741568660289655449)
XLA Ops:
  0.0 0.0 collective-permute-start
  0.0 0.5 %collective-permute-start.1 = (f32[1,15,8,256]{3,2,1,0:T(8,128)}, f32[1,15,8,256]{3,2,1,0:T(8,128)S(1)}, u32[]{:S(2)}, u32[]{:S(2)}) collective-permute-start(f32[1,15,8,256]{3,2,1,0:T(8,128)} %diffusion.1), channel_id=1, source_target_pairs={{0,1},{1,0},{2,3},{3,2},{4,5},{5,4},{6,7},{7,6},{8,9},{9,8},{10,11... | collective-permute-start | bytes 368648 | tf_op jit(solution)/shard_map/ppermute | solution.py:19
  0.5 1.2 %copy-done = f32[8,16,8,256]{3,2,1,0:T(8,128)S(1)} copy-done((f32[8,16,8,256]{3,2,1,0:T(8,128)S(1)}, f32[8,16,8,256]{3,2,1,0:T(8,128)}, u32[]{:S(2)}) %copy-start) | copy-done | bytes 1048600
  1.7 0.4 shard_map.67
  2.2 1.6 %collective-permute-start.11 = (f32[3,2,6,8,256]{4,3,2,1,0:T(8,128)S(1)}, f32[3,2,6,8,256]{4,3,2,1,0:T(8,128)S(1)}, u32[]{:S(2)}, u32[]{:S(2)}) collective-permute-start(f32[3,2,6,8,256]{4,3,2,1,0:T(8,128)S(1)} %get-tuple-element.24), channel_id=1, source_target_pairs={{0,4},{4,0},{8,12},{12,8},{16,20},{20,16},{24,28},{28,24},{1,5},{5... | collective-permute-start | bytes 884744 | tf_op jit(solution)/shard_map/ppermute | solution.py:19
  3.8 0.0 collective-permute-done.1.diffusion_other
  3.8 0.0 collective-permute-done.wind_other
  3.8 0.9 %copy-done.3 = f32[1,2,16,8,256]{4,3,2,1,0:T(8,128)S(1)} copy-done((f32[1,2,16,8,256]{4,3,2,1,0:T(8,128)S(1)}, f32[1,2,16,8,256]{4,3,2,1,0:T(8,128)}, u32[]{:S(2)}) %copy-start.3) | copy-done | bytes 262168
  4.7 0.9 %copy-done.4 = f32[1,15,8,256]{3,2,1,0:T(8,128)S(1)} copy-done((f32[1,15,8,256]{3,2,1,0:T(8,128)S(1)}, f32[1,15,8,256]{3,2,1,0:T(8,128)}, u32[]{:S(2)}) %copy-start.4) | copy-done | bytes 122904
  5.6 0.7 %copy-done.6 = s32[8]{0:T(128)S(1)} copy-done((s32[8]{0:T(128)S(1)}, s32[8]{0:T(128)}, u32[]{:S(2)}) %copy-start.6) | copy-done | bytes 56
  6.3 0.6 %shard_map.64.met = f32[3,8,8,256]{3,2,1,0:T(8,128)S(1)} custom-call(s32[8]{0:T(128)S(1)} %copy-done.6, f32[1,2,16,8,256]{4,3,2,1,0:T(8,128)S(1)} %copy-done.3, f32[1,2,16,8,256]{4,3,2,1,0:T(8,128)S(1)} %collective-permute-done.wind_other, f32[1,15,8,256]{3,2,1,0:T(8,128)S(1)} %copy-done.4, f32[1,15,8,256]{3,2,1,0:T(8,128)S(1)} %collective-permute-done.1.diffusion_other), custom_call_target="tpu_custom_call" | custom-call | bytes 1048576 | tf_op jit(solution)/shard_map/pallas_call | solution.py:102
  6.9 1.6 %collective-permute-start.2 = (f32[3,8,8,256]{3,2,1,0:T(8,128)S(1)}, f32[3,8,8,256]{3,2,1,0:T(8,128)S(1)}, u32[]{:S(2)}, u32[]{:S(2)}) collective-permute-start(f32[3,8,8,256]{3,2,1,0:T(8,128)S(1)} %shard_map.64.met), channel_id=1, source_target_pairs={{0,2},{1,3},{2,0},{3,1},{4,6},{5,7},{6,4},{7,5},{8,10},{9,11},{10,... | collective-permute-start | bytes 589832 | tf_op jit(solution)/shard_map/ppermute | solution.py:19
  8.4 0.5 %collective-permute-start.14 = (f32[3,2,6,8,256]{4,3,2,1,0:T(8,128)S(1)}, f32[3,2,6,8,256]{4,3,2,1,0:T(8,128)S(1)}, u32[]{:S(2)}, u32[]{:S(2)}) collective-permute-start(f32[3,2,6,8,256]{4,3,2,1,0:T(8,128)S(1)} %get-tuple-element.26), channel_id=1, source_target_pairs={{0,4},{4,0},{8,12},{12,8},{16,20},{20,16},{24,28},{28,24},{1,5},{5... | collective-permute-start | bytes 884744 | tf_op jit(solution)/shard_map/ppermute | solution.py:19
  8.9 4.5 %collective-permute-done.2.other = f32[3,8,8,256]{3,2,1,0:T(8,128)S(1)} collective-permute-done((f32[3,8,8,256]{3,2,1,0:T(8,128)S(1)}, f32[3,8,8,256]{3,2,1,0:T(8,128)S(1)}, u32[]{:S(2)}, u32[]{:S(2)}) %collective-permute-start.2) | collective-permute-done | bytes 196640 | tf_op jit(solution)/shard_map/ppermute | solution.py:19
  13.5 0.6 %shard_map.65 = (f32[2,8,8,256]{3,2,1,0:T(8,128)S(1)}, f32[2,6,8,256]{3,2,1,0:T(8,128)S(1)}, f32[2,6,8,256]{3,2,1,0:T(8,128)S(1)}, f32[8,8,256]{2,1,0:T(8,128)S(1)}) custom-call(s32[8]{0:T(128)S(1)} %copy-done.6, f32[3,8,8,256]{3,2,1,0:T(8,128)S(1)} %shard_map.64.met, f32[3,8,8,256]{3,2,1,0:T(8,128)S(1)} %collective-permute-done.2.other), custom_call_target="tpu_custom_call" | custom-call | bytes 1048576 | tf_op jit(solution)/shard_map/pallas_call | solution.py:102
  14.1 2.4 %collective-permute-start.4 = (f32[2,6,8,256]{3,2,1,0:T(8,128)S(1)}, f32[2,6,8,256]{3,2,1,0:T(8,128)S(1)}, u32[]{:S(2)}, u32[]{:S(2)}) collective-permute-start(f32[2,6,8,256]{3,2,1,0:T(8,128)S(1)} %get-tuple-element.17), channel_id=1, source_target_pairs={{0,4},{4,8},{8,12},{12,16},{16,20},{20,24},{24,28},{1,5},{5,9},{9,... | collective-permute-start | bytes 294920 | tf_op jit(solution)/shard_map/ppermute | solution.py:24
  16.5 4.3 %collective-permute-start.6 = (f32[2,6,8,256]{3,2,1,0:T(8,128)S(1)}, f32[2,6,8,256]{3,2,1,0:T(8,128)S(1)}, u32[]{:S(2)}, u32[]{:S(2)}) collective-permute-start(f32[2,6,8,256]{3,2,1,0:T(8,128)S(1)} %get-tuple-element.18), channel_id=1, source_target_pairs={{4,0},{8,4},{12,8},{16,12},{20,16},{24,20},{28,24},{5,1},{9,5},{13... | collective-permute-start | bytes 294920 | tf_op jit(solution)/shard_map/ppermute | solution.py:24
  20.9 0.1 collective-permute-start.8
  21.0 0.5 collective-permute-start.3
  21.4 3.5 %collective-permute-start.15 = (f32[3,2,6,8,256]{4,3,2,1,0:T(8,128)S(1)}, f32[3,2,6,8,256]{4,3,2,1,0:T(8,128)S(1)}, u32[]{:S(2)}, u32[]{:S(2)}) collective-permute-start(f32[3,2,6,8,256]{4,3,2,1,0:T(8,128)S(1)} %collective-permute-done.14.rest_0_), channel_id=1, source_target_pairs={{0,8},{8,16},{16,24},{12,4},{20,12},{28,20},{1,9},{9,17},{17,25},{... | collective-permute-start | bytes 884744 | tf_op jit(solution)/shard_map/ppermute | solution.py:30
  24.9 0.1 collective-permute-start.5
  25.0 3.5 %collective-permute-start.13 = (f32[3,2,6,8,256]{4,3,2,1,0:T(8,128)S(1)}, f32[3,2,6,8,256]{4,3,2,1,0:T(8,128)S(1)}, u32[]{:S(2)}, u32[]{:S(2)}) collective-permute-start(f32[3,2,6,8,256]{4,3,2,1,0:T(8,128)S(1)} %collective-permute-done.11.rest_0_), channel_id=1, source_target_pairs={{0,8},{8,16},{16,24},{12,4},{20,12},{28,20},{1,9},{9,17},{17,25},{... | collective-permute-start | bytes 884744 | tf_op jit(solution)/shard_map/ppermute | solution.py:30
  28.5 0.3 collective-permute-start.7
  28.8 3.9 %collective-permute-start.9 = (f32[2,2,6,8,256]{4,3,2,1,0:T(8,128)S(1)}, f32[2,2,6,8,256]{4,3,2,1,0:T(8,128)S(1)}, u32[]{:S(2)}, u32[]{:S(2)}) collective-permute-start(f32[2,2,6,8,256]{4,3,2,1,0:T(8,128)S(1)} %get-tuple-element.22), channel_id=1, source_target_pairs={{0,4},{4,8},{8,12},{12,16},{16,20},{20,24},{24,28},{1,5},{5,9},{9,... | collective-permute-start | bytes 589832 | tf_op jit(solution)/shard_map/ppermute | solution.py:24
  32.7 2.8 %collective-permute-start.10 = (f32[2,2,6,8,256]{4,3,2,1,0:T(8,128)S(1)}, f32[2,2,6,8,256]{4,3,2,1,0:T(8,128)S(1)}, u32[]{:S(2)}, u32[]{:S(2)}) collective-permute-start(f32[2,2,6,8,256]{4,3,2,1,0:T(8,128)S(1)} %get-tuple-element.23), channel_id=1, source_target_pairs={{4,0},{8,4},{12,8},{16,12},{20,16},{24,20},{28,24},{5,1},{9,5},{13... | collective-permute-start | bytes 589832 | tf_op jit(solution)/shard_map/ppermute | solution.py:24
  35.6 0.0 copy-start.5
  35.6 0.6 %copy-done.5 = s32[8]{0:T(128)S(1)} copy-done((s32[8]{0:T(128)S(1)}, s32[8]{0:T(128)}, u32[]{:S(2)}) %copy-start.5) | copy-done | bytes 56
  36.2 0.9 %shard_map.66 = (f32[3,24,5,8,256]{4,3,2,1,0:T(8,128)S(1)}, f32[16,3,8,256]{3,2,1,0:T(8,128)S(1)}) custom-call(s32[8]{0:T(128)S(1)} %copy-done.5, f32[2,8,8,256]{3,2,1,0:T(8,128)S(1)} %get-tuple-element.16.own, f32[2,8,8,256]{3,2,1,0:T(8,128)S(1)} %collective-permute-done.3.own_other, f32[2,6,8,256]{3,2,1,0:T(8,128)S(1)} %collective-permute-done.4.up, ...), custom_call_target="tpu_custom_call" | custom-call | bytes 4194304 | tf_op jit(solution)/shard_map/pallas_call | solution.py:173
  37.2 3.6 %collective-permute-done.12.rest_1_ = f32[6,2,2,8,256]{4,3,2,1,0:T(8,128)S(1)} collective-permute-done((f32[6,2,2,8,256]{4,3,2,1,0:T(8,128)S(1)}, f32[6,2,2,8,256]{4,3,2,1,0:T(8,128)S(1)}, u32[]{:S(2)}, u32[]{:S(2)}) %collective-permute-start.12) | collective-permute-done | bytes 196640 | tf_op jit(solution)/shard_map/ppermute | solution.py:19
  40.8 3.0 %shard_map.68.rest_3_ = f32[8,16,8,256]{3,2,1,0:T(8,128)S(1)} custom-call(s32[8]{0:T(128)S(1)} %copy-done.5, f32[3,24,5,8,256]{4,3,2,1,0:T(8,128)S(1)} %get-tuple-element.20.coef, f32[16,3,8,256]{3,2,1,0:T(8,128)S(1)} %get-tuple-element.21.solve, f32[8,16,8,256]{3,2,1,0:T(8,128)S(1)} %copy-done.1, f32[8,8,256]{2,1,0:T(8,128)S(1)} %copy-done.2, ...), custom_call_target="tpu_custom_call" | custom-call | bytes 14680064 | tf_op jit(solution)/shard_map/pallas_call | solution.py:292
  43.7 3.0 %shard_map.69.rest_2_ = f32[8,16,8,256]{3,2,1,0:T(8,128)S(1)} custom-call(s32[8]{0:T(128)S(1)} %copy-done.5, f32[3,24,5,8,256]{4,3,2,1,0:T(8,128)S(1)} %get-tuple-element.20.coef, f32[16,3,8,256]{3,2,1,0:T(8,128)S(1)} %get-tuple-element.21.solve, f32[8,16,8,256]{3,2,1,0:T(8,128)S(1)} %copy-done.1, ...), custom_call_target="tpu_custom_call", output_to_operand_aliasing={{}: (8, {})} | custom-call | bytes 14680064 | tf_op jit(solution)/shard_map/pallas_call | solution.py:292
  46.7 3.0 %shard_map.70 = f32[8,16,8,256]{3,2,1,0:T(8,128)} custom-call(s32[8]{0:T(128)S(1)} %copy-done.5, f32[3,24,5,8,256]{4,3,2,1,0:T(8,128)S(1)} %get-tuple-element.20.coef, f32[16,3,8,256]{3,2,1,0:T(8,128)S(1)} %get-tuple-element.21.solve, f32[8,16,8,256]{3,2,1,0:T(8,128)S(1)} %copy-done.1, f32[8,8,256]{2,1,0:T(8,128)S(1)} %copy-done.2, ...), custom_call_target="tpu_custom_call" | custom-call | bytes 10485760 | tf_op jit(solution)/shard_map/pallas_call | solution.py:292
  (21 shorter events, 0.0 us)
Async XLA Ops:
  0.0 3.8 %collective-permute-start = (f32[1,2,16,8,256]{4,3,2,1,0:T(8,128)}, f32[1,2,16,8,256]{4,3,2,1,0:T(8,128)S(1)}, u32[]{:S(2)}, u32[]{:S(2)}) collective-permute-start(f32[1,2,16,8,256]{4,3,2,1,0:T(8,128)} %wind.1), channel_id=1, source_target_pairs={{0,1},{1,0},{2,3},{3,2},{4,5},{5,4},{6,7},{7,6},{8,9},{9,8},{10,11... | collective-permute-start | bytes 786440 | tf_op jit(solution)/shard_map/ppermute | solution.py:19
  0.0 3.8 %collective-permute-start.1 = (f32[1,15,8,256]{3,2,1,0:T(8,128)}, f32[1,15,8,256]{3,2,1,0:T(8,128)S(1)}, u32[]{:S(2)}, u32[]{:S(2)}) collective-permute-start(f32[1,15,8,256]{3,2,1,0:T(8,128)} %diffusion.1), channel_id=1, source_target_pairs={{0,1},{1,0},{2,3},{3,2},{4,5},{5,4},{6,7},{7,6},{8,9},{9,8},{10,11... | collective-permute-start | bytes 368648 | tf_op jit(solution)/shard_map/ppermute | solution.py:19
  0.5 1.2 %copy-start = (f32[8,16,8,256]{3,2,1,0:T(8,128)S(1)}, f32[8,16,8,256]{3,2,1,0:T(8,128)}, u32[]{:S(2)}) copy-start(f32[8,16,8,256]{3,2,1,0:T(8,128)} %own.5) | copy-start | bytes 3145732
  1.7 39.0 %copy-start.1 = (f32[8,16,8,256]{3,2,1,0:T(8,128)S(1)}, f32[8,16,8,256]{3,2,1,0:T(8,128)}, u32[]{:S(2)}) copy-start(f32[8,16,8,256]{3,2,1,0:T(8,128)} %own.5) | copy-start | bytes 3145732
  1.7 39.0 %copy-start.2 = (f32[8,8,256]{2,1,0:T(8,128)S(1)}, f32[8,8,256]{2,1,0:T(8,128)}, u32[]{:S(2)}) copy-start(f32[8,8,256]{2,1,0:T(8,128)} %source.5) | copy-start | bytes 196612
  2.2 18.8 %collective-permute-start.11 = (f32[3,2,6,8,256]{4,3,2,1,0:T(8,128)S(1)}, f32[3,2,6,8,256]{4,3,2,1,0:T(8,128)S(1)}, u32[]{:S(2)}, u32[]{:S(2)}) collective-permute-start(f32[3,2,6,8,256]{4,3,2,1,0:T(8,128)S(1)} %get-tuple-element.24), channel_id=1, source_target_pairs={{0,4},{4,0},{8,12},{12,8},{16,20},{20,16},{24,28},{28,24},{1,5},{5... | collective-permute-start | bytes 884744 | tf_op jit(solution)/shard_map/ppermute | solution.py:19
  3.8 1.0 %copy-start.3 = (f32[1,2,16,8,256]{4,3,2,1,0:T(8,128)S(1)}, f32[1,2,16,8,256]{4,3,2,1,0:T(8,128)}, u32[]{:S(2)}) copy-start(f32[1,2,16,8,256]{4,3,2,1,0:T(8,128)} %wind.1) | copy-start | bytes 786436
  4.7 0.9 %copy-start.4 = (f32[1,15,8,256]{3,2,1,0:T(8,128)S(1)}, f32[1,15,8,256]{3,2,1,0:T(8,128)}, u32[]{:S(2)}) copy-start(f32[1,15,8,256]{3,2,1,0:T(8,128)} %diffusion.1) | copy-start | bytes 368644
  5.6 0.7 %copy-start.6 = (s32[8]{0:T(128)S(1)}, s32[8]{0:T(128)}, u32[]{:S(2)}) copy-start(s32[8]{0:T(128)} %loader.3) | copy-start | bytes 100
  6.9 6.6 %collective-permute-start.2 = (f32[3,8,8,256]{3,2,1,0:T(8,128)S(1)}, f32[3,8,8,256]{3,2,1,0:T(8,128)S(1)}, u32[]{:S(2)}, u32[]{:S(2)}) collective-permute-start(f32[3,8,8,256]{3,2,1,0:T(8,128)S(1)} %shard_map.64.met), channel_id=1, source_target_pairs={{0,2},{1,3},{2,0},{3,1},{4,6},{5,7},{6,4},{7,5},{8,10},{9,11},{10,... | collective-permute-start | bytes 589832 | tf_op jit(solution)/shard_map/ppermute | solution.py:19
  8.4 13.0 %collective-permute-start.14 = (f32[3,2,6,8,256]{4,3,2,1,0:T(8,128)S(1)}, f32[3,2,6,8,256]{4,3,2,1,0:T(8,128)S(1)}, u32[]{:S(2)}, u32[]{:S(2)}) collective-permute-start(f32[3,2,6,8,256]{4,3,2,1,0:T(8,128)S(1)} %get-tuple-element.26), channel_id=1, source_target_pairs={{0,4},{4,0},{8,12},{12,8},{16,20},{20,16},{24,28},{28,24},{1,5},{5... | collective-permute-start | bytes 884744 | tf_op jit(solution)/shard_map/ppermute | solution.py:19
  14.1 10.8 %collective-permute-start.4 = (f32[2,6,8,256]{3,2,1,0:T(8,128)S(1)}, f32[2,6,8,256]{3,2,1,0:T(8,128)S(1)}, u32[]{:S(2)}, u32[]{:S(2)}) collective-permute-start(f32[2,6,8,256]{3,2,1,0:T(8,128)S(1)} %get-tuple-element.17), channel_id=1, source_target_pairs={{0,4},{4,8},{8,12},{12,16},{16,20},{20,24},{24,28},{1,5},{5,9},{9,... | collective-permute-start | bytes 294920 | tf_op jit(solution)/shard_map/ppermute | solution.py:24
  16.5 12.0 %collective-permute-start.6 = (f32[2,6,8,256]{3,2,1,0:T(8,128)S(1)}, f32[2,6,8,256]{3,2,1,0:T(8,128)S(1)}, u32[]{:S(2)}, u32[]{:S(2)}) collective-permute-start(f32[2,6,8,256]{3,2,1,0:T(8,128)S(1)} %get-tuple-element.18), channel_id=1, source_target_pairs={{4,0},{8,4},{12,8},{16,12},{20,16},{24,20},{28,24},{5,1},{9,5},{13... | collective-permute-start | bytes 294920 | tf_op jit(solution)/shard_map/ppermute | solution.py:24
  20.9 4.2 %collective-permute-start.8 = (f32[8,8,256]{2,1,0:T(8,128)S(1)}, f32[8,8,256]{2,1,0:T(8,128)S(1)}, u32[]{:S(2)}, u32[]{:S(2)}) collective-permute-start(f32[8,8,256]{2,1,0:T(8,128)S(1)} %get-tuple-element.19.mix), channel_id=1, source_target_pairs={{0,1},{1,0},{2,3},{3,2},{4,5},{5,4},{6,7},{7,6},{8,9},{9,8},{10,11... | collective-permute-start | bytes 196616 | tf_op jit(solution)/shard_map/ppermute | solution.py:19
  21.0 7.8 %collective-permute-start.3 = (f32[2,8,8,256]{3,2,1,0:T(8,128)S(1)}, f32[2,8,8,256]{3,2,1,0:T(8,128)S(1)}, u32[]{:S(2)}, u32[]{:S(2)}) collective-permute-start(f32[2,8,8,256]{3,2,1,0:T(8,128)S(1)} %get-tuple-element.16.own), channel_id=1, source_target_pairs={{0,1},{1,0},{2,3},{3,2},{4,5},{5,4},{6,7},{7,6},{8,9},{9,8},{10,11... | collective-permute-start | bytes 393224 | tf_op jit(solution)/shard_map/ppermute | solution.py:19
  21.4 19.3 %collective-permute-start.15 = (f32[3,2,6,8,256]{4,3,2,1,0:T(8,128)S(1)}, f32[3,2,6,8,256]{4,3,2,1,0:T(8,128)S(1)}, u32[]{:S(2)}, u32[]{:S(2)}) collective-permute-start(f32[3,2,6,8,256]{4,3,2,1,0:T(8,128)S(1)} %collective-permute-done.14.rest_0_), channel_id=1, source_target_pairs={{0,8},{8,16},{16,24},{12,4},{20,12},{28,20},{1,9},{9,17},{17,25},{... | collective-permute-start | bytes 884744 | tf_op jit(solution)/shard_map/ppermute | solution.py:30
  24.9 3.9 %collective-permute-start.5 = (f32[2,6,8,256]{3,2,1,0:T(8,128)S(1)}, f32[2,6,8,256]{3,2,1,0:T(8,128)S(1)}, u32[]{:S(2)}, u32[]{:S(2)}) collective-permute-start(f32[2,6,8,256]{3,2,1,0:T(8,128)S(1)} %collective-permute-done.4.up), channel_id=1, source_target_pairs={{0,1},{1,0},{2,3},{3,2},{4,5},{5,4},{6,7},{7,6},{8,9},{9,8},{10,11... | collective-permute-start | bytes 294920 | tf_op jit(solution)/shard_map/ppermute | solution.py:19
  25.0 18.7 %collective-permute-start.13 = (f32[3,2,6,8,256]{4,3,2,1,0:T(8,128)S(1)}, f32[3,2,6,8,256]{4,3,2,1,0:T(8,128)S(1)}, u32[]{:S(2)}, u32[]{:S(2)}) collective-permute-start(f32[3,2,6,8,256]{4,3,2,1,0:T(8,128)S(1)} %collective-permute-done.11.rest_0_), channel_id=1, source_target_pairs={{0,8},{8,16},{16,24},{12,4},{20,12},{28,20},{1,9},{9,17},{17,25},{... | collective-permute-start | bytes 884744 | tf_op jit(solution)/shard_map/ppermute | solution.py:30
  28.5 4.2 %collective-permute-start.7 = (f32[2,6,8,256]{3,2,1,0:T(8,128)S(1)}, f32[2,6,8,256]{3,2,1,0:T(8,128)S(1)}, u32[]{:S(2)}, u32[]{:S(2)}) collective-permute-start(f32[2,6,8,256]{3,2,1,0:T(8,128)S(1)} %collective-permute-done.6.down), channel_id=1, source_target_pairs={{0,1},{1,0},{2,3},{3,2},{4,5},{5,4},{6,7},{7,6},{8,9},{9,8},{10,11... | collective-permute-start | bytes 294920 | tf_op jit(solution)/shard_map/ppermute | solution.py:19
  28.8 11.9 %collective-permute-start.12 = (f32[6,2,2,8,256]{4,3,2,1,0:T(8,128)S(1)}, f32[6,2,2,8,256]{4,3,2,1,0:T(8,128)S(1)}, u32[]{:S(2)}, u32[]{:S(2)}) collective-permute-start(f32[6,2,2,8,256]{4,3,2,1,0:T(8,128)S(1)} %get-tuple-element.25), channel_id=1, source_target_pairs={{0,4},{4,0},{8,12},{12,8},{16,20},{20,16},{24,28},{28,24},{1,5},{5... | collective-permute-start | bytes 589832 | tf_op jit(solution)/shard_map/ppermute | solution.py:19
  28.8 17.9 %collective-permute-start.9 = (f32[2,2,6,8,256]{4,3,2,1,0:T(8,128)S(1)}, f32[2,2,6,8,256]{4,3,2,1,0:T(8,128)S(1)}, u32[]{:S(2)}, u32[]{:S(2)}) collective-permute-start(f32[2,2,6,8,256]{4,3,2,1,0:T(8,128)S(1)} %get-tuple-element.22), channel_id=1, source_target_pairs={{0,4},{4,8},{8,12},{12,16},{16,20},{20,24},{24,28},{1,5},{5,9},{9,... | collective-permute-start | bytes 589832 | tf_op jit(solution)/shard_map/ppermute | solution.py:24
  32.7 14.0 %collective-permute-start.10 = (f32[2,2,6,8,256]{4,3,2,1,0:T(8,128)S(1)}, f32[2,2,6,8,256]{4,3,2,1,0:T(8,128)S(1)}, u32[]{:S(2)}, u32[]{:S(2)}) collective-permute-start(f32[2,2,6,8,256]{4,3,2,1,0:T(8,128)S(1)} %get-tuple-element.23), channel_id=1, source_target_pairs={{4,0},{8,4},{12,8},{16,12},{20,16},{24,20},{28,24},{5,1},{9,5},{13... | collective-permute-start | bytes 589832 | tf_op jit(solution)/shard_map/ppermute | solution.py:24
  35.6 0.7 %copy-start.5 = (s32[8]{0:T(128)S(1)}, s32[8]{0:T(128)}, u32[]{:S(2)}) copy-start(s32[8]{0:T(128)} %substeps.7) | copy-start | bytes 100

commit v3 on v2

v3 whole, which is shorter than its diff:
```python
import functools

import jax
import jax.numpy as jnp
from jax import lax
from jax.experimental import pallas as pl
from jax.experimental.pallas import tpu as pltpu
from jax.sharding import PartitionSpec as P

ROUNDS = 6
DEEP = 8
RELAYED = (4,)
WITH_WINDS = 1
STRAIGHT = 3
MIB = 1024 * 1024
VMEM_LIMIT = 32 * MIB
WINDOW_COST = 1
PREPARE_COST = 1


def exchange(value, axis, bit):
    count = lax.axis_size(axis)
    return lax.ppermute(value, axis, [(i, i ^ bit) for i in range(count)])


def shift(value, axis, by):
    count = lax.axis_size(axis)
    return lax.ppermute(value, axis, [(i, i + by) for i in range(count) if 0 <= i + by < count])


def relay(value, axis):
    count = lax.axis_size(axis)
    pairs = [(i, i + 2) for i in range(0, count - 2, 2)] + [(i, i - 2) for i in range(3, count, 2)]
    return lax.ppermute(value, axis, pairs)


def in_smem(value):
    return pltpu.with_memory_space_constraint(value, pltpu.SMEM)


def in_vmem(values):
    return [pltpu.with_memory_space_constraint(value, pltpu.VMEM) for value in values]


def first_choice_kernel(numbers, wind, wind_other, diffusion, diffusion_other, *rest):
    out = rest[-1]
    slot, group = numbers[0], lax.axis_index("group")
    mine = slot % 2 == group % 2
    half = out.shape[1]
    base = group % 2 * half
    for k in range(half):
        for kind in range(2):
            out[kind, k] = jnp.where(mine, wind[0, kind, base + k], wind_other[0, kind, base + k])
        at = jnp.minimum(base + k, diffusion.shape[1] - 1)
        out[2, k] = jnp.where(mine, diffusion[0, at], diffusion_other[0, at])


def next_choice_kernel(bit, numbers, met, other, out):
    slot, group = numbers[0], lax.axis_index("group")
    out[...] = jnp.where((slot & bit) == (group & bit), met[...], other[...])


def last_choice_kernel(bit, numbers, met, other, tracers_up, tracers_down, *rest):
    wind, up, down, mix = rest[-4:]
    group = lax.axis_index("group")
    mine = (numbers[0] & bit) == (group & bit)
    _, height, deep, width = wind.shape
    count, groups, reach = tracers_up.shape[:3]
    for kind in range(2):
        for j in range(height):
            value = jnp.where(mine, met[kind, :, j, :], other[kind, :, j, :])
            wind[kind, j] = value
            if j < reach:
                down[kind * reach + j] = value
            if j >= height - reach:
                up[kind * reach + j - (height - reach)] = value
    mix[...] = jnp.where(mine, met[2], other[2])
    for n in range(count):
        for g in range(groups):
            at = (2 + n * groups + g) * reach
            up[at : at + reach] = tracers_up[n, g]
            down[at : at + reach] = tracers_down[n, g]


def onward_kernel(_, pair, *rest):
    out = rest[-1]
    tracers, groups, reach = out.shape[:3]
    skip = jnp.where(lax.axis_index("tile") % 2 == 0, pair.shape[2] - reach, 0)
    for n in range(tracers):
        for g in range(groups):
            out[n, g] = pair[n, g, pl.ds(skip, reach)]


def pack_kernel(relayed, tiles, substeps_in, loader_in, tracers_in, wind_in, diffusion_in, *rest):
    numbers, tracers, wind, diffusion, *outs, substeps, loader, sem = rest
    copies = [
        pltpu.make_async_copy(source, target, sem.at[i])
        for i, (source, target) in enumerate(
            (
                (substeps_in, substeps),
                (loader_in, loader),
                (tracers_in, tracers),
                (wind_in, wind),
                (diffusion_in, diffusion),
            )
        )
    ]
    for copy in copies:
        copy.start()
    tile = lax.axis_index("tile")
    _, levels, height, _ = tracers.shape
    straight = [outs[-4:-2], outs[-2:]]
    reach = outs[-1].shape[2]
    copies[2].wait()
    for g in range(levels // DEEP):
        deep = slice(g * DEEP, (g + 1) * DEEP)
        start = 0
        for part, count in zip(outs, relayed):
            for n in range(count):
                for j in range(height):
                    part[n, g, j] = tracers[start + n, deep, j, :]
            start += count
        for up, down in straight:
            for n in range(up.shape[0]):
                for j in range(reach):
                    up[n, g, j] = tracers[start + n, deep, height - reach + j, :]
                    down[n, g, j] = tracers[start + n, deep, j, :]
            start += up.shape[0]
    copies[0].wait()
    copies[1].wait()
    numbers[0] = loader[tile]
    numbers[1] = substeps[jnp.maximum(tile - 1, 0)]
    numbers[2] = substeps[tile]
    numbers[3] = substeps[jnp.minimum(tile + 1, tiles - 1)]
    copies[3].wait()
    copies[4].wait()


def pack(tiles, substeps, loader, tracers, winds, diffusivity):
    _, levels, height, width = tracers.shape

    def rows_of(count, rows):
        return pltpu.VMEM((count, levels // DEEP, rows, DEEP, width), jnp.float32)

    out_shape = [pltpu.SMEM((4,), jnp.int32)]
    out_shape += [pltpu.VMEM(x.shape, x.dtype) for x in (tracers, winds, diffusivity)]
    out_shape += [rows_of(count, height) for count in RELAYED]
    out_shape += [rows_of(WITH_WINDS, ROUNDS)] * 2 + [rows_of(STRAIGHT, ROUNDS)] * 2
    vmem = pl.BlockSpec(memory_space=pltpu.VMEM)
    smem = pl.BlockSpec(memory_space=pltpu.SMEM)
    hbm = pl.BlockSpec(memory_space=pltpu.HBM)
    return pl.pallas_call(
        functools.partial(pack_kernel, RELAYED, tiles),
        out_shape=out_shape,
        in_specs=[hbm] * 5,
        out_specs=[smem] + [vmem] * (len(out_shape) - 1),
        scratch_shapes=[
            pltpu.SMEM(substeps.shape, jnp.int32),
            pltpu.SMEM(loader.shape, jnp.int32),
            pltpu.SemaphoreType.DMA((5,)),
        ],
        compiler_params=pltpu.CompilerParams(vmem_limit_bytes=VMEM_LIMIT),
        cost_estimate=pl.CostEstimate(flops=0, bytes_accessed=MIB, transcendentals=0),
    )(
        *[
            pltpu.with_memory_space_constraint(x, pltpu.HBM)
            for x in (substeps, loader, tracers, winds, diffusivity)
        ]
    )


def on_core(kernel, numbers, operands, out_shape, waits=(), cost=1):
    vmem = pl.BlockSpec(memory_space=pltpu.VMEM)
    return pl.pallas_call(
        kernel,
        out_shape=out_shape,
        in_specs=[pl.BlockSpec(memory_space=pltpu.SMEM)]
        + [vmem] * len(operands)
        + [pl.BlockSpec(memory_space=pl.ANY)] * len(waits),
        out_specs=jax.tree.map(lambda _: vmem, out_shape),
        compiler_params=pltpu.CompilerParams(vmem_limit_bytes=VMEM_LIMIT),
        cost_estimate=pl.CostEstimate(
            flops=0, bytes_accessed=cost * MIB, transcendentals=0
        ),
    )(in_smem(numbers), *in_vmem(operands), *waits)


def gather_kernel(_, wind, up, down, mix, *rest):
    height = wind.shape[1]
    half = height // 2
    rows = rest[-1].shape[0] - half
    reach = (rows - height) // 2
    for kind, out in enumerate(rest[-2:]):
        out[:reach] = up[pl.ds(kind * reach, reach)]
        out[pl.ds(reach, height)] = wind[kind]
        out[pl.ds(reach + height, reach)] = down[pl.ds(kind * reach, reach)]
        out[rows:] = mix[pl.ds(kind * half, half)]


def prepare_kernel(height, reach, numbers, *rest):
    *blocks, coef, solve, faces, mixing = rest
    width = coef.shape[-1]
    groups = 2
    levels = groups * DEEP
    rows = height + 2 * reach
    half = height // 2
    tile, core = lax.axis_index("tile"), lax.axis_index("group") % 2
    for g, pair in ((core, blocks[:2]), (1 - core, blocks[2:4])):
        for kind, block in enumerate(pair):
            for j in range(rows):
                value = block[j]
                if kind == 1 and j == reach:
                    value = jnp.where(tile == 0, 0.0, value)
                faces[kind, g, height - reach + j] = value
            for k in range(half):
                mixing[g * DEEP + kind * half + k] = block[rows + k]
    counts = [numbers[t] for t in range(1, 4)]
    ones = jnp.ones((DEEP, width), jnp.float32)
    fractions = [ones / (ones * count.astype(jnp.float32)) for count in counts]
    reach -= 1
    for g in range(groups):
        for j in range(height - reach, 2 * height + reach):
            f = fractions[j // height]
            zonal, south, north = faces[0, g, j], faces[1, g, j], faces[1, g, j + 1]
            zonal_east = pltpu.roll(zonal, width - 1, 1)
            coef[g, j, 0] = 1.0 - f * (
                (jnp.maximum(zonal_east, 0.0) - jnp.minimum(zonal, 0.0))
                + (jnp.maximum(north, 0.0) - jnp.minimum(south, 0.0))
            )
            coef[g, j, 1] = f * jnp.maximum(zonal, 0.0)
            coef[g, j, 2] = -f * jnp.minimum(zonal_east, 0.0)
            coef[g, j, 3] = f * jnp.maximum(south, 0.0)
            coef[g, j, 4] = -f * jnp.minimum(north, 0.0)
    for j in range(height - reach, 2 * height + reach):
        coef[groups, j, 0] = ones
        for k in range(1, 5):
            coef[groups, j, k] = jnp.zeros_like(ones)
    ratio = lower = jnp.zeros((height, width), jnp.float32)
    for k in range(levels):
        upper = mixing[k] if k < levels - 1 else jnp.zeros_like(lower)
        pivot = 1.0 / (1.0 + lower + upper - lower * ratio)
        ratio = upper * pivot
        solve[k, 0] = lower
        solve[k, 1] = pivot
        solve[k, 2] = ratio
        lower = upper


def prepare(numbers, height, reach, blocks, waits):
    width = blocks[0].shape[-1]
    vmem = pl.BlockSpec(memory_space=pltpu.VMEM)
    return pl.pallas_call(
        functools.partial(prepare_kernel, height, reach),
        out_shape=(
            pltpu.VMEM((3, 3 * height, 5, DEEP, width), jnp.float32),
            pltpu.VMEM((2 * DEEP, 3, height, width), jnp.float32),
        ),
        in_specs=[pl.BlockSpec(memory_space=pltpu.SMEM)]
        + [vmem] * len(blocks)
        + [pl.BlockSpec(memory_space=pl.ANY)] * len(waits),
        out_specs=(vmem, vmem),
        scratch_shapes=[
            pltpu.VMEM((2, 2, 3 * height, DEEP, width), jnp.float32),
            pltpu.VMEM((2 * DEEP, height, width), jnp.float32),
        ],
        compiler_params=pltpu.CompilerParams(vmem_limit_bytes=VMEM_LIMIT),
        cost_estimate=pl.CostEstimate(
            flops=0, bytes_accessed=PREPARE_COST * MIB, transcendentals=0
        ),
    )(in_smem(numbers), *in_vmem(blocks), *waits)


def window_kernel(way, start, count, last, numbers, coef, solve, own, source, *rest):
    first, second, *rest = rest
    if last:
        prior, out, field, advected, values, solved, sem = rest
        early = pltpu.make_async_copy(prior.at[:start], out.at[:start], sem.at[0])
        early.start()
    else:
        out, field, advected, values = rest[-4:]
    tracers = count
    reach = ROUNDS
    _, levels, height, width = own.shape
    groups = levels // DEEP
    tile = lax.axis_index("tile")
    even = tile % 2 == 0
    pair_at = jnp.where(even, 2 * height, 0)
    far_at = jnp.where(even, height - reach, 2 * height)
    counts = [numbers[t] for t in range(1, 4)]
    for n in range(tracers):
        for g in range(groups):
            deep = slice(g * DEEP, (g + 1) * DEEP)
            for j in range(height):
                field[0, n, g, height + j] = own[start + n, deep, j, :]
            for j in range(reach):
                if way == "relay":
                    field[0, n, g, far_at + j] = second[n, g, j]
                else:
                    if way == "winds":
                        at = (2 + n * groups + g) * reach + j
                        south, north = first[at], second[at]
                    else:
                        south, north = first[n, g, j], second[n, g, j]
                    field[0, n, g, height - reach + j] = south
                    field[0, n, g, 2 * height + j] = north
            if way == "relay":
                for j in range(height):
                    field[0, n, g, pair_at + j] = first[n, g, j]
    for step in range(ROUNDS):
        reach = ROUNDS - 1 - step
        low, high = height - reach, 2 * height + reach
        src, dst = step % 2, (step + 1) % 2
        for g in range(groups):
            pages = [jnp.where(step < count, g, groups) for count in counts]
            south = [field[src, n, g, low - 1] for n in range(tracers)]
            here = [field[src, n, g, low] for n in range(tracers)]
            for j in range(low, high):
                c = [coef[pages[j // height], j, k] for k in range(5)]
                for n in range(tracers):
                    north = field[src, n, g, j + 1]
                    new = (
                        c[0] * here[n]
                        + c[1] * pltpu.roll(here[n], 1, 1)
                        + c[2] * pltpu.roll(here[n], width - 1, 1)
                        + c[3] * south[n]
                        + c[4] * north
                    )
                    if step < ROUNDS - 1:
                        field[dst, n, g, j] = new
                    else:
                        advected[n, g * DEEP : (g + 1) * DEEP, j - height, :] = new
                    south[n], here[n] = here[n], north
    for k in range(levels):
        lower, pivot = solve[k, 0], solve[k, 1]
        for n in range(tracers):
            q = advected[n, k]
            q = q + (source[start + n] if k == 0 else lower * values[n, k - 1])
            values[n, k] = q * pivot
    for n in range(tracers):
        target = solved.at[n] if last else out.at[start + n]
        current = values[n, levels - 1]
        target[levels - 1] = current
        for k in range(levels - 2, -1, -1):
            current = values[n, k] + solve[k, 2] * current
            target[k] = current
    if last:
        late = pltpu.make_async_copy(solved, out.at[start:], sem.at[1])
        late.start()
        early.wait()
        late.wait()


def window(numbers, coef, solve, tracers, emissions, way, start, count, halos, prior):
    total, levels, height, width = tracers.shape
    groups = levels // DEEP
    last = start + count == total
    vmem = pl.BlockSpec(memory_space=pltpu.VMEM)
    operands = [coef, solve, tracers, emissions, *halos]
    scratch = [
        pltpu.VMEM((2, count, groups, 3 * height, DEEP, width), jnp.float32),
        pltpu.VMEM((count, levels, height, width), jnp.float32),
        pltpu.VMEM((count, levels, height, width), jnp.float32),
    ]
    aliases = {}
    if prior is not None:
        operands.append(prior)
        if not last:
            aliases = {len(operands): 0}
    if last:
        scratch += [
            pltpu.VMEM((count, levels, height, width), jnp.float32),
            pltpu.SemaphoreType.DMA((2,)),
        ]
    shape = tracers.shape
    return pl.pallas_call(
        functools.partial(window_kernel, way, start, count, last),
        out_shape=jax.ShapeDtypeStruct(shape, jnp.float32)
        if last
        else pltpu.VMEM(shape, jnp.float32),
        in_specs=[pl.BlockSpec(memory_space=pltpu.SMEM)] + [vmem] * len(operands),
        out_specs=pl.BlockSpec(memory_space=pl.ANY) if last else vmem,
        scratch_shapes=scratch,
        input_output_aliases=aliases,
        compiler_params=pltpu.CompilerParams(vmem_limit_bytes=VMEM_LIMIT),
        cost_estimate=pl.CostEstimate(
            flops=0, bytes_accessed=WINDOW_COST * MIB, transcendentals=0
        ),
    )(in_smem(numbers), *in_vmem(operands))


def shards(tracers, emissions, winds, diffusivity, substeps, loader):
    tiles, groups = lax.axis_size("tile"), lax.axis_size("group")
    _, levels, height, width = tracers.shape
    half = levels // 2
    wind_other, diffusion_other = exchange(winds, "group", 1), exchange(diffusivity, "group", 1)
    numbers, tracers, winds, diffusivity, *parts, up_first, down_first, up, down = pack(
        tiles, substeps, loader, tracers, winds, diffusivity
    )

    pairs = [exchange(part, "tile", 1) for part in parts]
    halos = []
    for pair in pairs:
        shape = (pair.shape[0], pair.shape[1], ROUNDS, *pair.shape[3:])
        onward = on_core(onward_kernel, numbers, [pair], pltpu.VMEM(shape, jnp.float32))
        halos.append(("relay", pair.shape[0], (pair, relay(onward, "tile"))))

    met = on_core(
        first_choice_kernel,
        numbers,
        [winds, wind_other, diffusivity, diffusion_other],
        pltpu.VMEM((3, half, height, width), jnp.float32),
    )
    bit = 2
    while 2 * bit < groups:
        met = on_core(
            functools.partial(next_choice_kernel, bit),
            numbers,
            [met, exchange(met, "group", bit)],
            pltpu.VMEM(met.shape, jnp.float32),
        )
        bit *= 2
    with_winds = 2 * ROUNDS * (1 + WITH_WINDS)
    wind, wind_up, wind_down, mix = on_core(
        functools.partial(last_choice_kernel, bit),
        numbers,
        [met, exchange(met, "group", bit), up_first, down_first],
        [
            pltpu.VMEM((2, height, half, width), jnp.float32),
            pltpu.VMEM((with_winds, half, width), jnp.float32),
            pltpu.VMEM((with_winds, half, width), jnp.float32),
            pltpu.VMEM((half, height, width), jnp.float32),
        ],
    )
    wind_up, wind_down = shift(wind_up, "tile", 1), shift(wind_down, "tile", -1)
    halos.append(("winds", WITH_WINDS, (wind_up, wind_down)))
    halos.append(("straight", STRAIGHT, (shift(up, "tile", 1), shift(down, "tile", -1))))
    known = on_core(
        gather_kernel,
        numbers,
        [wind, wind_up, wind_down, mix],
        [pltpu.VMEM((height + 2 * ROUNDS + height // 2, half, width), jnp.float32)] * 2,
    )
    coef, solve = prepare(
        numbers, height, ROUNDS, [*known, *(exchange(x, "group", 1) for x in known)], []
    )

    result, start = None, 0
    for way, count, halo in halos:
        result = window(
            numbers, coef, solve, tracers, emissions, way, start, count, halo, result
        )
        start += count
    return result


def solution(mesh):
    return jax.shard_map(
        shards,
        mesh=mesh,
        in_specs=(
            P("group", None, "tile", None),
            P("group", "tile", None),
            P("group", None, None, "tile", None),
            P("group", None, "tile", None),
            P(),
            P(),
        ),
        out_specs=P("group", None, "tile", None),
        check_vma=False,
    )
```

time: 50 us -> 42.6 us (0.85)
  local copies, waits for them, and re-layouts: 4.39 us -> 0.01 us
  starting transfers between devices: 25.5 us -> 21.2 us
  waiting for transfers between devices: 8.15 us -> 11.7 us
  Pallas kernels: 11.5 us -> 9.14 us
    unnamed x14 -> x2, local copies, waits for them, and re-layouts: 4.39 us -> 0.01 us
    ppermute x4, waiting for transfers between devices: 0.01 us -> 3.65 us  [shift(): lax.ppermute(value, axis, [(i, i + by) for i in range(count) if 0 <= i +...]
    ppermute x2 -> x1, starting transfers between devices: 6.96 us -> 3.48 us  [relay(): return lax.ppermute(value, axis, pairs)]
    pallas_call x3 -> x4, Pallas kernels: 1.65 us -> 0.2 us  [on_core(): pl.pallas_call(kernel, out_shape=out_shape, in_specs=[pl.BlockSpec(memory...]
    pallas_call x4 -> x5, Pallas kernels: 9.83 us -> 8.94 us  [the longest x3 6.91 us: window(): pl.pallas_call(functools.partial(window_kernel, way, start, count, last),...]
    ppermute x10 -> x6, starting transfers between devices: 5.06 us -> 4.22 us  [exchange(): return lax.ppermute(value, axis, [(i, i ^ bit) for i in range(count)])]
    ppermute x10 -> x6, waiting for transfers between devices: 8.13 us -> 8.08 us  [exchange(): return lax.ppermute(value, axis, [(i, i ^ bit) for i in range(count)])]
  transfers between devices with their start and end apart: 16 -> 11, of which waited for: 2 -> 6; matrix products, arithmetic and copies ran while one was open for 0% -> 0% of each run, Pallas kernels for 17% -> 10%
where the time goes in v3:
time: 42.6 us; the launch traced here: 42.2 us
  starting transfers between devices  21.2 us (50%)
  waiting for transfers between devices  11.7 us (27%)
  Pallas kernels  9.14 us (21%)
    ppermute x4, starting transfers between devices, shift(): lax.ppermute(value, axis, [(i, i + by) for i in range(count) if 0 <= i +...  13.5 us
    ppermute x6, waiting for transfers between devices, exchange(): return lax.ppermute(value, axis, [(i, i ^ bit) for i in range(count)])  8.08 us
    pallas_call x3, Pallas kernels, window(): pl.pallas_call(functools.partial(window_kernel, way, start, count, last),...  6.91 us
    ppermute x6, starting transfers between devices, exchange(): return lax.ppermute(value, axis, [(i, i ^ bit) for i in range(count)])  4.22 us
    ppermute x4, waiting for transfers between devices, shift(): lax.ppermute(value, axis, [(i, i + by) for i in range(count) if 0 <= i +...  3.65 us
    ppermute x1, starting transfers between devices, relay(): return lax.ppermute(value, axis, pairs)  3.48 us
    pallas_call x1, Pallas kernels, pack(): pl.pallas_call(functools.partial(pack_kernel, RELAYED, tiles), out_shape=...  1.65 us
  transfers between devices with their start and end apart: 11, of which 6 were waited for; matrix products, arithmetic and copies ran while one was open for 0% of the time, Pallas kernels for 10%

profile of v3, /device:TPU:8, one launch (start us, length us, event | category | flops | bytes accessed | tf_op | source)
XLA Modules:
  0.0 42.2 jit_solution(10748374887526383926)
XLA Ops:
  0.0 0.0 copy-start
  0.0 1.7 %shard_map.64 = (s32[4]{0:T(128)S(4)}, f32[8,16,8,256]{3,2,1,0:T(8,128)S(1)}, f32[1,2,16,8,256]{4,3,2,1,0:T(8,128)S(1)}, f32[1,15,8,256]{3,2,1,0:T(8,128)S(1)}, ...) custom-call(s32[8]{0:T(128)} %substeps_in.1, ...), custom_call_target="tpu_custom_call" | custom-call | bytes 1048576 | tf_op jit(solution)/shard_map/pallas_call | solution.py:152
  1.7 1.6 %collective-permute-start.9 = (f32[4,2,8,8,256]{4,3,2,1,0:T(8,128)S(1)}, f32[4,2,8,8,256]{4,3,2,1,0:T(8,128)S(1)}, u32[]{:S(2)}, u32[]{:S(2)}) collective-permute-start(f32[4,2,8,8,256]{4,3,2,1,0:T(8,128)S(1)} %get-tuple-element.38), channel_id=1, source_target_pairs={{0,4},{4,0},{8,12},{12,8},{16,20},{20,16},{24,28},{28,24},{1,5},{5... | collective-permute-start | bytes 1572872 | tf_op jit(solution)/shard_map/ppermute | solution.py:23
  3.2 0.0 collective-permute-start
  3.3 0.5 %collective-permute-start.1 = (f32[1,15,8,256]{3,2,1,0:T(8,128)}, f32[1,15,8,256]{3,2,1,0:T(8,128)S(1)}, u32[]{:S(2)}, u32[]{:S(2)}) collective-permute-start(f32[1,15,8,256]{3,2,1,0:T(8,128)} %diffusion_in.1), channel_id=1, source_target_pairs={{0,1},{1,0},{2,3},{3,2},{4,5},{5,4},{6,7},{7,6},{8,9},{9,8},{10,11... | collective-permute-start | bytes 368648 | tf_op jit(solution)/shard_map/ppermute | solution.py:23
  3.8 1.4 %collective-permute-done.1.diffusion_other = f32[1,15,8,256]{3,2,1,0:T(8,128)S(1)} collective-permute-done((f32[1,15,8,256]{3,2,1,0:T(8,128)}, f32[1,15,8,256]{3,2,1,0:T(8,128)S(1)}, u32[]{:S(2)}, u32[]{:S(2)}) %collective-permute-start.1) | collective-permute-done | bytes 122912 | tf_op jit(solution)/shard_map/ppermute | solution.py:23
  5.2 0.0 collective-permute-done.wind_other
  5.2 1.6 %collective-permute-start.2 = (f32[3,8,8,256]{3,2,1,0:T(8,128)S(1)}, f32[3,8,8,256]{3,2,1,0:T(8,128)S(1)}, u32[]{:S(2)}, u32[]{:S(2)}) collective-permute-start(f32[3,8,8,256]{3,2,1,0:T(8,128)S(1)} %shard_map.65.met), channel_id=1, source_target_pairs={{0,2},{1,3},{2,0},{3,1},{4,6},{5,7},{6,4},{7,5},{8,10},{9,11},{10,... | collective-permute-start | bytes 589832 | tf_op jit(solution)/shard_map/ppermute | solution.py:23
  6.8 5.5 %collective-permute-done.2.other = f32[3,8,8,256]{3,2,1,0:T(8,128)S(1)} collective-permute-done((f32[3,8,8,256]{3,2,1,0:T(8,128)S(1)}, f32[3,8,8,256]{3,2,1,0:T(8,128)S(1)}, u32[]{:S(2)}, u32[]{:S(2)}) %collective-permute-start.2) | collective-permute-done | bytes 196640 | tf_op jit(solution)/shard_map/ppermute | solution.py:23
  12.2 0.1 shard_map.66
  12.3 2.4 %collective-permute-start.3 = (f32[24,8,256]{2,1,0:T(8,128)S(1)}, f32[24,8,256]{2,1,0:T(8,128)S(1)}, u32[]{:S(2)}, u32[]{:S(2)}) collective-permute-start(f32[24,8,256]{2,1,0:T(8,128)S(1)} %get-tuple-element.28), channel_id=1, source_target_pairs={{0,4},{4,8},{8,12},{12,16},{16,20},{20,24},{24,28},{1,5},{5,9},{9,... | collective-permute-start | bytes 589832 | tf_op jit(solution)/shard_map/ppermute | solution.py:28
  14.7 4.3 %collective-permute-start.4 = (f32[24,8,256]{2,1,0:T(8,128)S(1)}, f32[24,8,256]{2,1,0:T(8,128)S(1)}, u32[]{:S(2)}, u32[]{:S(2)}) collective-permute-start(f32[24,8,256]{2,1,0:T(8,128)S(1)} %get-tuple-element.29), channel_id=1, source_target_pairs={{4,0},{8,4},{12,8},{16,12},{20,16},{24,20},{28,24},{5,1},{9,5},{13... | collective-permute-start | bytes 589832 | tf_op jit(solution)/shard_map/ppermute | solution.py:28
  19.1 0.0 collective-permute-done.9.pair.rest_0_
  19.1 3.5 %collective-permute-start.10 = (f32[4,2,6,8,256]{4,3,2,1,0:T(8,128)S(1)}, f32[4,2,6,8,256]{4,3,2,1,0:T(8,128)S(1)}, u32[]{:S(2)}, u32[]{:S(2)}) collective-permute-start(f32[4,2,6,8,256]{4,3,2,1,0:T(8,128)S(1)} %shard_map.69), channel_id=1, source_target_pairs={{0,8},{8,16},{16,24},{12,4},{20,12},{28,20},{1,9},{9,17},{17,25},{... | collective-permute-start | bytes 1179656 | tf_op jit(solution)/shard_map/ppermute | solution.py:34
  22.6 1.9 %collective-permute-start.7 = (f32[3,2,6,8,256]{4,3,2,1,0:T(8,128)S(1)}, f32[3,2,6,8,256]{4,3,2,1,0:T(8,128)S(1)}, u32[]{:S(2)}, u32[]{:S(2)}) collective-permute-start(f32[3,2,6,8,256]{4,3,2,1,0:T(8,128)S(1)} %get-tuple-element.36), channel_id=1, source_target_pairs={{0,4},{4,8},{8,12},{12,16},{16,20},{20,24},{24,28},{1,5},{5,9},{9,... | collective-permute-start | bytes 884744 | tf_op jit(solution)/shard_map/ppermute | solution.py:28
  24.6 4.8 %collective-permute-start.8 = (f32[3,2,6,8,256]{4,3,2,1,0:T(8,128)S(1)}, f32[3,2,6,8,256]{4,3,2,1,0:T(8,128)S(1)}, u32[]{:S(2)}, u32[]{:S(2)}) collective-permute-start(f32[3,2,6,8,256]{4,3,2,1,0:T(8,128)S(1)} %get-tuple-element.37), channel_id=1, source_target_pairs={{4,0},{8,4},{12,8},{16,12},{20,16},{24,20},{28,24},{5,1},{9,5},{13... | collective-permute-start | bytes 884744 | tf_op jit(solution)/shard_map/ppermute | solution.py:28
  29.4 0.0 collective-permute-done.3.up.rest_0_
  29.4 0.0 collective-permute-done.4.down.rest_1_
  29.4 0.1 collective-permute-start.5
  29.5 0.5 %collective-permute-start.6 = (f32[24,8,256]{2,1,0:T(8,128)S(1)}, f32[24,8,256]{2,1,0:T(8,128)S(1)}, u32[]{:S(2)}, u32[]{:S(2)}) collective-permute-start(f32[24,8,256]{2,1,0:T(8,128)S(1)} %get-tuple-element.32.rest_1_), channel_id=1, source_target_pairs={{0,1},{1,0},{2,3},{3,2},{4,5},{5,4},{6,7},{7,6},{8,9},{9,8},{10,11... | collective-permute-start | bytes 589832 | tf_op jit(solution)/shard_map/ppermute | solution.py:23
  30.0 0.9 %collective-permute-done.5.rest_2_ = f32[24,8,256]{2,1,0:T(8,128)S(1)} collective-permute-done((f32[24,8,256]{2,1,0:T(8,128)S(1)}, f32[24,8,256]{2,1,0:T(8,128)S(1)}, u32[]{:S(2)}, u32[]{:S(2)}) %collective-permute-start.5) | collective-permute-done | bytes 196640 | tf_op jit(solution)/shard_map/ppermute | solution.py:23
  31.0 0.3 collective-permute-done.6.rest_3_
  31.2 0.4 shard_map.68
  31.6 0.0 collective-permute-done.10.rest_1_
  31.6 0.0 copy-done
  31.6 3.0 %shard_map.70.rest_2_ = f32[8,16,8,256]{3,2,1,0:T(8,128)S(1)} custom-call(s32[4]{0:T(128)S(4)} %get-tuple-element.22.numbers._, f32[3,24,5,8,256]{4,3,2,1,0:T(8,128)S(1)} %get-tuple-element.33.coef, f32[16,3,8,256]{3,2,1,0:T(8,128)S(1)} %get-tuple-element.34.solve, f32[8,16,8,256]{3,2,1,0:T(8,128)S(1)} %get-tuple-element.35.own, f32[8,8,256]{2,1,0:T(8,128)S(1)} %copy-done, ...), custom_call_target="tpu_custom_call" | custom-call | bytes 1048576 | tf_op jit(solution)/shard_map/pallas_call | solution.py:375
  34.6 0.8 %shard_map.71.rest_2_ = f32[8,16,8,256]{3,2,1,0:T(8,128)S(1)} custom-call(s32[4]{0:T(128)S(4)} %get-tuple-element.22.numbers._, f32[3,24,5,8,256]{4,3,2,1,0:T(8,128)S(1)} %get-tuple-element.33.coef, f32[16,3,8,256]{3,2,1,0:T(8,128)S(1)} %get-tuple-element.34.solve, f32[8,16,8,256]{3,2,1,0:T(8,128)S(1)} %get-tuple-element.35.own, ...), custom_call_target="tpu_custom_call", output_to_operand_aliasing={{}: (7, {})} | custom-call | bytes 1048576 | tf_op jit(solution)/shard_map/pallas_call | solution.py:375
  35.5 0.6 %collective-permute-done.7.rest_0_ = f32[3,2,6,8,256]{4,3,2,1,0:T(8,128)S(1)} collective-permute-done((f32[3,2,6,8,256]{4,3,2,1,0:T(8,128)S(1)}, f32[3,2,6,8,256]{4,3,2,1,0:T(8,128)S(1)}, u32[]{:S(2)}, u32[]{:S(2)}) %collective-permute-start.7) | collective-permute-done | bytes 294944 | tf_op jit(solution)/shard_map/ppermute | solution.py:28
  36.1 3.1 %collective-permute-done.8.rest_1_ = f32[3,2,6,8,256]{4,3,2,1,0:T(8,128)S(1)} collective-permute-done((f32[3,2,6,8,256]{4,3,2,1,0:T(8,128)S(1)}, f32[3,2,6,8,256]{4,3,2,1,0:T(8,128)S(1)}, u32[]{:S(2)}, u32[]{:S(2)}) %collective-permute-start.8) | collective-permute-done | bytes 294944 | tf_op jit(solution)/shard_map/ppermute | solution.py:28
  39.1 3.1 %shard_map.72 = f32[8,16,8,256]{3,2,1,0:T(8,128)} custom-call(s32[4]{0:T(128)S(4)} %get-tuple-element.22.numbers._, f32[3,24,5,8,256]{4,3,2,1,0:T(8,128)S(1)} %get-tuple-element.33.coef, f32[16,3,8,256]{3,2,1,0:T(8,128)S(1)} %get-tuple-element.34.solve, f32[8,16,8,256]{3,2,1,0:T(8,128)S(1)} %get-tuple-element.35.own, f32[8,8,256]{2,1,0:T(8,128)S(1)} %copy-done, ...), custom_call_target="tpu_custom_call" | custom-call | bytes 1048576 | tf_op jit(solution)/shard_map/pallas_call | solution.py:375
  (3 shorter events, 0.1 us)
Async XLA Ops:
  0.0 31.6 %copy-start = (f32[8,8,256]{2,1,0:T(8,128)S(1)}, f32[8,8,256]{2,1,0:T(8,128)}, u32[]{:S(2)}) copy-start(f32[8,8,256]{2,1,0:T(8,128)} %source.5) | copy-start | bytes 196612
  1.7 17.4 %collective-permute-start.9 = (f32[4,2,8,8,256]{4,3,2,1,0:T(8,128)S(1)}, f32[4,2,8,8,256]{4,3,2,1,0:T(8,128)S(1)}, u32[]{:S(2)}, u32[]{:S(2)}) collective-permute-start(f32[4,2,8,8,256]{4,3,2,1,0:T(8,128)S(1)} %get-tuple-element.38), channel_id=1, source_target_pairs={{0,4},{4,0},{8,12},{12,8},{16,20},{20,16},{24,28},{28,24},{1,5},{5... | collective-permute-start | bytes 1572872 | tf_op jit(solution)/shard_map/ppermute | solution.py:23
  3.2 1.9 %collective-permute-start = (f32[1,2,16,8,256]{4,3,2,1,0:T(8,128)}, f32[1,2,16,8,256]{4,3,2,1,0:T(8,128)S(1)}, u32[]{:S(2)}, u32[]{:S(2)}) collective-permute-start(f32[1,2,16,8,256]{4,3,2,1,0:T(8,128)} %wind_in.1), channel_id=1, source_target_pairs={{0,1},{1,0},{2,3},{3,2},{4,5},{5,4},{6,7},{7,6},{8,9},{9,8},{10,11... | collective-permute-start | bytes 786440 | tf_op jit(solution)/shard_map/ppermute | solution.py:23
  3.3 1.9 %collective-permute-start.1 = (f32[1,15,8,256]{3,2,1,0:T(8,128)}, f32[1,15,8,256]{3,2,1,0:T(8,128)S(1)}, u32[]{:S(2)}, u32[]{:S(2)}) collective-permute-start(f32[1,15,8,256]{3,2,1,0:T(8,128)} %diffusion_in.1), channel_id=1, source_target_pairs={{0,1},{1,0},{2,3},{3,2},{4,5},{5,4},{6,7},{7,6},{8,9},{9,8},{10,11... | collective-permute-start | bytes 368648 | tf_op jit(solution)/shard_map/ppermute | solution.py:23
  5.2 7.0 %collective-permute-start.2 = (f32[3,8,8,256]{3,2,1,0:T(8,128)S(1)}, f32[3,8,8,256]{3,2,1,0:T(8,128)S(1)}, u32[]{:S(2)}, u32[]{:S(2)}) collective-permute-start(f32[3,8,8,256]{3,2,1,0:T(8,128)S(1)} %shard_map.65.met), channel_id=1, source_target_pairs={{0,2},{1,3},{2,0},{3,1},{4,6},{5,7},{6,4},{7,5},{8,10},{9,11},{10,... | collective-permute-start | bytes 589832 | tf_op jit(solution)/shard_map/ppermute | solution.py:23
  12.3 17.1 %collective-permute-start.3 = (f32[24,8,256]{2,1,0:T(8,128)S(1)}, f32[24,8,256]{2,1,0:T(8,128)S(1)}, u32[]{:S(2)}, u32[]{:S(2)}) collective-permute-start(f32[24,8,256]{2,1,0:T(8,128)S(1)} %get-tuple-element.28), channel_id=1, source_target_pairs={{0,4},{4,8},{8,12},{12,16},{16,20},{20,24},{24,28},{1,5},{5,9},{9,... | collective-permute-start | bytes 589832 | tf_op jit(solution)/shard_map/ppermute | solution.py:28
  14.7 14.7 %collective-permute-start.4 = (f32[24,8,256]{2,1,0:T(8,128)S(1)}, f32[24,8,256]{2,1,0:T(8,128)S(1)}, u32[]{:S(2)}, u32[]{:S(2)}) collective-permute-start(f32[24,8,256]{2,1,0:T(8,128)S(1)} %get-tuple-element.29), channel_id=1, source_target_pairs={{4,0},{8,4},{12,8},{16,12},{20,16},{24,20},{28,24},{5,1},{9,5},{13... | collective-permute-start | bytes 589832 | tf_op jit(solution)/shard_map/ppermute | solution.py:28
  19.1 12.5 %collective-permute-start.10 = (f32[4,2,6,8,256]{4,3,2,1,0:T(8,128)S(1)}, f32[4,2,6,8,256]{4,3,2,1,0:T(8,128)S(1)}, u32[]{:S(2)}, u32[]{:S(2)}) collective-permute-start(f32[4,2,6,8,256]{4,3,2,1,0:T(8,128)S(1)} %shard_map.69), channel_id=1, source_target_pairs={{0,8},{8,16},{16,24},{12,4},{20,12},{28,20},{1,9},{9,17},{17,25},{... | collective-permute-start | bytes 1179656 | tf_op jit(solution)/shard_map/ppermute | solution.py:34
  22.6 13.4 %collective-permute-start.7 = (f32[3,2,6,8,256]{4,3,2,1,0:T(8,128)S(1)}, f32[3,2,6,8,256]{4,3,2,1,0:T(8,128)S(1)}, u32[]{:S(2)}, u32[]{:S(2)}) collective-permute-start(f32[3,2,6,8,256]{4,3,2,1,0:T(8,128)S(1)} %get-tuple-element.36), channel_id=1, source_target_pairs={{0,4},{4,8},{8,12},{12,16},{16,20},{20,24},{24,28},{1,5},{5,9},{9,... | collective-permute-start | bytes 884744 | tf_op jit(solution)/shard_map/ppermute | solution.py:28
  24.6 14.6 %collective-permute-start.8 = (f32[3,2,6,8,256]{4,3,2,1,0:T(8,128)S(1)}, f32[3,2,6,8,256]{4,3,2,1,0:T(8,128)S(1)}, u32[]{:S(2)}, u32[]{:S(2)}) collective-permute-start(f32[3,2,6,8,256]{4,3,2,1,0:T(8,128)S(1)} %get-tuple-element.37), channel_id=1, source_target_pairs={{4,0},{8,4},{12,8},{16,12},{20,16},{24,20},{28,24},{5,1},{9,5},{13... | collective-permute-start | bytes 884744 | tf_op jit(solution)/shard_map/ppermute | solution.py:28
  29.4 1.5 %collective-permute-start.5 = (f32[24,8,256]{2,1,0:T(8,128)S(1)}, f32[24,8,256]{2,1,0:T(8,128)S(1)}, u32[]{:S(2)}, u32[]{:S(2)}) collective-permute-start(f32[24,8,256]{2,1,0:T(8,128)S(1)} %get-tuple-element.31.rest_0_), channel_id=1, source_target_pairs={{0,1},{1,0},{2,3},{3,2},{4,5},{5,4},{6,7},{7,6},{8,9},{9,8},{10,11... | collective-permute-start | bytes 589832 | tf_op jit(solution)/shard_map/ppermute | solution.py:23
  29.5 1.7 %collective-permute-start.6 = (f32[24,8,256]{2,1,0:T(8,128)S(1)}, f32[24,8,256]{2,1,0:T(8,128)S(1)}, u32[]{:S(2)}, u32[]{:S(2)}) collective-permute-start(f32[24,8,256]{2,1,0:T(8,128)S(1)} %get-tuple-element.32.rest_1_), channel_id=1, source_target_pairs={{0,1},{1,0},{2,3},{3,2},{4,5},{5,4},{6,7},{7,6},{8,9},{9,8},{10,11... | collective-permute-start | bytes 589832 | tf_op jit(solution)/shard_map/ppermute | solution.py:23

commit v4 on v3

--- a/solution.py
+++ b/solution.py
@@ -23,9 +23,10 @@
     return lax.ppermute(value, axis, [(i, i ^ bit) for i in range(count)])
 
 
-def shift(value, axis, by):
+def cross(value, axis):
     count = lax.axis_size(axis)
-    return lax.ppermute(value, axis, [(i, i + by) for i in range(count) if 0 <= i + by < count])
+    pairs = [(i, i + 1) for i in range(1, count - 1, 2)]
+    return lax.ppermute(value, axis, pairs + [(j, i) for i, j in pairs])
 
 
 def relay(value, axis):
@@ -60,26 +61,29 @@
     out[...] = jnp.where((slot & bit) == (group & bit), met[...], other[...])
 
 
-def last_choice_kernel(bit, numbers, met, other, tracers_up, tracers_down, *rest):
-    wind, up, down, mix = rest[-4:]
+def last_choice_kernel(bit, numbers, met, other, tracers_pair, tracers_far, *rest):
+    wind, to_pair, to_far, mix = rest[-4:]
     group = lax.axis_index("group")
     mine = (numbers[0] & bit) == (group & bit)
+    even = lax.axis_index("tile") % 2 == 0
     _, height, deep, width = wind.shape
-    count, groups, reach = tracers_up.shape[:3]
+    count, groups, reach = tracers_pair.shape[:3]
     for kind in range(2):
+        rows = [
+            jnp.where(mine, met[kind, :, j, :], other[kind, :, j, :]) for j in range(height)
+        ]
         for j in range(height):
-            value = jnp.where(mine, met[kind, :, j, :], other[kind, :, j, :])
-            wind[kind, j] = value
-            if j < reach:
-                down[kind * reach + j] = value
-            if j >= height - reach:
-                up[kind * reach + j - (height - reach)] = value
+            wind[kind, j] = rows[j]
+        for j in range(reach):
+            last, first = rows[height - reach + j], rows[j]
+            to_pair[kind * reach + j] = jnp.where(even, last, first)
+            to_far[kind * reach + j] = jnp.where(even, first, last)
     mix[...] = jnp.where(mine, met[2], other[2])
     for n in range(count):
         for g in range(groups):
             at = (2 + n * groups + g) * reach
-            up[at : at + reach] = tracers_up[n, g]
-            down[at : at + reach] = tracers_down[n, g]
+            to_pair[at : at + reach] = tracers_pair[n, g]
+            to_far[at : at + reach] = tracers_far[n, g]
 
 
 def onward_kernel(_, pair, *rest):
@@ -108,6 +112,7 @@
     for copy in copies:
         copy.start()
     tile = lax.axis_index("tile")
+    even = tile % 2 == 0
     _, levels, height, _ = tracers.shape
     straight = [outs[-4:-2], outs[-2:]]
     reach = outs[-1].shape[2]
@@ -120,12 +125,14 @@
                 for j in range(height):
                     part[n, g, j] = tracers[start + n, deep, j, :]
             start += count
-        for up, down in straight:
-            for n in range(up.shape[0]):
+        for to_pair, to_far in straight:
+            for n in range(to_pair.shape[0]):
+                rows = [tracers[start + n, deep, j, :] for j in range(height)]
                 for j in range(reach):
-                    up[n, g, j] = tracers[start + n, deep, height - reach + j, :]
-                    down[n, g, j] = tracers[start + n, deep, j, :]
-            start += up.shape[0]
+                    last, first = rows[height - reach + j], rows[j]
+                    to_pair[n, g, j] = jnp.where(even, last, first)
+                    to_far[n, g, j] = jnp.where(even, first, last)
+            start += to_pair.shape[0]
     copies[0].wait()
     copies[1].wait()
     numbers[0] = loader[tile]
@@ -185,15 +192,18 @@
     )(in_smem(numbers), *in_vmem(operands), *waits)
 
 
-def gather_kernel(_, wind, up, down, mix, *rest):
+def gather_kernel(_, wind, pair, far, mix, *rest):
     height = wind.shape[1]
     half = height // 2
     rows = rest[-1].shape[0] - half
     reach = (rows - height) // 2
+    even = lax.axis_index("tile") % 2 == 0
+    pair_at = jnp.where(even, reach + height, 0)
+    far_at = jnp.where(even, 0, reach + height)
     for kind, out in enumerate(rest[-2:]):
-        out[:reach] = up[pl.ds(kind * reach, reach)]
+        out[pl.ds(pair_at, reach)] = pair[pl.ds(kind * reach, reach)]
         out[pl.ds(reach, height)] = wind[kind]
-        out[pl.ds(reach + height, reach)] = down[pl.ds(kind * reach, reach)]
+        out[pl.ds(far_at, reach)] = far[pl.ds(kind * reach, reach)]
         out[rows:] = mix[pl.ds(kind * half, half)]
 
 
@@ -271,7 +281,7 @@
 
 
 def window_kernel(way, start, count, last, numbers, coef, solve, own, source, *rest):
-    first, second, *rest = rest
+    pair, far, *rest = rest
     if last:
         prior, out, field, advected, values, solved, sem = rest
         early = pltpu.make_async_copy(prior.at[:start], out.at[:start], sem.at[0])
@@ -284,7 +294,7 @@
     groups = levels // DEEP
     tile = lax.axis_index("tile")
     even = tile % 2 == 0
-    pair_at = jnp.where(even, 2 * height, 0)
+    pair_at = jnp.where(even, 2 * height, 0 if way == "relay" else height - reach)
     far_at = jnp.where(even, height - reach, 2 * height)
     counts = [numbers[t] for t in range(1, 4)]
     for n in range(tracers):
@@ -293,19 +303,16 @@
             for j in range(height):
                 field[0, n, g, height + j] = own[start + n, deep, j, :]
             for j in range(reach):
-                if way == "relay":
-                    field[0, n, g, far_at + j] = second[n, g, j]
+                if way == "winds":
+                    at = (2 + n * groups + g) * reach + j
+                    near, distant = pair[at], far[at]
                 else:
-                    if way == "winds":
-                        at = (2 + n * groups + g) * reach + j
-                        south, north = first[at], second[at]
-                    else:
-                        south, north = first[n, g, j], second[n, g, j]
-                    field[0, n, g, height - reach + j] = south
-                    field[0, n, g, 2 * height + j] = north
+                    near, distant = pair[n, g, j], far[n, g, j]
+                field[0, n, g, pair_at + j] = near
+                field[0, n, g, far_at + j] = distant
             if way == "relay":
-                for j in range(height):
-                    field[0, n, g, pair_at + j] = first[n, g, j]
+                for j in range(reach, height):
+                    field[0, n, g, pair_at + j] = pair[n, g, j]
     for step in range(ROUNDS):
         reach = ROUNDS - 1 - step
         low, high = height - reach, 2 * height + reach
@@ -393,7 +400,7 @@
     _, levels, height, width = tracers.shape
     half = levels // 2
     wind_other, diffusion_other = exchange(winds, "group", 1), exchange(diffusivity, "group", 1)
-    numbers, tracers, winds, diffusivity, *parts, up_first, down_first, up, down = pack(
+    numbers, tracers, winds, diffusivity, *parts, pair_first, far_first, to_pair, to_far = pack(
         tiles, substeps, loader, tracers, winds, diffusivity
     )
 
@@ -420,10 +427,10 @@
         )
         bit *= 2
     with_winds = 2 * ROUNDS * (1 + WITH_WINDS)
-    wind, wind_up, wind_down, mix = on_core(
+    wind, wind_pair, wind_far, mix = on_core(
         functools.partial(last_choice_kernel, bit),
         numbers,
-        [met, exchange(met, "group", bit), up_first, down_first],
+        [met, exchange(met, "group", bit), pair_first, far_first],
         [
             pltpu.VMEM((2, height, half, width), jnp.float32),
             pltpu.VMEM((with_winds, half, width), jnp.float32),
@@ -431,13 +438,13 @@
             pltpu.VMEM((half, height, width), jnp.float32),
         ],
     )
-    wind_up, wind_down = shift(wind_up, "tile", 1), shift(wind_down, "tile", -1)
-    halos.append(("winds", WITH_WINDS, (wind_up, wind_down)))
-    halos.append(("straight", STRAIGHT, (shift(up, "tile", 1), shift(down, "tile", -1))))
+    wind_pair, wind_far = exchange(wind_pair, "tile", 1), cross(wind_far, "tile")
+    halos.append(("winds", WITH_WINDS, (wind_pair, wind_far)))
+    halos.append(("straight", STRAIGHT, (exchange(to_pair, "tile", 1), cross(to_far, "tile"))))
     known = on_core(
         gather_kernel,
         numbers,
-        [wind, wind_up, wind_down, mix],
+        [wind, wind_pair, wind_far, mix],
         [pltpu.VMEM((height + 2 * ROUNDS + height // 2, half, width), jnp.float32)] * 2,
     )
     coef, solve = prepare(

time: 42.6 us -> 41.3 us (0.969)
  the two profiles are of different devices: /device:TPU:8 before, /device:TPU:0 now
where the time goes in v4:
time: 41.3 us; the launch traced here: 41.1 us
  waiting for transfers between devices  20.3 us (49%)
  starting transfers between devices  11.4 us (28%)
  Pallas kernels  9.38 us (23%)
    ppermute x8, waiting for transfers between devices, exchange(): return lax.ppermute(value, axis, [(i, i ^ bit) for i in range(count)])  20.3 us
    pallas_call x3, Pallas kernels, window(): pl.pallas_call(functools.partial(window_kernel, way, start, count, last),...  6.9 us
    ppermute x8, starting transfers between devices, exchange(): return lax.ppermute(value, axis, [(i, i ^ bit) for i in range(count)])  6.06 us
    ppermute x1, starting transfers between devices, relay(): return lax.ppermute(value, axis, pairs)  3.95 us
    pallas_call x1, Pallas kernels, pack(): pl.pallas_call(functools.partial(pack_kernel, RELAYED, tiles), out_shape=...  1.84 us
    ppermute x2, starting transfers between devices, cross(): return lax.ppermute(value, axis, pairs + [(j, i) for i, j in pairs])  1.34 us
  transfers between devices with their start and end apart: 11, of which 6 were waited for; matrix products, arithmetic and copies ran while one was open for 0% of the time, Pallas kernels for 11%

profile of v4, /device:TPU:0, one launch (start us, length us, event | category | flops | bytes accessed | tf_op | source)
XLA Modules:
  0.0 41.1 jit_solution(3013220309965494015)
XLA Ops:
  0.0 0.0 copy-start
  0.0 1.8 %shard_map.64 = (s32[4]{0:T(128)S(4)}, f32[8,16,8,256]{3,2,1,0:T(8,128)S(1)}, f32[1,2,16,8,256]{4,3,2,1,0:T(8,128)S(1)}, f32[1,15,8,256]{3,2,1,0:T(8,128)S(1)}, ...) custom-call(s32[8]{0:T(128)} %substeps_in.1, ...), custom_call_target="tpu_custom_call" | custom-call | bytes 1048576 | tf_op jit(solution)/shard_map/pallas_call | solution.py:159
  1.8 3.0 %collective-permute-start.9 = (f32[4,2,8,8,256]{4,3,2,1,0:T(8,128)S(1)}, f32[4,2,8,8,256]{4,3,2,1,0:T(8,128)S(1)}, u32[]{:S(2)}, u32[]{:S(2)}) collective-permute-start(f32[4,2,8,8,256]{4,3,2,1,0:T(8,128)S(1)} %get-tuple-element.38), channel_id=1, source_target_pairs={{0,4},{4,0},{8,12},{12,8},{16,20},{20,16},{24,28},{28,24},{1,5},{5... | collective-permute-start | bytes 1572872 | tf_op jit(solution)/shard_map/ppermute | solution.py:23
  4.9 0.0 collective-permute-start
  4.9 0.5 %collective-permute-start.1 = (f32[1,15,8,256]{3,2,1,0:T(8,128)}, f32[1,15,8,256]{3,2,1,0:T(8,128)S(1)}, u32[]{:S(2)}, u32[]{:S(2)}) collective-permute-start(f32[1,15,8,256]{3,2,1,0:T(8,128)} %diffusion_in.1), channel_id=1, source_target_pairs={{0,1},{1,0},{2,3},{3,2},{4,5},{5,4},{6,7},{7,6},{8,9},{9,8},{10,11... | collective-permute-start | bytes 368648 | tf_op jit(solution)/shard_map/ppermute | solution.py:23
  5.4 1.4 %collective-permute-done.1.diffusion_other = f32[1,15,8,256]{3,2,1,0:T(8,128)S(1)} collective-permute-done((f32[1,15,8,256]{3,2,1,0:T(8,128)}, f32[1,15,8,256]{3,2,1,0:T(8,128)S(1)}, u32[]{:S(2)}, u32[]{:S(2)}) %collective-permute-start.1) | collective-permute-done | bytes 122912 | tf_op jit(solution)/shard_map/ppermute | solution.py:23
  6.8 0.0 collective-permute-done.wind_other
  6.8 1.6 %collective-permute-start.2 = (f32[3,8,8,256]{3,2,1,0:T(8,128)S(1)}, f32[3,8,8,256]{3,2,1,0:T(8,128)S(1)}, u32[]{:S(2)}, u32[]{:S(2)}) collective-permute-start(f32[3,8,8,256]{3,2,1,0:T(8,128)S(1)} %shard_map.65.met), channel_id=1, source_target_pairs={{0,2},{1,3},{2,0},{3,1},{4,6},{5,7},{6,4},{7,5},{8,10},{9,11},{10,... | collective-permute-start | bytes 589832 | tf_op jit(solution)/shard_map/ppermute | solution.py:23
  8.4 5.5 %collective-permute-done.2.other = f32[3,8,8,256]{3,2,1,0:T(8,128)S(1)} collective-permute-done((f32[3,8,8,256]{3,2,1,0:T(8,128)S(1)}, f32[3,8,8,256]{3,2,1,0:T(8,128)S(1)}, u32[]{:S(2)}, u32[]{:S(2)}) %collective-permute-start.2) | collective-permute-done | bytes 196640 | tf_op jit(solution)/shard_map/ppermute | solution.py:23
  13.8 0.2 shard_map.66
  14.0 0.3 collective-permute-start.3
  14.4 0.7 %collective-permute-start.4 = (f32[24,8,256]{2,1,0:T(8,128)S(1)}, f32[24,8,256]{2,1,0:T(8,128)S(1)}, u32[]{:S(2)}, u32[]{:S(2)}) collective-permute-start(f32[24,8,256]{2,1,0:T(8,128)S(1)} %get-tuple-element.29), channel_id=1, source_target_pairs={{4,8},{12,16},{20,24},{8,4},{16,12},{24,20},{5,9},{13,17},{21,25},... | collective-permute-start | bytes 589832 | tf_op jit(solution)/shard_map/ppermute | solution.py:29
  15.0 2.5 %collective-permute-done.9.pair.rest_0_ = f32[4,2,8,8,256]{4,3,2,1,0:T(8,128)S(1)} collective-permute-done((f32[4,2,8,8,256]{4,3,2,1,0:T(8,128)S(1)}, f32[4,2,8,8,256]{4,3,2,1,0:T(8,128)S(1)}, u32[]{:S(2)}, u32[]{:S(2)}) %collective-permute-start.9) | collective-permute-done | bytes 524320 | tf_op jit(solution)/shard_map/ppermute | solution.py:23
  17.6 4.0 %collective-permute-start.10 = (f32[4,2,6,8,256]{4,3,2,1,0:T(8,128)S(1)}, f32[4,2,6,8,256]{4,3,2,1,0:T(8,128)S(1)}, u32[]{:S(2)}, u32[]{:S(2)}) collective-permute-start(f32[4,2,6,8,256]{4,3,2,1,0:T(8,128)S(1)} %shard_map.69), channel_id=1, source_target_pairs={{0,8},{8,16},{16,24},{12,4},{20,12},{28,20},{1,9},{9,17},{17,25},{... | collective-permute-start | bytes 1179656 | tf_op jit(solution)/shard_map/ppermute | solution.py:35
  21.5 0.1 collective-permute-start.7
  21.6 0.7 %collective-permute-start.8 = (f32[3,2,6,8,256]{4,3,2,1,0:T(8,128)S(1)}, f32[3,2,6,8,256]{4,3,2,1,0:T(8,128)S(1)}, u32[]{:S(2)}, u32[]{:S(2)}) collective-permute-start(f32[3,2,6,8,256]{4,3,2,1,0:T(8,128)S(1)} %get-tuple-element.37), channel_id=1, source_target_pairs={{4,8},{12,16},{20,24},{8,4},{16,12},{24,20},{5,9},{13,17},{21,25},... | collective-permute-start | bytes 884744 | tf_op jit(solution)/shard_map/ppermute | solution.py:29
  22.3 9.7 %collective-permute-done.3.pair.rest_0_ = f32[24,8,256]{2,1,0:T(8,128)S(1)} collective-permute-done((f32[24,8,256]{2,1,0:T(8,128)S(1)}, f32[24,8,256]{2,1,0:T(8,128)S(1)}, u32[]{:S(2)}, u32[]{:S(2)}) %collective-permute-start.3) | collective-permute-done | bytes 196640 | tf_op jit(solution)/shard_map/ppermute | solution.py:23
  32.0 0.0 collective-permute-done.4.far.rest_1_
  32.0 0.1 collective-permute-start.5
  32.1 0.5 %collective-permute-start.6 = (f32[24,8,256]{2,1,0:T(8,128)S(1)}, f32[24,8,256]{2,1,0:T(8,128)S(1)}, u32[]{:S(2)}, u32[]{:S(2)}) collective-permute-start(f32[24,8,256]{2,1,0:T(8,128)S(1)} %get-tuple-element.32.rest_1_), channel_id=1, source_target_pairs={{0,1},{1,0},{2,3},{3,2},{4,5},{5,4},{6,7},{7,6},{8,9},{9,8},{10,11... | collective-permute-start | bytes 589832 | tf_op jit(solution)/shard_map/ppermute | solution.py:23
  32.6 0.9 %collective-permute-done.5.rest_2_ = f32[24,8,256]{2,1,0:T(8,128)S(1)} collective-permute-done((f32[24,8,256]{2,1,0:T(8,128)S(1)}, f32[24,8,256]{2,1,0:T(8,128)S(1)}, u32[]{:S(2)}, u32[]{:S(2)}) %collective-permute-start.5) | collective-permute-done | bytes 196640 | tf_op jit(solution)/shard_map/ppermute | solution.py:23
  33.5 0.3 collective-permute-done.6.rest_3_
  33.8 0.4 shard_map.68
  34.2 0.0 collective-permute-done.10.rest_1_
  34.2 0.0 copy-done
  34.2 3.0 %shard_map.70.rest_2_ = f32[8,16,8,256]{3,2,1,0:T(8,128)S(1)} custom-call(s32[4]{0:T(128)S(4)} %get-tuple-element.22.numbers._, f32[3,24,5,8,256]{4,3,2,1,0:T(8,128)S(1)} %get-tuple-element.33.coef, f32[16,3,8,256]{3,2,1,0:T(8,128)S(1)} %get-tuple-element.34.solve, f32[8,16,8,256]{3,2,1,0:T(8,128)S(1)} %get-tuple-element.35.own, f32[8,8,256]{2,1,0:T(8,128)S(1)} %copy-done, ...), custom_call_target="tpu_custom_call" | custom-call | bytes 1048576 | tf_op jit(solution)/shard_map/pallas_call | solution.py:382
  37.2 0.9 %shard_map.71.rest_2_ = f32[8,16,8,256]{3,2,1,0:T(8,128)S(1)} custom-call(s32[4]{0:T(128)S(4)} %get-tuple-element.22.numbers._, f32[3,24,5,8,256]{4,3,2,1,0:T(8,128)S(1)} %get-tuple-element.33.coef, f32[16,3,8,256]{3,2,1,0:T(8,128)S(1)} %get-tuple-element.34.solve, f32[8,16,8,256]{3,2,1,0:T(8,128)S(1)} %get-tuple-element.35.own, ...), custom_call_target="tpu_custom_call", output_to_operand_aliasing={{}: (7, {})} | custom-call | bytes 1048576 | tf_op jit(solution)/shard_map/pallas_call | solution.py:382
  38.1 0.0 collective-permute-done.7.rest_0_
  38.1 0.0 collective-permute-done.8.rest_1_
  38.1 3.0 %shard_map.72 = f32[8,16,8,256]{3,2,1,0:T(8,128)} custom-call(s32[4]{0:T(128)S(4)} %get-tuple-element.22.numbers._, f32[3,24,5,8,256]{4,3,2,1,0:T(8,128)S(1)} %get-tuple-element.33.coef, f32[16,3,8,256]{3,2,1,0:T(8,128)S(1)} %get-tuple-element.34.solve, f32[8,16,8,256]{3,2,1,0:T(8,128)S(1)} %get-tuple-element.35.own, f32[8,8,256]{2,1,0:T(8,128)S(1)} %copy-done, ...), custom_call_target="tpu_custom_call" | custom-call | bytes 1048576 | tf_op jit(solution)/shard_map/pallas_call | solution.py:382
  (3 shorter events, 0.1 us)
Async XLA Ops:
  0.0 34.2 %copy-start = (f32[8,8,256]{2,1,0:T(8,128)S(1)}, f32[8,8,256]{2,1,0:T(8,128)}, u32[]{:S(2)}) copy-start(f32[8,8,256]{2,1,0:T(8,128)} %source.5) | copy-start | bytes 196612
  1.8 15.7 %collective-permute-start.9 = (f32[4,2,8,8,256]{4,3,2,1,0:T(8,128)S(1)}, f32[4,2,8,8,256]{4,3,2,1,0:T(8,128)S(1)}, u32[]{:S(2)}, u32[]{:S(2)}) collective-permute-start(f32[4,2,8,8,256]{4,3,2,1,0:T(8,128)S(1)} %get-tuple-element.38), channel_id=1, source_target_pairs={{0,4},{4,0},{8,12},{12,8},{16,20},{20,16},{24,28},{28,24},{1,5},{5... | collective-permute-start | bytes 1572872 | tf_op jit(solution)/shard_map/ppermute | solution.py:23
  4.9 1.9 %collective-permute-start = (f32[1,2,16,8,256]{4,3,2,1,0:T(8,128)}, f32[1,2,16,8,256]{4,3,2,1,0:T(8,128)S(1)}, u32[]{:S(2)}, u32[]{:S(2)}) collective-permute-start(f32[1,2,16,8,256]{4,3,2,1,0:T(8,128)} %wind_in.1), channel_id=1, source_target_pairs={{0,1},{1,0},{2,3},{3,2},{4,5},{5,4},{6,7},{7,6},{8,9},{9,8},{10,11... | collective-permute-start | bytes 786440 | tf_op jit(solution)/shard_map/ppermute | solution.py:23
  4.9 1.9 %collective-permute-start.1 = (f32[1,15,8,256]{3,2,1,0:T(8,128)}, f32[1,15,8,256]{3,2,1,0:T(8,128)S(1)}, u32[]{:S(2)}, u32[]{:S(2)}) collective-permute-start(f32[1,15,8,256]{3,2,1,0:T(8,128)} %diffusion_in.1), channel_id=1, source_target_pairs={{0,1},{1,0},{2,3},{3,2},{4,5},{5,4},{6,7},{7,6},{8,9},{9,8},{10,11... | collective-permute-start | bytes 368648 | tf_op jit(solution)/shard_map/ppermute | solution.py:23
  6.8 7.0 %collective-permute-start.2 = (f32[3,8,8,256]{3,2,1,0:T(8,128)S(1)}, f32[3,8,8,256]{3,2,1,0:T(8,128)S(1)}, u32[]{:S(2)}, u32[]{:S(2)}) collective-permute-start(f32[3,8,8,256]{3,2,1,0:T(8,128)S(1)} %shard_map.65.met), channel_id=1, source_target_pairs={{0,2},{1,3},{2,0},{3,1},{4,6},{5,7},{6,4},{7,5},{8,10},{9,11},{10,... | collective-permute-start | bytes 589832 | tf_op jit(solution)/shard_map/ppermute | solution.py:23
  14.0 17.9 %collective-permute-start.3 = (f32[24,8,256]{2,1,0:T(8,128)S(1)}, f32[24,8,256]{2,1,0:T(8,128)S(1)}, u32[]{:S(2)}, u32[]{:S(2)}) collective-permute-start(f32[24,8,256]{2,1,0:T(8,128)S(1)} %get-tuple-element.28), channel_id=1, source_target_pairs={{0,4},{4,0},{8,12},{12,8},{16,20},{20,16},{24,28},{28,24},{1,5},{5... | collective-permute-start | bytes 589832 | tf_op jit(solution)/shard_map/ppermute | solution.py:23
  14.4 17.6 %collective-permute-start.4 = (f32[24,8,256]{2,1,0:T(8,128)S(1)}, f32[24,8,256]{2,1,0:T(8,128)S(1)}, u32[]{:S(2)}, u32[]{:S(2)}) collective-permute-start(f32[24,8,256]{2,1,0:T(8,128)S(1)} %get-tuple-element.29), channel_id=1, source_target_pairs={{4,8},{12,16},{20,24},{8,4},{16,12},{24,20},{5,9},{13,17},{21,25},... | collective-permute-start | bytes 589832 | tf_op jit(solution)/shard_map/ppermute | solution.py:29
  17.6 16.6 %collective-permute-start.10 = (f32[4,2,6,8,256]{4,3,2,1,0:T(8,128)S(1)}, f32[4,2,6,8,256]{4,3,2,1,0:T(8,128)S(1)}, u32[]{:S(2)}, u32[]{:S(2)}) collective-permute-start(f32[4,2,6,8,256]{4,3,2,1,0:T(8,128)S(1)} %shard_map.69), channel_id=1, source_target_pairs={{0,8},{8,16},{16,24},{12,4},{20,12},{28,20},{1,9},{9,17},{17,25},{... | collective-permute-start | bytes 1179656 | tf_op jit(solution)/shard_map/ppermute | solution.py:35
  21.5 16.5 %collective-permute-start.7 = (f32[3,2,6,8,256]{4,3,2,1,0:T(8,128)S(1)}, f32[3,2,6,8,256]{4,3,2,1,0:T(8,128)S(1)}, u32[]{:S(2)}, u32[]{:S(2)}) collective-permute-start(f32[3,2,6,8,256]{4,3,2,1,0:T(8,128)S(1)} %get-tuple-element.36), channel_id=1, source_target_pairs={{0,4},{4,0},{8,12},{12,8},{16,20},{20,16},{24,28},{28,24},{1,5},{5... | collective-permute-start | bytes 884744 | tf_op jit(solution)/shard_map/ppermute | solution.py:23
  21.6 16.5 %collective-permute-start.8 = (f32[3,2,6,8,256]{4,3,2,1,0:T(8,128)S(1)}, f32[3,2,6,8,256]{4,3,2,1,0:T(8,128)S(1)}, u32[]{:S(2)}, u32[]{:S(2)}) collective-permute-start(f32[3,2,6,8,256]{4,3,2,1,0:T(8,128)S(1)} %get-tuple-element.37), channel_id=1, source_target_pairs={{4,8},{12,16},{20,24},{8,4},{16,12},{24,20},{5,9},{13,17},{21,25},... | collective-permute-start | bytes 884744 | tf_op jit(solution)/shard_map/ppermute | solution.py:29
  32.0 1.5 %collective-permute-start.5 = (f32[24,8,256]{2,1,0:T(8,128)S(1)}, f32[24,8,256]{2,1,0:T(8,128)S(1)}, u32[]{:S(2)}, u32[]{:S(2)}) collective-permute-start(f32[24,8,256]{2,1,0:T(8,128)S(1)} %get-tuple-element.31.rest_0_), channel_id=1, source_target_pairs={{0,1},{1,0},{2,3},{3,2},{4,5},{5,4},{6,7},{7,6},{8,9},{9,8},{10,11... | collective-permute-start | bytes 589832 | tf_op jit(solution)/shard_map/ppermute | solution.py:23
  32.1 1.7 %collective-permute-start.6 = (f32[24,8,256]{2,1,0:T(8,128)S(1)}, f32[24,8,256]{2,1,0:T(8,128)S(1)}, u32[]{:S(2)}, u32[]{:S(2)}) collective-permute-start(f32[24,8,256]{2,1,0:T(8,128)S(1)} %get-tuple-element.32.rest_1_), channel_id=1, source_target_pairs={{0,1},{1,0},{2,3},{3,2},{4,5},{5,4},{6,7},{7,6},{8,9},{9,8},{10,11... | collective-permute-start | bytes 589832 | tf_op jit(solution)/shard_map/ppermute | solution.py:23

commit v5 on v4

--- a/solution.py
+++ b/solution.py
@@ -10,8 +10,8 @@
 ROUNDS = 6
 DEEP = 8
 RELAYED = (4,)
-WITH_WINDS = 1
-STRAIGHT = 3
+STRAIGHT = (3, 1)
+ORDER = (0, 1, 2)
 MIB = 1024 * 1024
 VMEM_LIMIT = 32 * MIB
 WINDOW_COST = 1
@@ -61,13 +61,13 @@
     out[...] = jnp.where((slot & bit) == (group & bit), met[...], other[...])
 
 
-def last_choice_kernel(bit, numbers, met, other, tracers_pair, tracers_far, *rest):
+def last_choice_kernel(bit, numbers, met, other, *rest):
     wind, to_pair, to_far, mix = rest[-4:]
     group = lax.axis_index("group")
     mine = (numbers[0] & bit) == (group & bit)
     even = lax.axis_index("tile") % 2 == 0
-    _, height, deep, width = wind.shape
-    count, groups, reach = tracers_pair.shape[:3]
+    _, height, _, _ = wind.shape
+    reach = to_pair.shape[1]
     for kind in range(2):
         rows = [
             jnp.where(mine, met[kind, :, j, :], other[kind, :, j, :]) for j in range(height)
@@ -76,14 +76,9 @@
             wind[kind, j] = rows[j]
         for j in range(reach):
             last, first = rows[height - reach + j], rows[j]
-            to_pair[kind * reach + j] = jnp.where(even, last, first)
-            to_far[kind * reach + j] = jnp.where(even, first, last)
+            to_pair[kind, j] = jnp.where(even, last, first)
+            to_far[kind, j] = jnp.where(even, first, last)
     mix[...] = jnp.where(mine, met[2], other[2])
-    for n in range(count):
-        for g in range(groups):
-            at = (2 + n * groups + g) * reach
-            to_pair[at : at + reach] = tracers_pair[n, g]
-            to_far[at : at + reach] = tracers_far[n, g]
 
 
 def onward_kernel(_, pair, *rest):
@@ -114,7 +109,7 @@
     tile = lax.axis_index("tile")
     even = tile % 2 == 0
     _, levels, height, _ = tracers.shape
-    straight = [outs[-4:-2], outs[-2:]]
+    straight = list(zip(outs[len(relayed) :: 2], outs[len(relayed) + 1 :: 2]))
     reach = outs[-1].shape[2]
     copies[2].wait()
     for g in range(levels // DEEP):
@@ -152,7 +147,8 @@
     out_shape = [pltpu.SMEM((4,), jnp.int32)]
     out_shape += [pltpu.VMEM(x.shape, x.dtype) for x in (tracers, winds, diffusivity)]
     out_shape += [rows_of(count, height) for count in RELAYED]
-    out_shape += [rows_of(WITH_WINDS, ROUNDS)] * 2 + [rows_of(STRAIGHT, ROUNDS)] * 2
+    for count in STRAIGHT:
+        out_shape += [rows_of(count, ROUNDS)] * 2
     vmem = pl.BlockSpec(memory_space=pltpu.VMEM)
     smem = pl.BlockSpec(memory_space=pltpu.SMEM)
     hbm = pl.BlockSpec(memory_space=pltpu.HBM)
@@ -192,19 +188,18 @@
     )(in_smem(numbers), *in_vmem(operands), *waits)
 
 
-def gather_kernel(_, wind, pair, far, mix, *rest):
+def gather_kernel(_, wind, mix, pair, far, *rest):
     height = wind.shape[1]
     half = height // 2
-    rows = rest[-1].shape[0] - half
-    reach = (rows - height) // 2
+    reach = pair.shape[1]
     even = lax.axis_index("tile") % 2 == 0
     pair_at = jnp.where(even, reach + height, 0)
     far_at = jnp.where(even, 0, reach + height)
     for kind, out in enumerate(rest[-2:]):
-        out[pl.ds(pair_at, reach)] = pair[pl.ds(kind * reach, reach)]
+        out[pl.ds(pair_at, reach)] = pair[kind]
         out[pl.ds(reach, height)] = wind[kind]
-        out[pl.ds(far_at, reach)] = far[pl.ds(kind * reach, reach)]
-        out[rows:] = mix[pl.ds(kind * half, half)]
+        out[pl.ds(far_at, reach)] = far[kind]
+        out[pl.ds(2 * reach + height, half)] = mix[pl.ds(kind * half, half)]
 
 
 def prepare_kernel(height, reach, numbers, *rest):
@@ -303,13 +298,8 @@
             for j in range(height):
                 field[0, n, g, height + j] = own[start + n, deep, j, :]
             for j in range(reach):
-                if way == "winds":
-                    at = (2 + n * groups + g) * reach + j
-                    near, distant = pair[at], far[at]
-                else:
-                    near, distant = pair[n, g, j], far[n, g, j]
-                field[0, n, g, pair_at + j] = near
-                field[0, n, g, far_at + j] = distant
+                field[0, n, g, pair_at + j] = pair[n, g, j]
+                field[0, n, g, far_at + j] = far[n, g, j]
             if way == "relay":
                 for j in range(reach, height):
                     field[0, n, g, pair_at + j] = pair[n, g, j]
@@ -400,16 +390,16 @@
     _, levels, height, width = tracers.shape
     half = levels // 2
     wind_other, diffusion_other = exchange(winds, "group", 1), exchange(diffusivity, "group", 1)
-    numbers, tracers, winds, diffusivity, *parts, pair_first, far_first, to_pair, to_far = pack(
+    numbers, tracers, winds, diffusivity, *parts = pack(
         tiles, substeps, loader, tracers, winds, diffusivity
     )
 
+    parts, rows = parts[: len(RELAYED)], parts[len(RELAYED) :]
     pairs = [exchange(part, "tile", 1) for part in parts]
-    halos = []
-    for pair in pairs:
-        shape = (pair.shape[0], pair.shape[1], ROUNDS, *pair.shape[3:])
-        onward = on_core(onward_kernel, numbers, [pair], pltpu.VMEM(shape, jnp.float32))
-        halos.append(("relay", pair.shape[0], (pair, relay(onward, "tile"))))
+    straights = [
+        (exchange(to_pair, "tile", 1), cross(to_far, "tile"))
+        for to_pair, to_far in zip(rows[::2], rows[1::2])
+    ]
 
     met = on_core(
         first_choice_kernel,
@@ -426,37 +416,49 @@
             pltpu.VMEM(met.shape, jnp.float32),
         )
         bit *= 2
-    with_winds = 2 * ROUNDS * (1 + WITH_WINDS)
     wind, wind_pair, wind_far, mix = on_core(
         functools.partial(last_choice_kernel, bit),
         numbers,
-        [met, exchange(met, "group", bit), pair_first, far_first],
+        [met, exchange(met, "group", bit)],
         [
             pltpu.VMEM((2, height, half, width), jnp.float32),
-            pltpu.VMEM((with_winds, half, width), jnp.float32),
-            pltpu.VMEM((with_winds, half, width), jnp.float32),
+            pltpu.VMEM((2, ROUNDS, half, width), jnp.float32),
+            pltpu.VMEM((2, ROUNDS, half, width), jnp.float32),
             pltpu.VMEM((half, height, width), jnp.float32),
         ],
     )
     wind_pair, wind_far = exchange(wind_pair, "tile", 1), cross(wind_far, "tile")
-    halos.append(("winds", WITH_WINDS, (wind_pair, wind_far)))
-    halos.append(("straight", STRAIGHT, (exchange(to_pair, "tile", 1), cross(to_far, "tile"))))
+    halos, start = [], 0
+    for pair in pairs:
+        shape = (pair.shape[0], pair.shape[1], ROUNDS, *pair.shape[3:])
+        onward = on_core(
+            onward_kernel,
+            numbers,
+            [pair],
+            pltpu.VMEM(shape, jnp.float32),
+        )
+        halos.append(("relay", start, (pair, relay(onward, "tile"))))
+        start += pair.shape[0]
+    start = sum(RELAYED)
+    for halo in straights:
+        halos.append(("straight", start, halo))
+        start += halo[0].shape[0]
     known = on_core(
         gather_kernel,
         numbers,
-        [wind, wind_pair, wind_far, mix],
+        [wind, mix, wind_pair, wind_far],
         [pltpu.VMEM((height + 2 * ROUNDS + height // 2, half, width), jnp.float32)] * 2,
     )
     coef, solve = prepare(
         numbers, height, ROUNDS, [*known, *(exchange(x, "group", 1) for x in known)], []
     )
 
-    result, start = None, 0
-    for way, count, halo in halos:
+    result = None
+    for way, start, halo in [halos[k] for k in ORDER]:
+        count = halo[0].shape[0]
         result = window(
             numbers, coef, solve, tracers, emissions, way, start, count, halo, result
         )
-        start += count
     return result
 
 

time: 41.3 us -> 40.6 us (0.983)
  the two profiles are of different devices: /device:TPU:0 before, /device:TPU:8 now
where the time goes in v5:
time: 40.6 us; the launch traced here: 40.4 us
  starting transfers between devices  19.9 us (49%)
  waiting for transfers between devices  11.1 us (27%)
  Pallas kernels  9.27 us (23%)
    ppermute x9, waiting for transfers between devices, exchange(): return lax.ppermute(value, axis, [(i, i ^ bit) for i in range(count)])  11.1 us
    ppermute x3, starting transfers between devices, cross(): return lax.ppermute(value, axis, pairs + [(j, i) for i, j in pairs])  9.68 us
    pallas_call x3, Pallas kernels, window(): pl.pallas_call(functools.partial(window_kernel, way, start, count, last),...  6.81 us
    ppermute x9, starting transfers between devices, exchange(): return lax.ppermute(value, axis, [(i, i ^ bit) for i in range(count)])  6.69 us
    ppermute x1, starting transfers between devices, relay(): return lax.ppermute(value, axis, pairs)  3.48 us
    pallas_call x1, Pallas kernels, pack(): pl.pallas_call(functools.partial(pack_kernel, RELAYED, tiles), out_shape=...  1.84 us
  transfers between devices with their start and end apart: 13, of which 4 were waited for; matrix products, arithmetic and copies ran while one was open for 0% of the time, Pallas kernels for 15%

profile of v5, /device:TPU:8, one launch (start us, length us, event | category | flops | bytes accessed | tf_op | source)
XLA Modules:
  0.0 40.4 jit_solution(10251154428848350373)
XLA Ops:
  0.0 1.8 %shard_map.64 = (s32[4]{0:T(128)S(4)}, f32[8,16,8,256]{3,2,1,0:T(8,128)S(1)}, f32[1,2,16,8,256]{4,3,2,1,0:T(8,128)S(1)}, f32[1,15,8,256]{3,2,1,0:T(8,128)S(1)}, ...) custom-call(s32[8]{0:T(128)} %substeps_in.1, ...), custom_call_target="tpu_custom_call" | custom-call | bytes 1048576 | tf_op jit(solution)/shard_map/pallas_call | solution.py:155
  1.8 1.6 %collective-permute-start.11 = (f32[4,2,8,8,256]{4,3,2,1,0:T(8,128)S(1)}, f32[4,2,8,8,256]{4,3,2,1,0:T(8,128)S(1)}, u32[]{:S(2)}, u32[]{:S(2)}) collective-permute-start(f32[4,2,8,8,256]{4,3,2,1,0:T(8,128)S(1)} %get-tuple-element.38), channel_id=1, source_target_pairs={{0,4},{4,0},{8,12},{12,8},{16,20},{20,16},{24,28},{28,24},{1,5},{5... | collective-permute-start | bytes 1572872 | tf_op jit(solution)/shard_map/ppermute | solution.py:23
  3.4 0.0 collective-permute-start
  3.4 0.5 %collective-permute-start.1 = (f32[1,15,8,256]{3,2,1,0:T(8,128)}, f32[1,15,8,256]{3,2,1,0:T(8,128)S(1)}, u32[]{:S(2)}, u32[]{:S(2)}) collective-permute-start(f32[1,15,8,256]{3,2,1,0:T(8,128)} %diffusion_in.1), channel_id=1, source_target_pairs={{0,1},{1,0},{2,3},{3,2},{4,5},{5,4},{6,7},{7,6},{8,9},{9,8},{10,11... | collective-permute-start | bytes 368648 | tf_op jit(solution)/shard_map/ppermute | solution.py:23
  3.9 1.4 %collective-permute-done.1.diffusion_other = f32[1,15,8,256]{3,2,1,0:T(8,128)S(1)} collective-permute-done((f32[1,15,8,256]{3,2,1,0:T(8,128)}, f32[1,15,8,256]{3,2,1,0:T(8,128)S(1)}, u32[]{:S(2)}, u32[]{:S(2)}) %collective-permute-start.1) | collective-permute-done | bytes 122912 | tf_op jit(solution)/shard_map/ppermute | solution.py:23
  5.4 0.0 collective-permute-done.wind_other
  5.4 1.6 %collective-permute-start.2 = (f32[3,8,8,256]{3,2,1,0:T(8,128)S(1)}, f32[3,8,8,256]{3,2,1,0:T(8,128)S(1)}, u32[]{:S(2)}, u32[]{:S(2)}) collective-permute-start(f32[3,8,8,256]{3,2,1,0:T(8,128)S(1)} %shard_map.65.met), channel_id=1, source_target_pairs={{0,2},{1,3},{2,0},{3,1},{4,6},{5,7},{6,4},{7,5},{8,10},{9,11},{10,... | collective-permute-start | bytes 589832 | tf_op jit(solution)/shard_map/ppermute | solution.py:23
  6.9 5.5 %collective-permute-done.2.other = f32[3,8,8,256]{3,2,1,0:T(8,128)S(1)} collective-permute-done((f32[3,8,8,256]{3,2,1,0:T(8,128)S(1)}, f32[3,8,8,256]{3,2,1,0:T(8,128)S(1)}, u32[]{:S(2)}, u32[]{:S(2)}) %collective-permute-start.2) | collective-permute-done | bytes 196640 | tf_op jit(solution)/shard_map/ppermute | solution.py:23
  12.4 0.2 shard_map.66
  12.6 0.6 %collective-permute-start.3 = (f32[2,6,8,256]{3,2,1,0:T(8,128)S(1)}, f32[2,6,8,256]{3,2,1,0:T(8,128)S(1)}, u32[]{:S(2)}, u32[]{:S(2)}) collective-permute-start(f32[2,6,8,256]{3,2,1,0:T(8,128)S(1)} %get-tuple-element.27), channel_id=1, source_target_pairs={{0,4},{4,0},{8,12},{12,8},{16,20},{20,16},{24,28},{28,24},{1,5},{5... | collective-permute-start | bytes 294920 | tf_op jit(solution)/shard_map/ppermute | solution.py:23
  13.1 3.3 %collective-permute-start.4 = (f32[2,6,8,256]{3,2,1,0:T(8,128)S(1)}, f32[2,6,8,256]{3,2,1,0:T(8,128)S(1)}, u32[]{:S(2)}, u32[]{:S(2)}) collective-permute-start(f32[2,6,8,256]{3,2,1,0:T(8,128)S(1)} %get-tuple-element.28), channel_id=1, source_target_pairs={{4,8},{12,16},{20,24},{8,4},{16,12},{24,20},{5,9},{13,17},{21,25},... | collective-permute-start | bytes 294920 | tf_op jit(solution)/shard_map/ppermute | solution.py:29
  16.4 0.1 collective-permute-done.11.pair.rest_0_
  16.6 3.5 %collective-permute-start.12 = (f32[4,2,6,8,256]{4,3,2,1,0:T(8,128)S(1)}, f32[4,2,6,8,256]{4,3,2,1,0:T(8,128)S(1)}, u32[]{:S(2)}, u32[]{:S(2)}) collective-permute-start(f32[4,2,6,8,256]{4,3,2,1,0:T(8,128)S(1)} %shard_map.69), channel_id=1, source_target_pairs={{0,8},{8,16},{16,24},{12,4},{20,12},{28,20},{1,9},{9,17},{17,25},{... | collective-permute-start | bytes 1179656 | tf_op jit(solution)/shard_map/ppermute | solution.py:35
  20.1 0.5 %collective-permute-start.9 = (f32[3,2,6,8,256]{4,3,2,1,0:T(8,128)S(1)}, f32[3,2,6,8,256]{4,3,2,1,0:T(8,128)S(1)}, u32[]{:S(2)}, u32[]{:S(2)}) collective-permute-start(f32[3,2,6,8,256]{4,3,2,1,0:T(8,128)S(1)} %get-tuple-element.36), channel_id=1, source_target_pairs={{0,4},{4,0},{8,12},{12,8},{16,20},{20,16},{24,28},{28,24},{1,5},{5... | collective-permute-start | bytes 884744 | tf_op jit(solution)/shard_map/ppermute | solution.py:23
  20.6 0.0 collective-permute-done.3.pair
  20.6 0.0 collective-permute-done.4.far
  20.7 0.1 collective-permute-start.5
  20.7 3.4 %collective-permute-start.10 = (f32[3,2,6,8,256]{4,3,2,1,0:T(8,128)S(1)}, f32[3,2,6,8,256]{4,3,2,1,0:T(8,128)S(1)}, u32[]{:S(2)}, u32[]{:S(2)}) collective-permute-start(f32[3,2,6,8,256]{4,3,2,1,0:T(8,128)S(1)} %get-tuple-element.37), channel_id=1, source_target_pairs={{4,8},{12,16},{20,24},{8,4},{16,12},{24,20},{5,9},{13,17},{21,25},... | collective-permute-start | bytes 884744 | tf_op jit(solution)/shard_map/ppermute | solution.py:29
  24.1 0.3 collective-permute-start.6
  24.4 0.0 collective-permute-done.5.rest_2_
  24.4 1.6 %collective-permute-start.7 = (f32[1,2,6,8,256]{4,3,2,1,0:T(8,128)S(1)}, f32[1,2,6,8,256]{4,3,2,1,0:T(8,128)S(1)}, u32[]{:S(2)}, u32[]{:S(2)}) collective-permute-start(f32[1,2,6,8,256]{4,3,2,1,0:T(8,128)S(1)} %get-tuple-element.34), channel_id=1, source_target_pairs={{0,4},{4,0},{8,12},{12,8},{16,20},{20,16},{24,28},{28,24},{1,5},{5... | collective-permute-start | bytes 294920 | tf_op jit(solution)/shard_map/ppermute | solution.py:23
  26.0 0.0 collective-permute-done.6.rest_3_
  26.0 3.0 %collective-permute-start.8 = (f32[1,2,6,8,256]{4,3,2,1,0:T(8,128)S(1)}, f32[1,2,6,8,256]{4,3,2,1,0:T(8,128)S(1)}, u32[]{:S(2)}, u32[]{:S(2)}) collective-permute-start(f32[1,2,6,8,256]{4,3,2,1,0:T(8,128)S(1)} %get-tuple-element.35), channel_id=1, source_target_pairs={{4,8},{12,16},{20,24},{8,4},{16,12},{24,20},{5,9},{13,17},{21,25},... | collective-permute-start | bytes 294920 | tf_op jit(solution)/shard_map/ppermute | solution.py:29
  29.0 0.4 shard_map.68
  29.4 0.0 collective-permute-done.12.rest_1_
  29.4 3.0 %shard_map.70.rest_2_ = f32[8,16,8,256]{3,2,1,0:T(8,128)S(1)} custom-call(s32[4]{0:T(128)S(4)} %get-tuple-element.22.numbers._, f32[3,24,5,8,256]{4,3,2,1,0:T(8,128)S(1)} %get-tuple-element.31.coef, f32[16,3,8,256]{3,2,1,0:T(8,128)S(1)} %get-tuple-element.32.solve, f32[8,16,8,256]{3,2,1,0:T(8,128)S(1)} %get-tuple-element.33.own, f32[8,8,256]{2,1,0:T(8,128)S(1)} %copy-done, ...), custom_call_target="tpu_custom_call" | custom-call | bytes 1048576 | tf_op jit(solution)/shard_map/pallas_call | solution.py:372
  32.4 4.2 %collective-permute-done.9.rest_0_ = f32[3,2,6,8,256]{4,3,2,1,0:T(8,128)S(1)} collective-permute-done((f32[3,2,6,8,256]{4,3,2,1,0:T(8,128)S(1)}, f32[3,2,6,8,256]{4,3,2,1,0:T(8,128)S(1)}, u32[]{:S(2)}, u32[]{:S(2)}) %collective-permute-start.9) | collective-permute-done | bytes 294944 | tf_op jit(solution)/shard_map/ppermute | solution.py:23
  36.6 0.0 collective-permute-done.10.rest_1_
  36.6 2.3 %shard_map.71.rest_2_ = f32[8,16,8,256]{3,2,1,0:T(8,128)S(1)} custom-call(s32[4]{0:T(128)S(4)} %get-tuple-element.22.numbers._, f32[3,24,5,8,256]{4,3,2,1,0:T(8,128)S(1)} %get-tuple-element.31.coef, f32[16,3,8,256]{3,2,1,0:T(8,128)S(1)} %get-tuple-element.32.solve, f32[8,16,8,256]{3,2,1,0:T(8,128)S(1)} %get-tuple-element.33.own, ...), custom_call_target="tpu_custom_call", output_to_operand_aliasing={{}: (7, {})} | custom-call | bytes 1048576 | tf_op jit(solution)/shard_map/pallas_call | solution.py:372
  38.8 0.0 collective-permute-done.7.rest_0_
  38.8 0.0 collective-permute-done.8.rest_1_
  38.8 1.5 %shard_map.72 = f32[8,16,8,256]{3,2,1,0:T(8,128)} custom-call(s32[4]{0:T(128)S(4)} %get-tuple-element.22.numbers._, f32[3,24,5,8,256]{4,3,2,1,0:T(8,128)S(1)} %get-tuple-element.31.coef, f32[16,3,8,256]{3,2,1,0:T(8,128)S(1)} %get-tuple-element.32.solve, f32[8,16,8,256]{3,2,1,0:T(8,128)S(1)} %get-tuple-element.33.own, f32[8,8,256]{2,1,0:T(8,128)S(1)} %copy-done, ...), custom_call_target="tpu_custom_call" | custom-call | bytes 1048576 | tf_op jit(solution)/shard_map/pallas_call | solution.py:372
  (5 shorter events, 0.1 us)
Async XLA Ops:
  0.0 29.4 %copy-start = (f32[8,8,256]{2,1,0:T(8,128)S(1)}, f32[8,8,256]{2,1,0:T(8,128)}, u32[]{:S(2)}) copy-start(f32[8,8,256]{2,1,0:T(8,128)} %source.5) | copy-start | bytes 196612
  1.8 14.7 %collective-permute-start.11 = (f32[4,2,8,8,256]{4,3,2,1,0:T(8,128)S(1)}, f32[4,2,8,8,256]{4,3,2,1,0:T(8,128)S(1)}, u32[]{:S(2)}, u32[]{:S(2)}) collective-permute-start(f32[4,2,8,8,256]{4,3,2,1,0:T(8,128)S(1)} %get-tuple-element.38), channel_id=1, source_target_pairs={{0,4},{4,0},{8,12},{12,8},{16,20},{20,16},{24,28},{28,24},{1,5},{5... | collective-permute-start | bytes 1572872 | tf_op jit(solution)/shard_map/ppermute | solution.py:23
  3.4 1.9 %collective-permute-start = (f32[1,2,16,8,256]{4,3,2,1,0:T(8,128)}, f32[1,2,16,8,256]{4,3,2,1,0:T(8,128)S(1)}, u32[]{:S(2)}, u32[]{:S(2)}) collective-permute-start(f32[1,2,16,8,256]{4,3,2,1,0:T(8,128)} %wind_in.1), channel_id=1, source_target_pairs={{0,1},{1,0},{2,3},{3,2},{4,5},{5,4},{6,7},{7,6},{8,9},{9,8},{10,11... | collective-permute-start | bytes 786440 | tf_op jit(solution)/shard_map/ppermute | solution.py:23
  3.4 1.9 %collective-permute-start.1 = (f32[1,15,8,256]{3,2,1,0:T(8,128)}, f32[1,15,8,256]{3,2,1,0:T(8,128)S(1)}, u32[]{:S(2)}, u32[]{:S(2)}) collective-permute-start(f32[1,15,8,256]{3,2,1,0:T(8,128)} %diffusion_in.1), channel_id=1, source_target_pairs={{0,1},{1,0},{2,3},{3,2},{4,5},{5,4},{6,7},{7,6},{8,9},{9,8},{10,11... | collective-permute-start | bytes 368648 | tf_op jit(solution)/shard_map/ppermute | solution.py:23
  5.4 7.0 %collective-permute-start.2 = (f32[3,8,8,256]{3,2,1,0:T(8,128)S(1)}, f32[3,8,8,256]{3,2,1,0:T(8,128)S(1)}, u32[]{:S(2)}, u32[]{:S(2)}) collective-permute-start(f32[3,8,8,256]{3,2,1,0:T(8,128)S(1)} %shard_map.65.met), channel_id=1, source_target_pairs={{0,2},{1,3},{2,0},{3,1},{4,6},{5,7},{6,4},{7,5},{8,10},{9,11},{10,... | collective-permute-start | bytes 589832 | tf_op jit(solution)/shard_map/ppermute | solution.py:23
  12.6 8.0 %collective-permute-start.3 = (f32[2,6,8,256]{3,2,1,0:T(8,128)S(1)}, f32[2,6,8,256]{3,2,1,0:T(8,128)S(1)}, u32[]{:S(2)}, u32[]{:S(2)}) collective-permute-start(f32[2,6,8,256]{3,2,1,0:T(8,128)S(1)} %get-tuple-element.27), channel_id=1, source_target_pairs={{0,4},{4,0},{8,12},{12,8},{16,20},{20,16},{24,28},{28,24},{1,5},{5... | collective-permute-start | bytes 294920 | tf_op jit(solution)/shard_map/ppermute | solution.py:23
  13.1 7.5 %collective-permute-start.4 = (f32[2,6,8,256]{3,2,1,0:T(8,128)S(1)}, f32[2,6,8,256]{3,2,1,0:T(8,128)S(1)}, u32[]{:S(2)}, u32[]{:S(2)}) collective-permute-start(f32[2,6,8,256]{3,2,1,0:T(8,128)S(1)} %get-tuple-element.28), channel_id=1, source_target_pairs={{4,8},{12,16},{20,24},{8,4},{16,12},{24,20},{5,9},{13,17},{21,25},... | collective-permute-start | bytes 294920 | tf_op jit(solution)/shard_map/ppermute | solution.py:29
  16.6 12.8 %collective-permute-start.12 = (f32[4,2,6,8,256]{4,3,2,1,0:T(8,128)S(1)}, f32[4,2,6,8,256]{4,3,2,1,0:T(8,128)S(1)}, u32[]{:S(2)}, u32[]{:S(2)}) collective-permute-start(f32[4,2,6,8,256]{4,3,2,1,0:T(8,128)S(1)} %shard_map.69), channel_id=1, source_target_pairs={{0,8},{8,16},{16,24},{12,4},{20,12},{28,20},{1,9},{9,17},{17,25},{... | collective-permute-start | bytes 1179656 | tf_op jit(solution)/shard_map/ppermute | solution.py:35
  20.1 16.5 %collective-permute-start.9 = (f32[3,2,6,8,256]{4,3,2,1,0:T(8,128)S(1)}, f32[3,2,6,8,256]{4,3,2,1,0:T(8,128)S(1)}, u32[]{:S(2)}, u32[]{:S(2)}) collective-permute-start(f32[3,2,6,8,256]{4,3,2,1,0:T(8,128)S(1)} %get-tuple-element.36), channel_id=1, source_target_pairs={{0,4},{4,0},{8,12},{12,8},{16,20},{20,16},{24,28},{28,24},{1,5},{5... | collective-permute-start | bytes 884744 | tf_op jit(solution)/shard_map/ppermute | solution.py:23
  20.7 3.7 %collective-permute-start.5 = (f32[24,8,256]{2,1,0:T(8,128)S(1)}, f32[24,8,256]{2,1,0:T(8,128)S(1)}, u32[]{:S(2)}, u32[]{:S(2)}) collective-permute-start(f32[24,8,256]{2,1,0:T(8,128)S(1)} %get-tuple-element.29.rest_0_), channel_id=1, source_target_pairs={{0,1},{1,0},{2,3},{3,2},{4,5},{5,4},{6,7},{7,6},{8,9},{9,8},{10,11... | collective-permute-start | bytes 589832 | tf_op jit(solution)/shard_map/ppermute | solution.py:23
  20.7 15.8 %collective-permute-start.10 = (f32[3,2,6,8,256]{4,3,2,1,0:T(8,128)S(1)}, f32[3,2,6,8,256]{4,3,2,1,0:T(8,128)S(1)}, u32[]{:S(2)}, u32[]{:S(2)}) collective-permute-start(f32[3,2,6,8,256]{4,3,2,1,0:T(8,128)S(1)} %get-tuple-element.37), channel_id=1, source_target_pairs={{4,8},{12,16},{20,24},{8,4},{16,12},{24,20},{5,9},{13,17},{21,25},... | collective-permute-start | bytes 884744 | tf_op jit(solution)/shard_map/ppermute | solution.py:29
  24.1 1.9 %collective-permute-start.6 = (f32[24,8,256]{2,1,0:T(8,128)S(1)}, f32[24,8,256]{2,1,0:T(8,128)S(1)}, u32[]{:S(2)}, u32[]{:S(2)}) collective-permute-start(f32[24,8,256]{2,1,0:T(8,128)S(1)} %get-tuple-element.30.rest_1_), channel_id=1, source_target_pairs={{0,1},{1,0},{2,3},{3,2},{4,5},{5,4},{6,7},{7,6},{8,9},{9,8},{10,11... | collective-permute-start | bytes 589832 | tf_op jit(solution)/shard_map/ppermute | solution.py:23
  24.4 14.5 %collective-permute-start.7 = (f32[1,2,6,8,256]{4,3,2,1,0:T(8,128)S(1)}, f32[1,2,6,8,256]{4,3,2,1,0:T(8,128)S(1)}, u32[]{:S(2)}, u32[]{:S(2)}) collective-permute-start(f32[1,2,6,8,256]{4,3,2,1,0:T(8,128)S(1)} %get-tuple-element.34), channel_id=1, source_target_pairs={{0,4},{4,0},{8,12},{12,8},{16,20},{20,16},{24,28},{28,24},{1,5},{5... | collective-permute-start | bytes 294920 | tf_op jit(solution)/shard_map/ppermute | solution.py:23
  26.0 12.9 %collective-permute-start.8 = (f32[1,2,6,8,256]{4,3,2,1,0:T(8,128)S(1)}, f32[1,2,6,8,256]{4,3,2,1,0:T(8,128)S(1)}, u32[]{:S(2)}, u32[]{:S(2)}) collective-permute-start(f32[1,2,6,8,256]{4,3,2,1,0:T(8,128)S(1)} %get-tuple-element.35), channel_id=1, source_target_pairs={{4,8},{12,16},{20,24},{8,4},{16,12},{24,20},{5,9},{13,17},{21,25},... | collective-permute-start | bytes 294920 | tf_op jit(solution)/shard_map/ppermute | solution.py:29

commit v6 on v5

--- a/solution.py
+++ b/solution.py
@@ -92,17 +92,16 @@
 
 def pack_kernel(relayed, tiles, substeps_in, loader_in, tracers_in, wind_in, diffusion_in, *rest):
     numbers, tracers, wind, diffusion, *outs, substeps, loader, sem = rest
+    sources = [(tracers_in.at[n], tracers.at[n]) for n in range(tracers.shape[0])]
+    sources += [
+        (substeps_in, substeps),
+        (loader_in, loader),
+        (wind_in, wind),
+        (diffusion_in, diffusion),
+    ]
     copies = [
         pltpu.make_async_copy(source, target, sem.at[i])
-        for i, (source, target) in enumerate(
-            (
-                (substeps_in, substeps),
-                (loader_in, loader),
-                (tracers_in, tracers),
-                (wind_in, wind),
-                (diffusion_in, diffusion),
-            )
-        )
+        for i, (source, target) in enumerate(sources)
     ]
     for copy in copies:
         copy.start()
@@ -111,31 +110,31 @@
     _, levels, height, _ = tracers.shape
     straight = list(zip(outs[len(relayed) :: 2], outs[len(relayed) + 1 :: 2]))
     reach = outs[-1].shape[2]
-    copies[2].wait()
-    for g in range(levels // DEEP):
-        deep = slice(g * DEEP, (g + 1) * DEEP)
-        start = 0
-        for part, count in zip(outs, relayed):
-            for n in range(count):
+    start = 0
+    for part, count in zip(outs, relayed):
+        for n in range(count):
+            copies[start + n].wait()
+            for g in range(levels // DEEP):
                 for j in range(height):
-                    part[n, g, j] = tracers[start + n, deep, j, :]
-            start += count
-        for to_pair, to_far in straight:
-            for n in range(to_pair.shape[0]):
+                    part[n, g, j] = tracers[start + n, g * DEEP : (g + 1) * DEEP, j, :]
+        start += count
+    for to_pair, to_far in straight:
+        for n in range(to_pair.shape[0]):
+            copies[start + n].wait()
+            for g in range(levels // DEEP):
+                deep = slice(g * DEEP, (g + 1) * DEEP)
                 rows = [tracers[start + n, deep, j, :] for j in range(height)]
                 for j in range(reach):
                     last, first = rows[height - reach + j], rows[j]
                     to_pair[n, g, j] = jnp.where(even, last, first)
                     to_far[n, g, j] = jnp.where(even, first, last)
-            start += to_pair.shape[0]
-    copies[0].wait()
-    copies[1].wait()
+        start += to_pair.shape[0]
+    for copy in copies[start:]:
+        copy.wait()
     numbers[0] = loader[tile]
     numbers[1] = substeps[jnp.maximum(tile - 1, 0)]
     numbers[2] = substeps[tile]
     numbers[3] = substeps[jnp.minimum(tile + 1, tiles - 1)]
-    copies[3].wait()
-    copies[4].wait()
 
 
 def pack(tiles, substeps, loader, tracers, winds, diffusivity):
@@ -160,7 +159,7 @@
         scratch_shapes=[
             pltpu.SMEM(substeps.shape, jnp.int32),
             pltpu.SMEM(loader.shape, jnp.int32),
-            pltpu.SemaphoreType.DMA((5,)),
+            pltpu.SemaphoreType.DMA((tracers.shape[0] + 4,)),
         ],
         compiler_params=pltpu.CompilerParams(vmem_limit_bytes=VMEM_LIMIT),
         cost_estimate=pl.CostEstimate(flops=0, bytes_accessed=MIB, transcendentals=0),

time: 40.6 us -> 40.4 us (level)
  no operation moved by 1% of the time
where the time goes in v6:
time: 40.4 us; the launch traced here: 40.2 us
  starting transfers between devices  19.9 us (49%)
  waiting for transfers between devices  11.1 us (27%)
  Pallas kernels  9.12 us (23%)
    ppermute x9, waiting for transfers between devices, exchange(): return lax.ppermute(value, axis, [(i, i ^ bit) for i in range(count)])  11.1 us
    ppermute x3, starting transfers between devices, cross(): return lax.ppermute(value, axis, pairs + [(j, i) for i, j in pairs])  9.68 us
    pallas_call x3, Pallas kernels, window(): pl.pallas_call(functools.partial(window_kernel, way, start, count, last),...  6.81 us
    ppermute x9, starting transfers between devices, exchange(): return lax.ppermute(value, axis, [(i, i ^ bit) for i in range(count)])  6.69 us
    ppermute x1, starting transfers between devices, relay(): return lax.ppermute(value, axis, pairs)  3.48 us
    pallas_call x1, Pallas kernels, pack(): pl.pallas_call(functools.partial(pack_kernel, RELAYED, tiles), out_shape=...  1.69 us
  transfers between devices with their start and end apart: 13, of which 4 were waited for; matrix products, arithmetic and copies ran while one was open for 0% of the time, Pallas kernels for 15%

profile of v6, /device:TPU:8, one launch (start us, length us, event | category | flops | bytes accessed | tf_op | source)
XLA Modules:
  0.0 40.2 jit_solution(4786148801640519660)
XLA Ops:
  0.0 1.7 %shard_map.64 = (s32[4]{0:T(128)S(4)}, f32[8,16,8,256]{3,2,1,0:T(8,128)S(1)}, f32[1,2,16,8,256]{4,3,2,1,0:T(8,128)S(1)}, f32[1,15,8,256]{3,2,1,0:T(8,128)S(1)}, ...) custom-call(s32[8]{0:T(128)} %substeps_in.1, ...), custom_call_target="tpu_custom_call" | custom-call | bytes 1048576 | tf_op jit(solution)/shard_map/pallas_call | solution.py:154
  1.7 1.6 %collective-permute-start.11 = (f32[4,2,8,8,256]{4,3,2,1,0:T(8,128)S(1)}, f32[4,2,8,8,256]{4,3,2,1,0:T(8,128)S(1)}, u32[]{:S(2)}, u32[]{:S(2)}) collective-permute-start(f32[4,2,8,8,256]{4,3,2,1,0:T(8,128)S(1)} %get-tuple-element.38), channel_id=1, source_target_pairs={{0,4},{4,0},{8,12},{12,8},{16,20},{20,16},{24,28},{28,24},{1,5},{5... | collective-permute-start | bytes 1572872 | tf_op jit(solution)/shard_map/ppermute | solution.py:23
  3.3 0.0 collective-permute-start
  3.3 0.5 %collective-permute-start.1 = (f32[1,15,8,256]{3,2,1,0:T(8,128)}, f32[1,15,8,256]{3,2,1,0:T(8,128)S(1)}, u32[]{:S(2)}, u32[]{:S(2)}) collective-permute-start(f32[1,15,8,256]{3,2,1,0:T(8,128)} %diffusion_in.1), channel_id=1, source_target_pairs={{0,1},{1,0},{2,3},{3,2},{4,5},{5,4},{6,7},{7,6},{8,9},{9,8},{10,11... | collective-permute-start | bytes 368648 | tf_op jit(solution)/shard_map/ppermute | solution.py:23
  3.8 1.4 %collective-permute-done.1.diffusion_other = f32[1,15,8,256]{3,2,1,0:T(8,128)S(1)} collective-permute-done((f32[1,15,8,256]{3,2,1,0:T(8,128)}, f32[1,15,8,256]{3,2,1,0:T(8,128)S(1)}, u32[]{:S(2)}, u32[]{:S(2)}) %collective-permute-start.1) | collective-permute-done | bytes 122912 | tf_op jit(solution)/shard_map/ppermute | solution.py:23
  5.2 0.0 collective-permute-done.wind_other
  5.2 1.6 %collective-permute-start.2 = (f32[3,8,8,256]{3,2,1,0:T(8,128)S(1)}, f32[3,8,8,256]{3,2,1,0:T(8,128)S(1)}, u32[]{:S(2)}, u32[]{:S(2)}) collective-permute-start(f32[3,8,8,256]{3,2,1,0:T(8,128)S(1)} %shard_map.65.met), channel_id=1, source_target_pairs={{0,2},{1,3},{2,0},{3,1},{4,6},{5,7},{6,4},{7,5},{8,10},{9,11},{10,... | collective-permute-start | bytes 589832 | tf_op jit(solution)/shard_map/ppermute | solution.py:23
  6.8 5.5 %collective-permute-done.2.other = f32[3,8,8,256]{3,2,1,0:T(8,128)S(1)} collective-permute-done((f32[3,8,8,256]{3,2,1,0:T(8,128)S(1)}, f32[3,8,8,256]{3,2,1,0:T(8,128)S(1)}, u32[]{:S(2)}, u32[]{:S(2)}) %collective-permute-start.2) | collective-permute-done | bytes 196640 | tf_op jit(solution)/shard_map/ppermute | solution.py:23
  12.2 0.2 shard_map.66
  12.4 0.6 %collective-permute-start.3 = (f32[2,6,8,256]{3,2,1,0:T(8,128)S(1)}, f32[2,6,8,256]{3,2,1,0:T(8,128)S(1)}, u32[]{:S(2)}, u32[]{:S(2)}) collective-permute-start(f32[2,6,8,256]{3,2,1,0:T(8,128)S(1)} %get-tuple-element.27), channel_id=1, source_target_pairs={{0,4},{4,0},{8,12},{12,8},{16,20},{20,16},{24,28},{28,24},{1,5},{5... | collective-permute-start | bytes 294920 | tf_op jit(solution)/shard_map/ppermute | solution.py:23
  13.0 3.3 %collective-permute-start.4 = (f32[2,6,8,256]{3,2,1,0:T(8,128)S(1)}, f32[2,6,8,256]{3,2,1,0:T(8,128)S(1)}, u32[]{:S(2)}, u32[]{:S(2)}) collective-permute-start(f32[2,6,8,256]{3,2,1,0:T(8,128)S(1)} %get-tuple-element.28), channel_id=1, source_target_pairs={{4,8},{12,16},{20,24},{8,4},{16,12},{24,20},{5,9},{13,17},{21,25},... | collective-permute-start | bytes 294920 | tf_op jit(solution)/shard_map/ppermute | solution.py:29
  16.3 0.1 collective-permute-done.11.pair.rest_0_
  16.4 3.5 %collective-permute-start.12 = (f32[4,2,6,8,256]{4,3,2,1,0:T(8,128)S(1)}, f32[4,2,6,8,256]{4,3,2,1,0:T(8,128)S(1)}, u32[]{:S(2)}, u32[]{:S(2)}) collective-permute-start(f32[4,2,6,8,256]{4,3,2,1,0:T(8,128)S(1)} %shard_map.69), channel_id=1, source_target_pairs={{0,8},{8,16},{16,24},{12,4},{20,12},{28,20},{1,9},{9,17},{17,25},{... | collective-permute-start | bytes 1179656 | tf_op jit(solution)/shard_map/ppermute | solution.py:35
  19.9 0.5 %collective-permute-start.9 = (f32[3,2,6,8,256]{4,3,2,1,0:T(8,128)S(1)}, f32[3,2,6,8,256]{4,3,2,1,0:T(8,128)S(1)}, u32[]{:S(2)}, u32[]{:S(2)}) collective-permute-start(f32[3,2,6,8,256]{4,3,2,1,0:T(8,128)S(1)} %get-tuple-element.36), channel_id=1, source_target_pairs={{0,4},{4,0},{8,12},{12,8},{16,20},{20,16},{24,28},{28,24},{1,5},{5... | collective-permute-start | bytes 884744 | tf_op jit(solution)/shard_map/ppermute | solution.py:23
  20.5 0.0 collective-permute-done.3.pair
  20.5 0.0 collective-permute-done.4.far
  20.5 0.1 collective-permute-start.5
  20.6 3.4 %collective-permute-start.10 = (f32[3,2,6,8,256]{4,3,2,1,0:T(8,128)S(1)}, f32[3,2,6,8,256]{4,3,2,1,0:T(8,128)S(1)}, u32[]{:S(2)}, u32[]{:S(2)}) collective-permute-start(f32[3,2,6,8,256]{4,3,2,1,0:T(8,128)S(1)} %get-tuple-element.37), channel_id=1, source_target_pairs={{4,8},{12,16},{20,24},{8,4},{16,12},{24,20},{5,9},{13,17},{21,25},... | collective-permute-start | bytes 884744 | tf_op jit(solution)/shard_map/ppermute | solution.py:29
  24.0 0.3 collective-permute-start.6
  24.2 0.0 collective-permute-done.5.rest_2_
  24.2 1.6 %collective-permute-start.7 = (f32[1,2,6,8,256]{4,3,2,1,0:T(8,128)S(1)}, f32[1,2,6,8,256]{4,3,2,1,0:T(8,128)S(1)}, u32[]{:S(2)}, u32[]{:S(2)}) collective-permute-start(f32[1,2,6,8,256]{4,3,2,1,0:T(8,128)S(1)} %get-tuple-element.34), channel_id=1, source_target_pairs={{0,4},{4,0},{8,12},{12,8},{16,20},{20,16},{24,28},{28,24},{1,5},{5... | collective-permute-start | bytes 294920 | tf_op jit(solution)/shard_map/ppermute | solution.py:23
  25.8 0.0 collective-permute-done.6.rest_3_
  25.8 3.0 %collective-permute-start.8 = (f32[1,2,6,8,256]{4,3,2,1,0:T(8,128)S(1)}, f32[1,2,6,8,256]{4,3,2,1,0:T(8,128)S(1)}, u32[]{:S(2)}, u32[]{:S(2)}) collective-permute-start(f32[1,2,6,8,256]{4,3,2,1,0:T(8,128)S(1)} %get-tuple-element.35), channel_id=1, source_target_pairs={{4,8},{12,16},{20,24},{8,4},{16,12},{24,20},{5,9},{13,17},{21,25},... | collective-permute-start | bytes 294920 | tf_op jit(solution)/shard_map/ppermute | solution.py:29
  28.8 0.4 shard_map.68
  29.2 0.0 collective-permute-done.12.rest_1_
  29.2 3.0 %shard_map.70.rest_2_ = f32[8,16,8,256]{3,2,1,0:T(8,128)S(1)} custom-call(s32[4]{0:T(128)S(4)} %get-tuple-element.22.numbers._, f32[3,24,5,8,256]{4,3,2,1,0:T(8,128)S(1)} %get-tuple-element.31.coef, f32[16,3,8,256]{3,2,1,0:T(8,128)S(1)} %get-tuple-element.32.solve, f32[8,16,8,256]{3,2,1,0:T(8,128)S(1)} %get-tuple-element.33.own, f32[8,8,256]{2,1,0:T(8,128)S(1)} %copy-done, ...), custom_call_target="tpu_custom_call" | custom-call | bytes 1048576 | tf_op jit(solution)/shard_map/pallas_call | solution.py:371
  32.2 4.2 %collective-permute-done.9.rest_0_ = f32[3,2,6,8,256]{4,3,2,1,0:T(8,128)S(1)} collective-permute-done((f32[3,2,6,8,256]{4,3,2,1,0:T(8,128)S(1)}, f32[3,2,6,8,256]{4,3,2,1,0:T(8,128)S(1)}, u32[]{:S(2)}, u32[]{:S(2)}) %collective-permute-start.9) | collective-permute-done | bytes 294944 | tf_op jit(solution)/shard_map/ppermute | solution.py:23
  36.4 0.0 collective-permute-done.10.rest_1_
  36.4 2.3 %shard_map.71.rest_2_ = f32[8,16,8,256]{3,2,1,0:T(8,128)S(1)} custom-call(s32[4]{0:T(128)S(4)} %get-tuple-element.22.numbers._, f32[3,24,5,8,256]{4,3,2,1,0:T(8,128)S(1)} %get-tuple-element.31.coef, f32[16,3,8,256]{3,2,1,0:T(8,128)S(1)} %get-tuple-element.32.solve, f32[8,16,8,256]{3,2,1,0:T(8,128)S(1)} %get-tuple-element.33.own, ...), custom_call_target="tpu_custom_call", output_to_operand_aliasing={{}: (7, {})} | custom-call | bytes 1048576 | tf_op jit(solution)/shard_map/pallas_call | solution.py:371
  38.7 0.0 collective-permute-done.7.rest_0_
  38.7 0.0 collective-permute-done.8.rest_1_
  38.7 1.5 %shard_map.72 = f32[8,16,8,256]{3,2,1,0:T(8,128)} custom-call(s32[4]{0:T(128)S(4)} %get-tuple-element.22.numbers._, f32[3,24,5,8,256]{4,3,2,1,0:T(8,128)S(1)} %get-tuple-element.31.coef, f32[16,3,8,256]{3,2,1,0:T(8,128)S(1)} %get-tuple-element.32.solve, f32[8,16,8,256]{3,2,1,0:T(8,128)S(1)} %get-tuple-element.33.own, f32[8,8,256]{2,1,0:T(8,128)S(1)} %copy-done, ...), custom_call_target="tpu_custom_call" | custom-call | bytes 1048576 | tf_op jit(solution)/shard_map/pallas_call | solution.py:371
  (5 shorter events, 0.1 us)
Async XLA Ops:
  0.0 29.2 %copy-start = (f32[8,8,256]{2,1,0:T(8,128)S(1)}, f32[8,8,256]{2,1,0:T(8,128)}, u32[]{:S(2)}) copy-start(f32[8,8,256]{2,1,0:T(8,128)} %source.5) | copy-start | bytes 196612
  1.7 14.7 %collective-permute-start.11 = (f32[4,2,8,8,256]{4,3,2,1,0:T(8,128)S(1)}, f32[4,2,8,8,256]{4,3,2,1,0:T(8,128)S(1)}, u32[]{:S(2)}, u32[]{:S(2)}) collective-permute-start(f32[4,2,8,8,256]{4,3,2,1,0:T(8,128)S(1)} %get-tuple-element.38), channel_id=1, source_target_pairs={{0,4},{4,0},{8,12},{12,8},{16,20},{20,16},{24,28},{28,24},{1,5},{5... | collective-permute-start | bytes 1572872 | tf_op jit(solution)/shard_map/ppermute | solution.py:23
  3.3 1.9 %collective-permute-start = (f32[1,2,16,8,256]{4,3,2,1,0:T(8,128)}, f32[1,2,16,8,256]{4,3,2,1,0:T(8,128)S(1)}, u32[]{:S(2)}, u32[]{:S(2)}) collective-permute-start(f32[1,2,16,8,256]{4,3,2,1,0:T(8,128)} %wind_in.1), channel_id=1, source_target_pairs={{0,1},{1,0},{2,3},{3,2},{4,5},{5,4},{6,7},{7,6},{8,9},{9,8},{10,11... | collective-permute-start | bytes 786440 | tf_op jit(solution)/shard_map/ppermute | solution.py:23
  3.3 1.9 %collective-permute-start.1 = (f32[1,15,8,256]{3,2,1,0:T(8,128)}, f32[1,15,8,256]{3,2,1,0:T(8,128)S(1)}, u32[]{:S(2)}, u32[]{:S(2)}) collective-permute-start(f32[1,15,8,256]{3,2,1,0:T(8,128)} %diffusion_in.1), channel_id=1, source_target_pairs={{0,1},{1,0},{2,3},{3,2},{4,5},{5,4},{6,7},{7,6},{8,9},{9,8},{10,11... | collective-permute-start | bytes 368648 | tf_op jit(solution)/shard_map/ppermute | solution.py:23
  5.2 7.0 %collective-permute-start.2 = (f32[3,8,8,256]{3,2,1,0:T(8,128)S(1)}, f32[3,8,8,256]{3,2,1,0:T(8,128)S(1)}, u32[]{:S(2)}, u32[]{:S(2)}) collective-permute-start(f32[3,8,8,256]{3,2,1,0:T(8,128)S(1)} %shard_map.65.met), channel_id=1, source_target_pairs={{0,2},{1,3},{2,0},{3,1},{4,6},{5,7},{6,4},{7,5},{8,10},{9,11},{10,... | collective-permute-start | bytes 589832 | tf_op jit(solution)/shard_map/ppermute | solution.py:23
  12.4 8.0 %collective-permute-start.3 = (f32[2,6,8,256]{3,2,1,0:T(8,128)S(1)}, f32[2,6,8,256]{3,2,1,0:T(8,128)S(1)}, u32[]{:S(2)}, u32[]{:S(2)}) collective-permute-start(f32[2,6,8,256]{3,2,1,0:T(8,128)S(1)} %get-tuple-element.27), channel_id=1, source_target_pairs={{0,4},{4,0},{8,12},{12,8},{16,20},{20,16},{24,28},{28,24},{1,5},{5... | collective-permute-start | bytes 294920 | tf_op jit(solution)/shard_map/ppermute | solution.py:23
  13.0 7.5 %collective-permute-start.4 = (f32[2,6,8,256]{3,2,1,0:T(8,128)S(1)}, f32[2,6,8,256]{3,2,1,0:T(8,128)S(1)}, u32[]{:S(2)}, u32[]{:S(2)}) collective-permute-start(f32[2,6,8,256]{3,2,1,0:T(8,128)S(1)} %get-tuple-element.28), channel_id=1, source_target_pairs={{4,8},{12,16},{20,24},{8,4},{16,12},{24,20},{5,9},{13,17},{21,25},... | collective-permute-start | bytes 294920 | tf_op jit(solution)/shard_map/ppermute | solution.py:29
  16.4 12.8 %collective-permute-start.12 = (f32[4,2,6,8,256]{4,3,2,1,0:T(8,128)S(1)}, f32[4,2,6,8,256]{4,3,2,1,0:T(8,128)S(1)}, u32[]{:S(2)}, u32[]{:S(2)}) collective-permute-start(f32[4,2,6,8,256]{4,3,2,1,0:T(8,128)S(1)} %shard_map.69), channel_id=1, source_target_pairs={{0,8},{8,16},{16,24},{12,4},{20,12},{28,20},{1,9},{9,17},{17,25},{... | collective-permute-start | bytes 1179656 | tf_op jit(solution)/shard_map/ppermute | solution.py:35
  19.9 16.5 %collective-permute-start.9 = (f32[3,2,6,8,256]{4,3,2,1,0:T(8,128)S(1)}, f32[3,2,6,8,256]{4,3,2,1,0:T(8,128)S(1)}, u32[]{:S(2)}, u32[]{:S(2)}) collective-permute-start(f32[3,2,6,8,256]{4,3,2,1,0:T(8,128)S(1)} %get-tuple-element.36), channel_id=1, source_target_pairs={{0,4},{4,0},{8,12},{12,8},{16,20},{20,16},{24,28},{28,24},{1,5},{5... | collective-permute-start | bytes 884744 | tf_op jit(solution)/shard_map/ppermute | solution.py:23
  20.5 3.7 %collective-permute-start.5 = (f32[24,8,256]{2,1,0:T(8,128)S(1)}, f32[24,8,256]{2,1,0:T(8,128)S(1)}, u32[]{:S(2)}, u32[]{:S(2)}) collective-permute-start(f32[24,8,256]{2,1,0:T(8,128)S(1)} %get-tuple-element.29.rest_0_), channel_id=1, source_target_pairs={{0,1},{1,0},{2,3},{3,2},{4,5},{5,4},{6,7},{7,6},{8,9},{9,8},{10,11... | collective-permute-start | bytes 589832 | tf_op jit(solution)/shard_map/ppermute | solution.py:23
  20.6 15.8 %collective-permute-start.10 = (f32[3,2,6,8,256]{4,3,2,1,0:T(8,128)S(1)}, f32[3,2,6,8,256]{4,3,2,1,0:T(8,128)S(1)}, u32[]{:S(2)}, u32[]{:S(2)}) collective-permute-start(f32[3,2,6,8,256]{4,3,2,1,0:T(8,128)S(1)} %get-tuple-element.37), channel_id=1, source_target_pairs={{4,8},{12,16},{20,24},{8,4},{16,12},{24,20},{5,9},{13,17},{21,25},... | collective-permute-start | bytes 884744 | tf_op jit(solution)/shard_map/ppermute | solution.py:29
  24.0 1.9 %collective-permute-start.6 = (f32[24,8,256]{2,1,0:T(8,128)S(1)}, f32[24,8,256]{2,1,0:T(8,128)S(1)}, u32[]{:S(2)}, u32[]{:S(2)}) collective-permute-start(f32[24,8,256]{2,1,0:T(8,128)S(1)} %get-tuple-element.30.rest_1_), channel_id=1, source_target_pairs={{0,1},{1,0},{2,3},{3,2},{4,5},{5,4},{6,7},{7,6},{8,9},{9,8},{10,11... | collective-permute-start | bytes 589832 | tf_op jit(solution)/shard_map/ppermute | solution.py:23
  24.2 14.5 %collective-permute-start.7 = (f32[1,2,6,8,256]{4,3,2,1,0:T(8,128)S(1)}, f32[1,2,6,8,256]{4,3,2,1,0:T(8,128)S(1)}, u32[]{:S(2)}, u32[]{:S(2)}) collective-permute-start(f32[1,2,6,8,256]{4,3,2,1,0:T(8,128)S(1)} %get-tuple-element.34), channel_id=1, source_target_pairs={{0,4},{4,0},{8,12},{12,8},{16,20},{20,16},{24,28},{28,24},{1,5},{5... | collective-permute-start | bytes 294920 | tf_op jit(solution)/shard_map/ppermute | solution.py:23
  25.8 12.9 %collective-permute-start.8 = (f32[1,2,6,8,256]{4,3,2,1,0:T(8,128)S(1)}, f32[1,2,6,8,256]{4,3,2,1,0:T(8,128)S(1)}, u32[]{:S(2)}, u32[]{:S(2)}) collective-permute-start(f32[1,2,6,8,256]{4,3,2,1,0:T(8,128)S(1)} %get-tuple-element.35), channel_id=1, source_target_pairs={{4,8},{12,16},{20,24},{8,4},{16,12},{24,20},{5,9},{13,17},{21,25},... | collective-permute-start | bytes 294920 | tf_op jit(solution)/shard_map/ppermute | solution.py:29

commit v7 on v5

--- a/solution.py
+++ b/solution.py
@@ -333,6 +333,7 @@
             q = advected[n, k]
             q = q + (source[start + n] if k == 0 else lower * values[n, k - 1])
             values[n, k] = q * pivot
+    late = []
     for n in range(tracers):
         target = solved.at[n] if last else out.at[start + n]
         current = values[n, levels - 1]
@@ -340,11 +341,18 @@
         for k in range(levels - 2, -1, -1):
             current = values[n, k] + solve[k, 2] * current
             target[k] = current
+            if last and k in (levels // 2, 0):
+                done = pl.ds(k, levels // 2)
+                late.append(
+                    pltpu.make_async_copy(
+                        solved.at[n, done], out.at[start + n, done], sem.at[1 + len(late)]
+                    )
+                )
+                late[-1].start()
     if last:
-        late = pltpu.make_async_copy(solved, out.at[start:], sem.at[1])
-        late.start()
         early.wait()
-        late.wait()
+        for copy in late:
+            copy.wait()
 
 
 def window(numbers, coef, solve, tracers, emissions, way, start, count, halos, prior):
@@ -366,7 +374,7 @@
     if last:
         scratch += [
             pltpu.VMEM((count, levels, height, width), jnp.float32),
-            pltpu.SemaphoreType.DMA((2,)),
+            pltpu.SemaphoreType.DMA((1 + 2 * count,)),
         ]
     shape = tracers.shape
     return pl.pallas_call(

time: 40.6 us -> 40.7 us (level)
  no operation moved by 1% of the time
where the time goes in v7:
time: 40.7 us; the launch traced here: 40.5 us
  starting transfers between devices  19.9 us (49%)
  waiting for transfers between devices  11.1 us (27%)
  Pallas kernels  9.4 us (23%)
    ppermute x9, waiting for transfers between devices, exchange(): return lax.ppermute(value, axis, [(i, i ^ bit) for i in range(count)])  11.1 us
    ppermute x3, starting transfers between devices, cross(): return lax.ppermute(value, axis, pairs + [(j, i) for i, j in pairs])  9.68 us
    pallas_call x3, Pallas kernels, window(): pl.pallas_call(functools.partial(window_kernel, way, start, count, last),...  6.94 us
    ppermute x9, starting transfers between devices, exchange(): return lax.ppermute(value, axis, [(i, i ^ bit) for i in range(count)])  6.69 us
    ppermute x1, starting transfers between devices, relay(): return lax.ppermute(value, axis, pairs)  3.48 us
    pallas_call x1, Pallas kernels, pack(): pl.pallas_call(functools.partial(pack_kernel, RELAYED, tiles), out_shape=...  1.84 us
  transfers between devices with their start and end apart: 13, of which 4 were waited for; matrix products, arithmetic and copies ran while one was open for 0% of the time, Pallas kernels for 15%

profile of v7, /device:TPU:8, one launch (start us, length us, event | category | flops | bytes accessed | tf_op | source)
XLA Modules:
  0.0 40.5 jit_solution(16970208891016532021)
XLA Ops:
  0.0 1.8 %shard_map.64 = (s32[4]{0:T(128)S(4)}, f32[8,16,8,256]{3,2,1,0:T(8,128)S(1)}, f32[1,2,16,8,256]{4,3,2,1,0:T(8,128)S(1)}, f32[1,15,8,256]{3,2,1,0:T(8,128)S(1)}, ...) custom-call(s32[8]{0:T(128)} %substeps_in.1, ...), custom_call_target="tpu_custom_call" | custom-call | bytes 1048576 | tf_op jit(solution)/shard_map/pallas_call | solution.py:155
  1.8 1.6 %collective-permute-start.11 = (f32[4,2,8,8,256]{4,3,2,1,0:T(8,128)S(1)}, f32[4,2,8,8,256]{4,3,2,1,0:T(8,128)S(1)}, u32[]{:S(2)}, u32[]{:S(2)}) collective-permute-start(f32[4,2,8,8,256]{4,3,2,1,0:T(8,128)S(1)} %get-tuple-element.38), channel_id=1, source_target_pairs={{0,4},{4,0},{8,12},{12,8},{16,20},{20,16},{24,28},{28,24},{1,5},{5... | collective-permute-start | bytes 1572872 | tf_op jit(solution)/shard_map/ppermute | solution.py:23
  3.4 0.0 collective-permute-start
  3.4 0.5 %collective-permute-start.1 = (f32[1,15,8,256]{3,2,1,0:T(8,128)}, f32[1,15,8,256]{3,2,1,0:T(8,128)S(1)}, u32[]{:S(2)}, u32[]{:S(2)}) collective-permute-start(f32[1,15,8,256]{3,2,1,0:T(8,128)} %diffusion_in.1), channel_id=1, source_target_pairs={{0,1},{1,0},{2,3},{3,2},{4,5},{5,4},{6,7},{7,6},{8,9},{9,8},{10,11... | collective-permute-start | bytes 368648 | tf_op jit(solution)/shard_map/ppermute | solution.py:23
  3.9 1.4 %collective-permute-done.1.diffusion_other = f32[1,15,8,256]{3,2,1,0:T(8,128)S(1)} collective-permute-done((f32[1,15,8,256]{3,2,1,0:T(8,128)}, f32[1,15,8,256]{3,2,1,0:T(8,128)S(1)}, u32[]{:S(2)}, u32[]{:S(2)}) %collective-permute-start.1) | collective-permute-done | bytes 122912 | tf_op jit(solution)/shard_map/ppermute | solution.py:23
  5.4 0.0 collective-permute-done.wind_other
  5.4 1.6 %collective-permute-start.2 = (f32[3,8,8,256]{3,2,1,0:T(8,128)S(1)}, f32[3,8,8,256]{3,2,1,0:T(8,128)S(1)}, u32[]{:S(2)}, u32[]{:S(2)}) collective-permute-start(f32[3,8,8,256]{3,2,1,0:T(8,128)S(1)} %shard_map.65.met), channel_id=1, source_target_pairs={{0,2},{1,3},{2,0},{3,1},{4,6},{5,7},{6,4},{7,5},{8,10},{9,11},{10,... | collective-permute-start | bytes 589832 | tf_op jit(solution)/shard_map/ppermute | solution.py:23
  6.9 5.5 %collective-permute-done.2.other = f32[3,8,8,256]{3,2,1,0:T(8,128)S(1)} collective-permute-done((f32[3,8,8,256]{3,2,1,0:T(8,128)S(1)}, f32[3,8,8,256]{3,2,1,0:T(8,128)S(1)}, u32[]{:S(2)}, u32[]{:S(2)}) %collective-permute-start.2) | collective-permute-done | bytes 196640 | tf_op jit(solution)/shard_map/ppermute | solution.py:23
  12.4 0.2 shard_map.66
  12.6 0.6 %collective-permute-start.3 = (f32[2,6,8,256]{3,2,1,0:T(8,128)S(1)}, f32[2,6,8,256]{3,2,1,0:T(8,128)S(1)}, u32[]{:S(2)}, u32[]{:S(2)}) collective-permute-start(f32[2,6,8,256]{3,2,1,0:T(8,128)S(1)} %get-tuple-element.27), channel_id=1, source_target_pairs={{0,4},{4,0},{8,12},{12,8},{16,20},{20,16},{24,28},{28,24},{1,5},{5... | collective-permute-start | bytes 294920 | tf_op jit(solution)/shard_map/ppermute | solution.py:23
  13.1 3.3 %collective-permute-start.4 = (f32[2,6,8,256]{3,2,1,0:T(8,128)S(1)}, f32[2,6,8,256]{3,2,1,0:T(8,128)S(1)}, u32[]{:S(2)}, u32[]{:S(2)}) collective-permute-start(f32[2,6,8,256]{3,2,1,0:T(8,128)S(1)} %get-tuple-element.28), channel_id=1, source_target_pairs={{4,8},{12,16},{20,24},{8,4},{16,12},{24,20},{5,9},{13,17},{21,25},... | collective-permute-start | bytes 294920 | tf_op jit(solution)/shard_map/ppermute | solution.py:29
  16.4 0.1 collective-permute-done.11.pair.rest_0_
  16.6 3.5 %collective-permute-start.12 = (f32[4,2,6,8,256]{4,3,2,1,0:T(8,128)S(1)}, f32[4,2,6,8,256]{4,3,2,1,0:T(8,128)S(1)}, u32[]{:S(2)}, u32[]{:S(2)}) collective-permute-start(f32[4,2,6,8,256]{4,3,2,1,0:T(8,128)S(1)} %shard_map.69), channel_id=1, source_target_pairs={{0,8},{8,16},{16,24},{12,4},{20,12},{28,20},{1,9},{9,17},{17,25},{... | collective-permute-start | bytes 1179656 | tf_op jit(solution)/shard_map/ppermute | solution.py:35
  20.1 0.5 %collective-permute-start.9 = (f32[3,2,6,8,256]{4,3,2,1,0:T(8,128)S(1)}, f32[3,2,6,8,256]{4,3,2,1,0:T(8,128)S(1)}, u32[]{:S(2)}, u32[]{:S(2)}) collective-permute-start(f32[3,2,6,8,256]{4,3,2,1,0:T(8,128)S(1)} %get-tuple-element.36), channel_id=1, source_target_pairs={{0,4},{4,0},{8,12},{12,8},{16,20},{20,16},{24,28},{28,24},{1,5},{5... | collective-permute-start | bytes 884744 | tf_op jit(solution)/shard_map/ppermute | solution.py:23
  20.6 0.0 collective-permute-done.3.pair
  20.6 0.0 collective-permute-done.4.far
  20.7 0.1 collective-permute-start.5
  20.7 3.4 %collective-permute-start.10 = (f32[3,2,6,8,256]{4,3,2,1,0:T(8,128)S(1)}, f32[3,2,6,8,256]{4,3,2,1,0:T(8,128)S(1)}, u32[]{:S(2)}, u32[]{:S(2)}) collective-permute-start(f32[3,2,6,8,256]{4,3,2,1,0:T(8,128)S(1)} %get-tuple-element.37), channel_id=1, source_target_pairs={{4,8},{12,16},{20,24},{8,4},{16,12},{24,20},{5,9},{13,17},{21,25},... | collective-permute-start | bytes 884744 | tf_op jit(solution)/shard_map/ppermute | solution.py:29
  24.1 0.3 collective-permute-start.6
  24.4 0.0 collective-permute-done.5.rest_2_
  24.4 1.6 %collective-permute-start.7 = (f32[1,2,6,8,256]{4,3,2,1,0:T(8,128)S(1)}, f32[1,2,6,8,256]{4,3,2,1,0:T(8,128)S(1)}, u32[]{:S(2)}, u32[]{:S(2)}) collective-permute-start(f32[1,2,6,8,256]{4,3,2,1,0:T(8,128)S(1)} %get-tuple-element.34), channel_id=1, source_target_pairs={{0,4},{4,0},{8,12},{12,8},{16,20},{20,16},{24,28},{28,24},{1,5},{5... | collective-permute-start | bytes 294920 | tf_op jit(solution)/shard_map/ppermute | solution.py:23
  26.0 0.0 collective-permute-done.6.rest_3_
  26.0 3.0 %collective-permute-start.8 = (f32[1,2,6,8,256]{4,3,2,1,0:T(8,128)S(1)}, f32[1,2,6,8,256]{4,3,2,1,0:T(8,128)S(1)}, u32[]{:S(2)}, u32[]{:S(2)}) collective-permute-start(f32[1,2,6,8,256]{4,3,2,1,0:T(8,128)S(1)} %get-tuple-element.35), channel_id=1, source_target_pairs={{4,8},{12,16},{20,24},{8,4},{16,12},{24,20},{5,9},{13,17},{21,25},... | collective-permute-start | bytes 294920 | tf_op jit(solution)/shard_map/ppermute | solution.py:29
  29.0 0.4 shard_map.68
  29.4 0.0 collective-permute-done.12.rest_1_
  29.4 3.0 %shard_map.70.rest_2_ = f32[8,16,8,256]{3,2,1,0:T(8,128)S(1)} custom-call(s32[4]{0:T(128)S(4)} %get-tuple-element.22.numbers._, f32[3,24,5,8,256]{4,3,2,1,0:T(8,128)S(1)} %get-tuple-element.31.coef, f32[16,3,8,256]{3,2,1,0:T(8,128)S(1)} %get-tuple-element.32.solve, f32[8,16,8,256]{3,2,1,0:T(8,128)S(1)} %get-tuple-element.33.own, f32[8,8,256]{2,1,0:T(8,128)S(1)} %copy-done, ...), custom_call_target="tpu_custom_call" | custom-call | bytes 1048576 | tf_op jit(solution)/shard_map/pallas_call | solution.py:380
  32.4 4.2 %collective-permute-done.9.rest_0_ = f32[3,2,6,8,256]{4,3,2,1,0:T(8,128)S(1)} collective-permute-done((f32[3,2,6,8,256]{4,3,2,1,0:T(8,128)S(1)}, f32[3,2,6,8,256]{4,3,2,1,0:T(8,128)S(1)}, u32[]{:S(2)}, u32[]{:S(2)}) %collective-permute-start.9) | collective-permute-done | bytes 294944 | tf_op jit(solution)/shard_map/ppermute | solution.py:23
  36.6 0.0 collective-permute-done.10.rest_1_
  36.6 2.3 %shard_map.71.rest_2_ = f32[8,16,8,256]{3,2,1,0:T(8,128)S(1)} custom-call(s32[4]{0:T(128)S(4)} %get-tuple-element.22.numbers._, f32[3,24,5,8,256]{4,3,2,1,0:T(8,128)S(1)} %get-tuple-element.31.coef, f32[16,3,8,256]{3,2,1,0:T(8,128)S(1)} %get-tuple-element.32.solve, f32[8,16,8,256]{3,2,1,0:T(8,128)S(1)} %get-tuple-element.33.own, ...), custom_call_target="tpu_custom_call", output_to_operand_aliasing={{}: (7, {})} | custom-call | bytes 1048576 | tf_op jit(solution)/shard_map/pallas_call | solution.py:380
  38.8 0.0 collective-permute-done.7.rest_0_
  38.8 0.0 collective-permute-done.8.rest_1_
  38.8 1.7 %shard_map.72 = f32[8,16,8,256]{3,2,1,0:T(8,128)} custom-call(s32[4]{0:T(128)S(4)} %get-tuple-element.22.numbers._, f32[3,24,5,8,256]{4,3,2,1,0:T(8,128)S(1)} %get-tuple-element.31.coef, f32[16,3,8,256]{3,2,1,0:T(8,128)S(1)} %get-tuple-element.32.solve, f32[8,16,8,256]{3,2,1,0:T(8,128)S(1)} %get-tuple-element.33.own, f32[8,8,256]{2,1,0:T(8,128)S(1)} %copy-done, ...), custom_call_target="tpu_custom_call" | custom-call | bytes 1048576 | tf_op jit(solution)/shard_map/pallas_call | solution.py:380
  (5 shorter events, 0.1 us)
Async XLA Ops:
  0.0 29.4 %copy-start = (f32[8,8,256]{2,1,0:T(8,128)S(1)}, f32[8,8,256]{2,1,0:T(8,128)}, u32[]{:S(2)}) copy-start(f32[8,8,256]{2,1,0:T(8,128)} %source.5) | copy-start | bytes 196612
  1.8 14.7 %collective-permute-start.11 = (f32[4,2,8,8,256]{4,3,2,1,0:T(8,128)S(1)}, f32[4,2,8,8,256]{4,3,2,1,0:T(8,128)S(1)}, u32[]{:S(2)}, u32[]{:S(2)}) collective-permute-start(f32[4,2,8,8,256]{4,3,2,1,0:T(8,128)S(1)} %get-tuple-element.38), channel_id=1, source_target_pairs={{0,4},{4,0},{8,12},{12,8},{16,20},{20,16},{24,28},{28,24},{1,5},{5... | collective-permute-start | bytes 1572872 | tf_op jit(solution)/shard_map/ppermute | solution.py:23
  3.4 1.9 %collective-permute-start = (f32[1,2,16,8,256]{4,3,2,1,0:T(8,128)}, f32[1,2,16,8,256]{4,3,2,1,0:T(8,128)S(1)}, u32[]{:S(2)}, u32[]{:S(2)}) collective-permute-start(f32[1,2,16,8,256]{4,3,2,1,0:T(8,128)} %wind_in.1), channel_id=1, source_target_pairs={{0,1},{1,0},{2,3},{3,2},{4,5},{5,4},{6,7},{7,6},{8,9},{9,8},{10,11... | collective-permute-start | bytes 786440 | tf_op jit(solution)/shard_map/ppermute | solution.py:23
  3.4 1.9 %collective-permute-start.1 = (f32[1,15,8,256]{3,2,1,0:T(8,128)}, f32[1,15,8,256]{3,2,1,0:T(8,128)S(1)}, u32[]{:S(2)}, u32[]{:S(2)}) collective-permute-start(f32[1,15,8,256]{3,2,1,0:T(8,128)} %diffusion_in.1), channel_id=1, source_target_pairs={{0,1},{1,0},{2,3},{3,2},{4,5},{5,4},{6,7},{7,6},{8,9},{9,8},{10,11... | collective-permute-start | bytes 368648 | tf_op jit(solution)/shard_map/ppermute | solution.py:23
  5.4 7.0 %collective-permute-start.2 = (f32[3,8,8,256]{3,2,1,0:T(8,128)S(1)}, f32[3,8,8,256]{3,2,1,0:T(8,128)S(1)}, u32[]{:S(2)}, u32[]{:S(2)}) collective-permute-start(f32[3,8,8,256]{3,2,1,0:T(8,128)S(1)} %shard_map.65.met), channel_id=1, source_target_pairs={{0,2},{1,3},{2,0},{3,1},{4,6},{5,7},{6,4},{7,5},{8,10},{9,11},{10,... | collective-permute-start | bytes 589832 | tf_op jit(solution)/shard_map/ppermute | solution.py:23
  12.6 8.0 %collective-permute-start.3 = (f32[2,6,8,256]{3,2,1,0:T(8,128)S(1)}, f32[2,6,8,256]{3,2,1,0:T(8,128)S(1)}, u32[]{:S(2)}, u32[]{:S(2)}) collective-permute-start(f32[2,6,8,256]{3,2,1,0:T(8,128)S(1)} %get-tuple-element.27), channel_id=1, source_target_pairs={{0,4},{4,0},{8,12},{12,8},{16,20},{20,16},{24,28},{28,24},{1,5},{5... | collective-permute-start | bytes 294920 | tf_op jit(solution)/shard_map/ppermute | solution.py:23
  13.1 7.5 %collective-permute-start.4 = (f32[2,6,8,256]{3,2,1,0:T(8,128)S(1)}, f32[2,6,8,256]{3,2,1,0:T(8,128)S(1)}, u32[]{:S(2)}, u32[]{:S(2)}) collective-permute-start(f32[2,6,8,256]{3,2,1,0:T(8,128)S(1)} %get-tuple-element.28), channel_id=1, source_target_pairs={{4,8},{12,16},{20,24},{8,4},{16,12},{24,20},{5,9},{13,17},{21,25},... | collective-permute-start | bytes 294920 | tf_op jit(solution)/shard_map/ppermute | solution.py:29
  16.6 12.8 %collective-permute-start.12 = (f32[4,2,6,8,256]{4,3,2,1,0:T(8,128)S(1)}, f32[4,2,6,8,256]{4,3,2,1,0:T(8,128)S(1)}, u32[]{:S(2)}, u32[]{:S(2)}) collective-permute-start(f32[4,2,6,8,256]{4,3,2,1,0:T(8,128)S(1)} %shard_map.69), channel_id=1, source_target_pairs={{0,8},{8,16},{16,24},{12,4},{20,12},{28,20},{1,9},{9,17},{17,25},{... | collective-permute-start | bytes 1179656 | tf_op jit(solution)/shard_map/ppermute | solution.py:35
  20.1 16.5 %collective-permute-start.9 = (f32[3,2,6,8,256]{4,3,2,1,0:T(8,128)S(1)}, f32[3,2,6,8,256]{4,3,2,1,0:T(8,128)S(1)}, u32[]{:S(2)}, u32[]{:S(2)}) collective-permute-start(f32[3,2,6,8,256]{4,3,2,1,0:T(8,128)S(1)} %get-tuple-element.36), channel_id=1, source_target_pairs={{0,4},{4,0},{8,12},{12,8},{16,20},{20,16},{24,28},{28,24},{1,5},{5... | collective-permute-start | bytes 884744 | tf_op jit(solution)/shard_map/ppermute | solution.py:23
  20.7 3.7 %collective-permute-start.5 = (f32[24,8,256]{2,1,0:T(8,128)S(1)}, f32[24,8,256]{2,1,0:T(8,128)S(1)}, u32[]{:S(2)}, u32[]{:S(2)}) collective-permute-start(f32[24,8,256]{2,1,0:T(8,128)S(1)} %get-tuple-element.29.rest_0_), channel_id=1, source_target_pairs={{0,1},{1,0},{2,3},{3,2},{4,5},{5,4},{6,7},{7,6},{8,9},{9,8},{10,11... | collective-permute-start | bytes 589832 | tf_op jit(solution)/shard_map/ppermute | solution.py:23
  20.7 15.8 %collective-permute-start.10 = (f32[3,2,6,8,256]{4,3,2,1,0:T(8,128)S(1)}, f32[3,2,6,8,256]{4,3,2,1,0:T(8,128)S(1)}, u32[]{:S(2)}, u32[]{:S(2)}) collective-permute-start(f32[3,2,6,8,256]{4,3,2,1,0:T(8,128)S(1)} %get-tuple-element.37), channel_id=1, source_target_pairs={{4,8},{12,16},{20,24},{8,4},{16,12},{24,20},{5,9},{13,17},{21,25},... | collective-permute-start | bytes 884744 | tf_op jit(solution)/shard_map/ppermute | solution.py:29
  24.1 1.9 %collective-permute-start.6 = (f32[24,8,256]{2,1,0:T(8,128)S(1)}, f32[24,8,256]{2,1,0:T(8,128)S(1)}, u32[]{:S(2)}, u32[]{:S(2)}) collective-permute-start(f32[24,8,256]{2,1,0:T(8,128)S(1)} %get-tuple-element.30.rest_1_), channel_id=1, source_target_pairs={{0,1},{1,0},{2,3},{3,2},{4,5},{5,4},{6,7},{7,6},{8,9},{9,8},{10,11... | collective-permute-start | bytes 589832 | tf_op jit(solution)/shard_map/ppermute | solution.py:23
  24.4 14.5 %collective-permute-start.7 = (f32[1,2,6,8,256]{4,3,2,1,0:T(8,128)S(1)}, f32[1,2,6,8,256]{4,3,2,1,0:T(8,128)S(1)}, u32[]{:S(2)}, u32[]{:S(2)}) collective-permute-start(f32[1,2,6,8,256]{4,3,2,1,0:T(8,128)S(1)} %get-tuple-element.34), channel_id=1, source_target_pairs={{0,4},{4,0},{8,12},{12,8},{16,20},{20,16},{24,28},{28,24},{1,5},{5... | collective-permute-start | bytes 294920 | tf_op jit(solution)/shard_map/ppermute | solution.py:23
  26.0 12.9 %collective-permute-start.8 = (f32[1,2,6,8,256]{4,3,2,1,0:T(8,128)S(1)}, f32[1,2,6,8,256]{4,3,2,1,0:T(8,128)S(1)}, u32[]{:S(2)}, u32[]{:S(2)}) collective-permute-start(f32[1,2,6,8,256]{4,3,2,1,0:T(8,128)S(1)} %get-tuple-element.35), channel_id=1, source_target_pairs={{4,8},{12,16},{20,24},{8,4},{16,12},{24,20},{5,9},{13,17},{21,25},... | collective-permute-start | bytes 294920 | tf_op jit(solution)/shard_map/ppermute | solution.py:29
